TPU v7x, 256 devices: a whole 4x4x8 slice. The times are simulated.
256 devices in a mesh: shot: 16 (over y_lo, z), slab: 16 (over y_hi, x, core).
Axes of the slice: x: 4, y: 4 (y_hi: 2, y_lo: 2; y = y_hi * 2 + y_lo), z: 8, core: 2. Of those that a mesh axis runs over, the one named last changes fastest.
Arguments:
- courant: float32 [256, 128, 128], P('slab'), may hold values from 0.225 to 0.45
- adj_prev: float32 [32, 256, 128, 128], P('shot', 'slab'), may hold values from -10 to 10
- adj_curr: float32 [32, 256, 128, 128], P('shot', 'slab'), may hold values from -8 to 8
- forward_snaps: bfloat16 [32, 2, 256, 128, 128], P('shot', None, 'slab'), may hold values from -6 to 6
- traces: float32 [32, 2, 128], P('shot'), may hold values from -12 to 12
- receiver_z: int32 [32, 128], P('shot'), may hold values from 0 to 255
- receiver_x: int32 [32, 128], P('shot'), may hold values from 0 to 127
- receiver_y: int32 [32, 128], P('shot'), may hold values from 0 to 127
- pml_cells: int32 [3], replicated, may hold values from 4 to 11
- omega_z: int32 [256, 128], P('slab'), may hold values from -2 to 2
- omega_x: int32 [128, 128], replicated, may hold values from -2 to 2
- omega_y: int32 [128, 128], replicated, may hold values from -2 to 2
Outputs:
- sketch: float32 [32, 128], P('shot')
- coarse: float32 [32, 256, 8192], P('shot', 'slab')
- gram_band: float32 [32, 4, 2], P('shot')
All inputs are finite; a program needn't handle non-finite values.
Results may differ from a plain program's by a relative error of at most 0.0047.
Values sent between devices are 32-bit elements; how exact they have to be, the bound alone decides.
No kernel may reach another device: no remote copies, remote signals or barrier semaphores. Data moves between devices by JAX's collectives and lax.ppermute only.
A program may use at most 128 MiB of HBM per device.

v0:
```python
import math

import jax
import jax.numpy as jnp
from jax import lax
from jax.sharding import PartitionSpec as P

STEPS = 2
LAGS = 4


stencil_coeffs = (-205.0 / 72.0, 8.0 / 5.0, -1.0 / 5.0, 8.0 / 315.0, -1.0 / 560.0)
damp_peak = 0.3


def with_halo(cells, sides, width):
    for axis, dim in sides:
        count = lax.axis_size(axis)
        ends = count - 1
        head = lax.slice_in_dim(cells, 0, width, axis=dim)
        tail = lax.slice_in_dim(cells, cells.shape[dim] - width, cells.shape[dim], axis=dim)
        cells = jnp.concatenate(
            [
                lax.ppermute(tail, axis, [(i, (i + 1) % count) for i in range(ends)]),
                cells,
                lax.ppermute(head, axis, [((i + 1) % count, i) for i in range(ends)]),
            ],
            axis=dim,
        )
    return cells


def from_behind(array, axis, by):
    peers = lax.axis_size(axis)
    return lax.ppermute(array, axis, [(i, (i + by) % peers) for i in range(peers)])


def pml_ramp(position, length, thickness):
    distance = jnp.minimum(position, length - 1 - position).astype(jnp.float32)
    reach = thickness.astype(jnp.float32)
    return jnp.maximum((reach - distance) / reach, 0.0)


def damping_field(index_z, index_x, index_y, total_z, cells_x, cells_y, pml_cells):
    ramp_z = pml_ramp(index_z, total_z, pml_cells[0])
    ramp_x = pml_ramp(index_x, cells_x, pml_cells[1])
    ramp_y = pml_ramp(index_y, cells_y, pml_cells[2])
    return damp_peak * (
        ramp_z[:, None, None] * ramp_z[:, None, None]
        + ramp_x[None, :, None] * ramp_x[None, :, None]
        + ramp_y[None, None, :] * ramp_y[None, None, :]
    )


def laplace(extended, values):
    cells_z, cells_x, cells_y = values.shape[-3:]
    leading = [(0, 0)] * (values.ndim - 3)
    padded = jnp.pad(extended, leading + [(0, 0), (4, 4), (4, 4)])
    total = 3.0 * stencil_coeffs[0] * values
    for offset in range(1, 5):
        weight = stencil_coeffs[offset]
        along_z = (
            padded[..., 4 + offset : 4 + offset + cells_z, 4 : 4 + cells_x, 4 : 4 + cells_y]
            + padded[..., 4 - offset : 4 - offset + cells_z, 4 : 4 + cells_x, 4 : 4 + cells_y]
        )
        along_x = (
            padded[..., 4 : 4 + cells_z, 4 + offset : 4 + offset + cells_x, 4 : 4 + cells_y]
            + padded[..., 4 : 4 + cells_z, 4 - offset : 4 - offset + cells_x, 4 : 4 + cells_y]
        )
        along_y = (
            padded[..., 4 : 4 + cells_z, 4 : 4 + cells_x, 4 + offset : 4 + offset + cells_y]
            + padded[..., 4 : 4 + cells_z, 4 : 4 + cells_x, 4 - offset : 4 - offset + cells_y]
        )
        total = total + weight * (along_z + along_x + along_y)
    return total


def inject(traces_now, receiver_z, receiver_x, receiver_y, first_z, depth, cells_x, cells_y):
    shot_count = traces_now.shape[0]
    local_z = receiver_z - first_z
    inside = (local_z >= 0) & (local_z < depth)
    clipped = jnp.clip(local_z, 0, depth - 1)
    shot_ids = jnp.broadcast_to(jnp.arange(shot_count, dtype=jnp.int32)[:, None], receiver_z.shape)
    amounts = jnp.where(inside, traces_now, 0.0)
    return (
        jnp.zeros((shot_count, depth, cells_x, cells_y), jnp.float32)
        .at[shot_ids, clipped, receiver_x, receiver_y]
        .add(amounts)
    )


def lag_product(mine, theirs):
    return jnp.einsum("sc,jc->sj", mine, theirs, precision=lax.Precision.HIGHEST)


def local(
    courant,
    adj_prev,
    adj_curr,
    forward_snaps,
    traces,
    receiver_z,
    receiver_x,
    receiver_y,
    pml_cells,
    omega_z,
    omega_x,
    omega_y,
):
    highest = lax.Precision.HIGHEST
    shot_count, cells_z, cells_x, cells_y = adj_curr.shape
    total_z = cells_z * lax.axis_size("slab")
    offset_z = lax.axis_index("slab") * cells_z
    index_z = offset_z + jnp.arange(cells_z, dtype=jnp.int32)
    index_x = jnp.arange(cells_x, dtype=jnp.int32)
    index_y = jnp.arange(cells_y, dtype=jnp.int32)
    damping = damping_field(index_z, index_x, index_y, total_z, cells_x, cells_y, pml_cells)
    speed_sq = courant * courant
    sketch_scale = 1.0 / math.sqrt(total_z * cells_x * cells_y)
    gram_scale = 1.0 / math.sqrt(total_z * cells_x * cells_y // 2)
    gradient = jnp.zeros((shot_count, cells_z, cells_x, cells_y), jnp.float32)
    previous = adj_prev
    current = adj_curr
    for instant in range(STEPS):
        source = inject(
            traces[:, instant],
            receiver_z,
            receiver_x,
            receiver_y,
            offset_z,
            cells_z,
            cells_x,
            cells_y,
        )
        extended = with_halo(current, (("slab", 1),), 4)
        updated = (
            2.0 * current
            - (1.0 - damping) * previous
            + speed_sq * laplace(extended, current)
            + source
        ) / (1.0 + damping)
        gradient = gradient + updated * forward_snaps[:, instant].astype(jnp.float32)
        previous, current = (current, updated)
    rounded = lax.optimization_barrier(gradient.astype(jnp.bfloat16))
    first = jnp.einsum(
        "szxy,yr->szxr", rounded, omega_y.astype(jnp.bfloat16), preferred_element_type=jnp.float32
    )
    second = jnp.einsum("szxr,xr->szr", first, omega_x.astype(jnp.float32), precision=highest)
    partial_sketch = jnp.sum(second * omega_z.astype(jnp.float32)[None], axis=1)
    sketch = lax.psum(partial_sketch, "slab") * sketch_scale
    widened = rounded.astype(jnp.float32)
    coarse = (0.5 * (widened[..., 0::2] + widened[..., 1::2])).reshape(
        shot_count, cells_z, cells_x * cells_y // 2
    )
    panel = coarse.reshape(shot_count, cells_z * cells_x * cells_y // 2)
    bands = []
    moving = panel
    for lag_index in range(LAGS):
        moving = from_behind(moving, "shot", 1)
        bands.append(lag_product(panel, moving))
    band_part = jnp.stack(bands, axis=1)
    gram_band = lax.psum(band_part, "slab") * gram_scale
    return (sketch, coarse, gram_band)


def solution(mesh):
    return jax.shard_map(
        local,
        mesh=mesh,
        in_specs=(
            P("slab", None, None),
            P("shot", "slab", None, None),
            P("shot", "slab", None, None),
            P("shot", None, "slab", None, None),
            P("shot", None, None),
            P("shot", None),
            P("shot", None),
            P("shot", None),
            P(),
            P("slab", None),
            P(),
            P(),
        ),
        out_specs=(P("shot", None), P("shot", "slab", None), P("shot", None, None)),
        check_vma=False,
    )
```

profile of v0, /device:TPU:120, one launch (start us, length us, event | category | flops | bytes accessed | tf_op | source)
XLA Modules:
  0.0 374.7 jit_solution(10905023267759119941)
XLA Ops:
  0.7 2.4 fusion.71
  3.1 1.9 collective-permute-start.1
  5.0 7.3 %collective-permute-start = (f32[2,4,128,128]{3,2,1,0:T(8,128)}, f32[2,4,128,128]{3,2,1,0:T(8,128)}, u32[]{:S(2)}, u32[]{:S(2)}) collective-permute-start(f32[2,4,128,128]{3,2,1,0:T(8,128)} %get-tuple-element.19), channel_id=1, source_target_pairs={{1,0},{2,1},{3,2},{4,3},{5,4},{6,5},{7,6},{8,7},{9,8},{10,9},{11,1... | collective-permute-start | bytes 1572872 | tf_op jit(solution)/shard_map/ppermute | solution.py:26
  19.4 2.5 constant_dynamic-update-slice_fusion.1
  21.9 3.8 %select_maximum_fusion.2 = f32[2,24,136,136]{3,2,1,0:T(8,128)S(1)} fusion(f32[2,4,128,128]{3,2,1,0:T(8,128)} %collective-permute-done, f32[2,16,128,128]{3,2,1,0:T(8,128)S(1)} %copy-done, f32[2,4,128,128]{3,2,1,0:T(8,128)} %collective-permute-done.1), kind=kLoop, calls=%fused_computation.8 | loop fusion | flops 13317120 | bytes 6696960 | tf_op jit(solution)/shard_map/concatenate | solution.py:22
  27.6 12.5 %fusion.35 = f32[2,16,128,128]{3,2,1,0:T(8,128)} fusion(f32[2,24,136,136]{3,2,1,0:T(8,128)S(1)} %select_maximum_fusion.2, f32[2,20,128,128]{3,2,1,0:T(8,128)} %get-tuple-element.17, f32[2,20,128,128]{3,2,1,0:T(8,128)} %constant_dynamic-update-slice_fusion, f32[2,16,128,128]{3,2,1,0:T(8,128)S(1)} %copy-done, f32[2,16,128,128]{3,2,1,0:T(8,128)} %param.13, ...), kind=kLoop, calls=%fused_computation.68 | loop fusion | flops 17825792 | bytes 58720256 | tf_op jit(solution)/shard_map/add | solution.py:137
  40.1 36.3 %scatter_fusion = f32[2,16,128,128]{3,2,1,0:T(8,128)} fusion(f32[2,16,128,128]{3,2,1,0:T(8,128)} %fusion.35, s32[256]{0:T(256)S(1)} %fusion.63, f32[256]{0:T(256)S(1)} %get-tuple-element.25), kind=kCustom, calls=%fused_computation | custom fusion | flops 256 | bytes 7168 | tf_op jit(solution)/shard_map/scatter-add | solution.py:88
  76.3 2.1 broadcast_divide_fusion
  78.5 4.8 %collective-permute-start.2 = (f32[2,4,128,128]{3,2,1,0:T(8,128)S(1)}, f32[2,4,128,128]{3,2,1,0:T(8,128)S(1)}, u32[]{:S(2)}, u32[]{:S(2)}) collective-permute-start(f32[2,4,128,128]{3,2,1,0:T(8,128)S(1)} %get-tuple-element.14), channel_id=1, source_target_pairs={{1,0},{2,1},{3,2},{4,3},{5,4},{6,5},{7,6},{8,7},{9,8},{10,9},{11,1... | collective-permute-start | bytes 1572872 | tf_op jit(solution)/shard_map/ppermute | solution.py:26
  83.4 2.4 collective-permute-start.3
  85.8 4.3 %collective-permute-done.2 = f32[2,4,128,128]{3,2,1,0:T(8,128)S(1)} collective-permute-done((f32[2,4,128,128]{3,2,1,0:T(8,128)S(1)}, f32[2,4,128,128]{3,2,1,0:T(8,128)S(1)}, u32[]{:S(2)}, u32[]{:S(2)}) %collective-permute-start.2) | collective-permute-done | bytes 524320 | tf_op jit(solution)/shard_map/ppermute | solution.py:26
  90.1 7.4 %collective-permute-done.3 = f32[2,4,128,128]{3,2,1,0:T(8,128)S(1)} collective-permute-done((f32[2,4,128,128]{3,2,1,0:T(8,128)S(1)}, f32[2,4,128,128]{3,2,1,0:T(8,128)S(1)}, u32[]{:S(2)}, u32[]{:S(2)}) %collective-permute-start.3) | collective-permute-done | bytes 524320 | tf_op jit(solution)/shard_map/ppermute | solution.py:24
  98.3 4.5 %select_maximum_fusion = f32[2,24,136,136]{3,2,1,0:T(8,128)} fusion(f32[2,4,128,128]{3,2,1,0:T(8,128)S(1)} %collective-permute-done.2, f32[2,16,128,128]{3,2,1,0:T(8,128)S(1)} %broadcast_divide_fusion, f32[2,4,128,128]{3,2,1,0:T(8,128)S(1)} %collective-permute-done.3), kind=kLoop, calls=%fused_computation.6 | loop fusion | flops 13317120 | bytes 6696960 | tf_op jit(solution)/shard_map/concatenate | solution.py:22
  102.8 37.2 %fusion.11 = f32[2,16,128,128]{3,2,1,0:T(8,128)} fusion(f32[2,16,128,128]{3,2,1,0:T(8,128)} %copy-done.2, f32[2,4,128,128]{3,2,1,0:T(8,128)} %copy-done.5, f32[2,4,128,128]{3,2,1,0:T(8,128)} %copy-done.4, f32[2,24,136,136]{3,2,1,0:T(8,128)} %select_maximum_fusion, f32[2,16,128,128]{3,2,1,0:T(8,128)S(1)} %copy-done, f32[16,128,128]{2,1,0:T(8,128)S(1)} %mul.145, ...), kind=kLoop, calls=%fused_computation.33 | loop fusion | flops 22020096 | bytes 42991616 | tf_op jit(solution)/shard_map/add | solution.py:137
  140.0 36.2 %scatter_fusion.1 = f32[2,16,128,128]{3,2,1,0:T(8,128)} fusion(f32[2,16,128,128]{3,2,1,0:T(8,128)} %fusion.11, s32[256]{0:T(256)S(1)} %fusion.63, f32[256]{0:T(256)S(1)} %get-tuple-element.24), kind=kCustom, calls=%fused_computation.1 | custom fusion | flops 256 | bytes 7168 | tf_op jit(solution)/shard_map/scatter-add | solution.py:88
  176.3 3.2 fusion.50
  179.5 19.2 %slice.274 = f32[2,16,128,64]{3,2,1,0:T(8,128)} slice(bf16[2,16,128,128]{3,2,1,0:T(8,128)(2,1)S(1)} %fusion.50), slice={[0:2:1], [0:16:1], [0:128:1], [0:128:2]} | slice | bytes 2097152 | tf_op jit(solution)/shard_map/slice | solution.py:152
  198.7 19.4 %slice.275 = f32[2,16,128,64]{3,2,1,0:T(8,128)} slice(bf16[2,16,128,128]{3,2,1,0:T(8,128)(2,1)S(1)} %fusion.50), slice={[0:2:1], [0:16:1], [0:128:1], [1:128:2]} | slice | bytes 2097152 | tf_op jit(solution)/shard_map/slice | solution.py:152
  218.1 2.5 add_multiply_fusion
  220.6 2.0 reshape_reshape.3
  222.6 3.3 collective-permute-start.4
  225.9 19.8 %collective-permute-done.4 = f32[2,131072]{1,0:T(2,128)S(1)} collective-permute-done((f32[2,131072]{1,0:T(2,128)}, f32[2,131072]{1,0:T(2,128)S(1)}, u32[]{:S(2)}, u32[]{:S(2)}) %collective-permute-start.4) | collective-permute-done | bytes 1048608 | tf_op jit(solution)/shard_map/ppermute | solution.py:35
  245.7 3.7 collective-permute-start.5
  249.4 19.3 %collective-permute-done.5 = f32[2,131072]{1,0:T(2,128)} collective-permute-done((f32[2,131072]{1,0:T(2,128)S(1)}, f32[2,131072]{1,0:T(2,128)}, u32[]{:S(2)}, u32[]{:S(2)}) %collective-permute-start.5) | collective-permute-done | bytes 1048608 | tf_op jit(solution)/shard_map/ppermute | solution.py:35
  268.8 3.8 %collective-permute-start.6 = (f32[2,131072]{1,0:T(2,128)}, f32[2,131072]{1,0:T(2,128)}, u32[]{:S(2)}, u32[]{:S(2)}) collective-permute-start(f32[2,131072]{1,0:T(2,128)} %collective-permute-done.5), channel_id=1, source_target_pairs={{0,16},{16,32},{32,48},{48,64},{64,80},{80,96},{96,112},{112,128},... | collective-permute-start | bytes 3145736 | tf_op jit(solution)/shard_map/ppermute | solution.py:35
  274.2 18.3 %collective-permute-done.6 = f32[2,131072]{1,0:T(2,128)} collective-permute-done((f32[2,131072]{1,0:T(2,128)}, f32[2,131072]{1,0:T(2,128)}, u32[]{:S(2)}, u32[]{:S(2)}) %collective-permute-start.6) | collective-permute-done | bytes 1048608 | tf_op jit(solution)/shard_map/ppermute | solution.py:35
  292.5 3.7 collective-permute-start.7
  296.6 11.3 %convolution_bitcast_fusion.3 = f32[2,1,2]{2,0,1:T(2,128)S(1)} fusion(f32[2,131072]{1,0:T(2,128)} %reshape_reshape.3, f32[2,131072]{1,0:T(2,128)} %copy-done.14), kind=kOutput, calls=%fused_computation.102 | convolution fusion | flops 6291456 | bytes 2097168 | tf_op jit(solution)/shard_map/sc,jc->sj/dot_general | solution.py:93
  307.9 11.0 %convolution_bitcast_fusion.2 = f32[2,1,2]{2,0,1:T(2,128)S(1)} fusion(f32[2,131072]{1,0:T(2,128)S(1)} %copy-done.6, f32[2,131072]{1,0:T(2,128)} %collective-permute-done.5), kind=kOutput, calls=%fused_computation.101 | convolution fusion | flops 6291456 | bytes 2097168 | tf_op jit(solution)/shard_map/sc,jc->sj/dot_general | solution.py:93
  318.9 10.9 %convolution_bitcast_fusion.1 = f32[2,1,2]{2,0,1:T(2,128)S(1)} fusion(f32[2,131072]{1,0:T(2,128)S(1)} %copy-done.6, f32[2,131072]{1,0:T(2,128)} %collective-permute-done.6), kind=kOutput, calls=%fused_computation.100 | convolution fusion | flops 6291456 | bytes 2097168 | tf_op jit(solution)/shard_map/sc,jc->sj/dot_general | solution.py:93
  329.8 9.7 %convolution_bitcast_fusion = f32[2,1,2]{2,0,1:T(2,128)S(1)} fusion(f32[2,131072]{1,0:T(2,128)S(1)} %copy-done.6, f32[2,131072]{1,0:T(2,128)S(1)} %collective-permute-done.7), kind=kOutput, calls=%fused_computation.99 | convolution fusion | flops 6291456 | bytes 2097168 | tf_op jit(solution)/shard_map/sc,jc->sj/dot_general | solution.py:93
  339.5 33.7 %all-reduce.2 = (f32[2,128]{1,0:T(2,128)S(1)}, f32[2,4,2]{2,0,1:T(2,128)S(1)}) all-reduce(f32[2,128]{1,0:T(2,128)S(1)} %fusion.55, f32[2,4,2]{2,0,1:T(2,128)S(1)} %pad_maximum_fusion.2), channel_id=1, replica_groups=mesh['shot'=16,'slab'=16] {'slab'}, use_global_device_ids=true, to_apply=%region_3.4 | all-reduce | flops 272 | bytes 2176 | tf_op jit(solution)/shard_map/psum | solution.py:150
  (57 shorter events, 11.2 us)
Async XLA Ops:
  0.6 11.6 %copy-start.9 = (s32[3]{0:T(128)S(1)}, s32[3]{0:T(128)}, u32[]{:S(2)}) copy-start(s32[3]{0:T(128)} %param.20) | copy-start | bytes 40
  0.6 14.2 %copy-start.11 = (f32[2,2,128]{2,1,0:T(2,128)S(1)}, f32[2,2,128]{2,1,0:T(2,128)}, u32[]{:S(2)}) copy-start(f32[2,2,128]{2,1,0:T(2,128)} %param.16) | copy-start | bytes 6148
  0.7 14.3 %copy-start.10 = (s32[2,128]{1,0:T(2,128)S(1)}, s32[2,128]{1,0:T(2,128)}, u32[]{:S(2)}) copy-start(s32[2,128]{1,0:T(2,128)} %param.17) | copy-start | bytes 3076
  0.7 14.3 %copy-start.3 = (f32[16,128,128]{2,1,0:T(8,128)S(1)}, f32[16,128,128]{2,1,0:T(8,128)}, u32[]{:S(2)}) copy-start(f32[16,128,128]{2,1,0:T(8,128)} %param.12) | copy-start | bytes 3145732
  3.1 14.4 %collective-permute-start.1 = (f32[2,4,128,128]{3,2,1,0:T(8,128)}, f32[2,4,128,128]{3,2,1,0:T(8,128)}, u32[]{:S(2)}, u32[]{:S(2)}) collective-permute-start(f32[2,4,128,128]{3,2,1,0:T(8,128)} %get-tuple-element.18), channel_id=1, source_target_pairs={{0,1},{1,2},{2,3},{3,4},{4,5},{5,6},{6,7},{7,8},{8,9},{9,10},{10,1... | collective-permute-start | bytes 1572872 | tf_op jit(solution)/shard_map/ppermute | solution.py:24
  5.0 16.9 %collective-permute-start = (f32[2,4,128,128]{3,2,1,0:T(8,128)}, f32[2,4,128,128]{3,2,1,0:T(8,128)}, u32[]{:S(2)}, u32[]{:S(2)}) collective-permute-start(f32[2,4,128,128]{3,2,1,0:T(8,128)} %get-tuple-element.19), channel_id=1, source_target_pairs={{1,0},{2,1},{3,2},{4,3},{5,4},{6,5},{7,6},{8,7},{9,8},{10,9},{11,1... | collective-permute-start | bytes 1572872 | tf_op jit(solution)/shard_map/ppermute | solution.py:26
  15.0 1.9 copy-start.12
  15.0 1.8 copy-start.13
  15.1 4.3 %copy-start = (f32[2,16,128,128]{3,2,1,0:T(8,128)S(1)}, f32[2,16,128,128]{3,2,1,0:T(8,128)}, u32[]{:S(2)}) copy-start(f32[2,16,128,128]{3,2,1,0:T(8,128)} %param.14) | copy-start | bytes 6291460
  78.4 19.0 %copy-start.2 = (f32[2,16,128,128]{3,2,1,0:T(8,128)}, f32[2,16,128,128]{3,2,1,0:T(8,128)S(1)}, u32[]{:S(2)}) copy-start(f32[2,16,128,128]{3,2,1,0:T(8,128)S(1)} %broadcast_divide_fusion) | copy-start | bytes 6291460
  78.5 11.5 %collective-permute-start.2 = (f32[2,4,128,128]{3,2,1,0:T(8,128)S(1)}, f32[2,4,128,128]{3,2,1,0:T(8,128)S(1)}, u32[]{:S(2)}, u32[]{:S(2)}) collective-permute-start(f32[2,4,128,128]{3,2,1,0:T(8,128)S(1)} %get-tuple-element.14), channel_id=1, source_target_pairs={{1,0},{2,1},{3,2},{4,3},{5,4},{6,5},{7,6},{8,7},{9,8},{10,9},{11,1... | collective-permute-start | bytes 1572872 | tf_op jit(solution)/shard_map/ppermute | solution.py:26
  83.4 14.1 %collective-permute-start.3 = (f32[2,4,128,128]{3,2,1,0:T(8,128)S(1)}, f32[2,4,128,128]{3,2,1,0:T(8,128)S(1)}, u32[]{:S(2)}, u32[]{:S(2)}) collective-permute-start(f32[2,4,128,128]{3,2,1,0:T(8,128)S(1)} %get-tuple-element.15), channel_id=1, source_target_pairs={{0,1},{1,2},{2,3},{3,4},{4,5},{5,6},{6,7},{7,8},{8,9},{9,10},{10,1... | collective-permute-start | bytes 1572872 | tf_op jit(solution)/shard_map/ppermute | solution.py:24
  90.1 7.4 %copy-start.4 = (f32[2,4,128,128]{3,2,1,0:T(8,128)}, f32[2,4,128,128]{3,2,1,0:T(8,128)S(1)}, u32[]{:S(2)}) copy-start(f32[2,4,128,128]{3,2,1,0:T(8,128)S(1)} %collective-permute-done.2) | copy-start | bytes 1572868
  97.5 0.8 copy-start.5
  140.0 36.3 %copy-start.1 = (f32[2,16,128,128]{3,2,1,0:T(8,128)S(1)}, f32[2,16,128,128]{3,2,1,0:T(8,128)}, u32[]{:S(2)}) copy-start(f32[2,16,128,128]{3,2,1,0:T(8,128)} %scatter_fusion) | copy-start | bytes 6291460
  220.6 52.0 %copy-start.8 = (s32[16,128]{1,0:T(8,128)S(1)}, s32[16,128]{1,0:T(8,128)}, u32[]{:S(2)}) copy-start(s32[16,128]{1,0:T(8,128)} %param.21) | copy-start | bytes 24580
  220.6 52.0 %copy-start.7 = (s32[128,128]{1,0:T(8,128)S(1)}, s32[128,128]{1,0:T(8,128)}, u32[]{:S(2)}) copy-start(s32[128,128]{1,0:T(8,128)} %param.22) | copy-start | bytes 196612
  222.6 73.5 %copy-start.15 = (s32[128,128]{1,0:T(8,128)S(1)}, s32[128,128]{1,0:T(8,128)}, u32[]{:S(2)}) copy-start(s32[128,128]{1,0:T(8,128)} %param.23) | copy-start | bytes 196612
  222.6 23.1 %collective-permute-start.4 = (f32[2,131072]{1,0:T(2,128)}, f32[2,131072]{1,0:T(2,128)S(1)}, u32[]{:S(2)}, u32[]{:S(2)}) collective-permute-start(f32[2,131072]{1,0:T(2,128)} %reshape_reshape.3), channel_id=1, source_target_pairs={{0,16},{16,32},{32,48},{48,64},{64,80},{80,96},{96,112},{112,128},... | collective-permute-start | bytes 3145736 | tf_op jit(solution)/shard_map/ppermute | solution.py:35
  245.7 23.1 %copy-start.14 = (f32[2,131072]{1,0:T(2,128)}, f32[2,131072]{1,0:T(2,128)S(1)}, u32[]{:S(2)}) copy-start(f32[2,131072]{1,0:T(2,128)S(1)} %collective-permute-done.4) | copy-start | bytes 3145732
  245.7 23.1 %collective-permute-start.5 = (f32[2,131072]{1,0:T(2,128)S(1)}, f32[2,131072]{1,0:T(2,128)}, u32[]{:S(2)}, u32[]{:S(2)}) collective-permute-start(f32[2,131072]{1,0:T(2,128)S(1)} %collective-permute-done.4), channel_id=1, source_target_pairs={{0,16},{16,32},{32,48},{48,64},{64,80},{80,96},{96,112},{112,128},... | collective-permute-start | bytes 3145736 | tf_op jit(solution)/shard_map/ppermute | solution.py:35
  268.8 23.7 %collective-permute-start.6 = (f32[2,131072]{1,0:T(2,128)}, f32[2,131072]{1,0:T(2,128)}, u32[]{:S(2)}, u32[]{:S(2)}) collective-permute-start(f32[2,131072]{1,0:T(2,128)} %collective-permute-done.5), channel_id=1, source_target_pairs={{0,16},{16,32},{32,48},{48,64},{64,80},{80,96},{96,112},{112,128},... | collective-permute-start | bytes 3145736 | tf_op jit(solution)/shard_map/ppermute | solution.py:35
  292.5 37.3 %collective-permute-start.7 = (f32[2,131072]{1,0:T(2,128)}, f32[2,131072]{1,0:T(2,128)S(1)}, u32[]{:S(2)}, u32[]{:S(2)}) collective-permute-start(f32[2,131072]{1,0:T(2,128)} %collective-permute-done.6), channel_id=1, source_target_pairs={{0,16},{16,32},{32,48},{48,64},{64,80},{80,96},{96,112},{112,128},... | collective-permute-start | bytes 3145736 | tf_op jit(solution)/shard_map/ppermute | solution.py:35
  296.6 11.3 %copy-start.6 = (f32[2,131072]{1,0:T(2,128)S(1)}, f32[2,131072]{1,0:T(2,128)}, u32[]{:S(2)}) copy-start(f32[2,131072]{1,0:T(2,128)} %reshape_reshape.3) | copy-start | bytes 3145732
where the time goes:
time: 381 us; the launch traced here: 375 us
  other arithmetic  141 us (37%)
  waiting for transfers between devices  69.8 us (18%)
  local copies, waits for them, and re-layouts  53.1 us (14%)
  matrix products  43.3 us (11%)
  blocking collectives  33.7 us (9%)
  starting transfers between devices  30.9 us (8%)
    scatter-add x2, other arithmetic, inject(): return jnp.zeros((shot_count, depth, cells_x, cells_y), jnp.float32).at[s...  72.5 us
    ppermute x4, waiting for transfers between devices, from_behind(): lax.ppermute(array, axis, [(i, (i + by) % peers) for i in range(peers)])  57.4 us
    add x2, other arithmetic, local(): 2.0 * current - (1.0 - damping) * previous  49.7 us
    dot_general x4, matrix products, lag_product(): jnp.einsum('sc,jc->sj', mine, theirs, precision=lax.Precision.HIGHEST)  42.9 us
    psum x1, blocking collectives, local(): sketch = lax.psum(partial_sketch, 'slab') * sketch_scale  33.7 us
    slice x1, local copies, waits for them, and re-layouts, local(): widened[..., 1::2]  19.4 us
    slice x1, local copies, waits for them, and re-layouts, local(): widened[..., 0::2] + widened[..., 1::2]  19.2 us
    ppermute x4, starting transfers between devices, from_behind(): lax.ppermute(array, axis, [(i, (i + by) % peers) for i in range(peers)])  14.5 us
  transfers between devices with their start and end apart: 8, of which 6 were waited for; matrix products, arithmetic and copies ran while one was open for 11% of the time, Pallas kernels for 0%

commit v1 on v0

v1 whole, which is shorter than its diff:
```python
import functools
import math

import jax
import jax.numpy as jnp
import ml_dtypes
import numpy as np
from jax import lax
from jax.experimental import pallas as pl
from jax.experimental.pallas import tpu as pltpu
from jax.sharding import PartitionSpec as P

LAGS = 4
REACH = 4
TAPS = (-205.0 / 72.0, 8.0 / 5.0, -1.0 / 5.0, 8.0 / 315.0, -1.0 / 560.0)
CENTRE = 3.0 * TAPS[0]
DAMP_PEAK = 0.3
F32 = jnp.float32
BF16 = jnp.bfloat16
VMEM_BYTES = 24 * 1024 * 1024


def band_parts(cells):
    index = np.arange(cells)
    apart = np.abs(index[:, None] - index[None, :])
    band = np.zeros((cells, cells), np.float32)
    for offset in range(1, REACH + 1):
        band[apart == offset] = TAPS[offset]
    high = band.astype(ml_dtypes.bfloat16)
    low = (band - high.astype(np.float32)).astype(ml_dtypes.bfloat16)
    return high, low


def pool_matrix(cells_y):
    half = cells_y // 2
    pool = np.zeros((2 * cells_y, 2 * half), np.float32)
    index = np.arange(cells_y)
    pool[index, index // 2] = 0.5
    pool[cells_y + index, half + index // 2] = 0.5
    return pool.astype(ml_dtypes.bfloat16)


def dot(left, right):
    return lax.dot_general(left, right, (((1,), (0,)), ((), ())), preferred_element_type=F32)


def dot_rows(left, right):
    return lax.dot_general(left, right, (((1,), (1,)), ((), ())), preferred_element_type=F32)


def two_parts(values):
    high = values.astype(BF16)
    low = (values - high.astype(F32)).astype(BF16)
    return high, low


def along_xy(plane, band_y, band_x):
    high, low = two_parts(plane)
    return dot(jnp.concatenate([high, low, high], axis=1), band_y) + dot(
        band_x, jnp.concatenate([high, low, high], axis=0)
    )


def ramp_squared(index, length, thickness):
    distance = jnp.minimum(index, length - 1 - index).astype(F32)
    reach = jnp.full(index.shape, thickness, jnp.int32).astype(F32)
    ramp = jnp.maximum((reach - distance) / reach, 0.0)
    return ramp * ramp


def begin_kernel(
    total_z,
    pml,
    courant,
    prev,
    curr,
    traces,
    place_z,
    place_x,
    place_y,
    band_y,
    band_x,
    updated,
    rest,
    gain_self,
    gain_lap,
    ramp_z,
    ramp_xy,
    inject,
):
    cells_z, cells_x, cells_y = courant.shape
    shots = curr.shape[0]
    first_z = lax.axis_index("slab") * cells_z
    plane = (cells_x, cells_y)
    row = lax.broadcasted_iota(jnp.int32, plane, 0)
    column = lax.broadcasted_iota(jnp.int32, plane, 1)
    ramp_z[...] = ramp_squared(
        lax.broadcasted_iota(jnp.int32, ramp_z.shape, 0) + first_z, total_z, pml[0]
    )
    ramp_xy[...] = ramp_squared(row, cells_x, pml[1]) + ramp_squared(column, cells_y, pml[2])
    receivers = traces.shape[2]
    for shot in range(shots):
        cell = lax.broadcasted_iota(jnp.int32, (cells_y, receivers), 0)
        here = cell == place_y[shot : shot + 1, :]
        for instant in range(2):
            high, low = two_parts(jnp.where(here, traces[shot, instant : instant + 1, :], 0.0))
            span = slice(instant * cells_y, (instant + 1) * cells_y)
            inject[shot, span, :receivers] = high
            inject[shot, span, receivers:] = low
    line = lax.broadcasted_iota(jnp.int32, (cells_x, receivers), 0)

    @pl.loop(0, cells_z)
    def _(z):
        damping = DAMP_PEAK * (ramp_z[pl.ds(z, 1), :] + ramp_xy[...])
        scale = 1.0 / (1.0 + damping)
        speed = courant[z]
        lap_gain = scale * (speed * speed)
        self_gain = 2.0 * scale + CENTRE * lap_gain
        prev_gain = scale * (1.0 - damping)
        gain_self[z] = self_gain
        gain_lap[z] = lap_gain
        for shot in range(shots):
            now = curr[shot, z]
            lap = along_xy(now, band_y[...], band_x[...])
            for offset in range(1, REACH + 1):
                below = jnp.where(z - offset >= 0, TAPS[offset], 0.0)
                above = jnp.where(z + offset < cells_z, TAPS[offset], 0.0)
                lap += below * curr[shot, jnp.maximum(z - offset, 0)]
                lap += above * curr[shot, jnp.minimum(z + offset, cells_z - 1)]
            code = (place_z[shot : shot + 1, :] - first_z - z) * cells_x + place_x[shot : shot + 1, :]
            mark = jnp.where(line == code, 1.0, 0.0).astype(BF16)
            source = dot_rows(jnp.concatenate([mark, mark], axis=1), inject[shot])
            updated[shot, z] = (
                self_gain * now
                - prev_gain * prev[shot, z]
                + lap_gain * lap
                + scale * source[:, :cells_y]
            )
            rest[shot, z] = scale * source[:, cells_y:] - prev_gain * now


def halo_terms(halo, shot, layer, upper):
    total = None
    for offset in range(1, REACH + 1):
        at = layer + offset - REACH if upper else layer - offset + REACH
        if 0 <= at < REACH:
            term = TAPS[offset] * halo[shot, at]
            total = term if total is None else total + term
    return total


def edge_kernel(upper, partial, halo, gain_lap, out):
    @pl.loop(0, partial.shape[0])
    def _(shot):
        for layer in range(REACH):
            out[shot, layer] = partial[shot, layer] + gain_lap[layer] * halo_terms(
                halo, shot, layer, upper
            )


def emit(gradient, shot, layer, spread_y, weight_z, pool, chunks, total, lines):
    rounded = gradient.astype(BF16)
    total[shot] += dot(rounded, spread_y[...]) * weight_z
    lines[...] = rounded.astype(F32)
    half = lines.shape[0] // 2
    even = lines[pl.ds(0, half, stride=2), :].astype(BF16)
    odd = lines[pl.ds(1, half, stride=2), :].astype(BF16)
    coarse = dot(jnp.concatenate([even, odd], axis=1), pool[...])
    part = chunks.shape[2]
    pieces = half // part
    for piece in range(pieces):
        chunks[layer * pieces + piece, shot] = coarse[piece * part : (piece + 1) * part]


def middle_kernel(
    partial,
    low,
    high,
    rest,
    gain_self,
    gain_lap,
    snaps,
    omega_z,
    omega_x,
    omega_y,
    band_y,
    band_x,
    pool,
    chunks,
    edge_low,
    edge_high,
    sketch,
    wave,
    total,
    spread_y,
    lines,
    sems,
):
    shots, cells_z = wave.shape[:2]
    last = cells_z - REACH
    copies = [
        pltpu.make_async_copy(low, wave.at[:, pl.ds(0, REACH)], sems.at[0]),
        pltpu.make_async_copy(
            partial.at[:, pl.ds(REACH, last - REACH)],
            wave.at[:, pl.ds(REACH, last - REACH)],
            sems.at[1],
        ),
        pltpu.make_async_copy(high, wave.at[:, pl.ds(last, REACH)], sems.at[2]),
    ]
    for copy in copies:
        copy.start()
    spread_y[...] = omega_y[...].astype(F32).astype(BF16)
    total[...] = jnp.zeros_like(total)
    for copy in copies:
        copy.wait()

    def gradient_at(shot, z, lap):
        now = wave[shot, z]
        later = gain_self[z] * now + rest[shot, z] + gain_lap[z] * lap
        return now * snaps[shot, 0, z].astype(F32) + later * snaps[shot, 1, z].astype(F32)

    @pl.loop(REACH, last)
    def _(z):
        weight_z = omega_z[pl.ds(z, 1), :].astype(F32)
        for shot in range(shots):
            lap = along_xy(wave[shot, z], band_y[...], band_x[...])
            for offset in range(1, REACH + 1):
                lap += TAPS[offset] * (wave[shot, z - offset] + wave[shot, z + offset])
            emit(
                gradient_at(shot, z, lap),
                shot,
                z - REACH,
                spread_y,
                weight_z,
                pool,
                chunks,
                total,
                lines,
            )

    @pl.loop(0, shots)
    def _(shot):
        for layer in range(REACH):
            for upper in (False, True):
                z = last + layer if upper else layer
                lap = along_xy(wave[shot, z], band_y[...], band_x[...])
                for offset in range(1, REACH + 1):
                    around = [
                        wave[shot, at]
                        for at in (z - offset, z + offset)
                        if 0 <= at < cells_z
                    ]
                    lap += TAPS[offset] * sum(around[1:], around[0])
                (edge_high if upper else edge_low)[shot, layer] = gradient_at(shot, z, lap)

    weights_x = omega_x[...].astype(F32)
    for shot in range(shots):
        sketch[shot : shot + 1, :] = jnp.sum(total[shot] * weights_x, axis=0, keepdims=True)


def finish_kernel(
    edge_low,
    edge_high,
    halo_low,
    halo_high,
    gain_low,
    gain_high,
    snaps_low,
    snaps_high,
    omega_z,
    omega_x,
    omega_y,
    pool,
    before,
    chunks,
    sketch,
    total,
    spread_y,
    lines,
):
    shots = edge_low.shape[0]
    cells_z = omega_z.shape[0]
    spread_y[...] = omega_y[...].astype(F32).astype(BF16)
    total[...] = jnp.zeros_like(total)
    sides = (
        (edge_low, halo_low, gain_low, snaps_low, False),
        (edge_high, halo_high, gain_high, snaps_high, True),
    )

    @pl.loop(0, shots)
    def _(shot):
        for layer in range(REACH):
            for edge, halo, gain, snaps, upper in sides:
                z = cells_z - REACH + layer if upper else layer
                terms = gain[layer] * halo_terms(halo, shot, layer, upper)
                gradient = edge[shot, layer] + terms * snaps[shot, 0, layer].astype(F32)
                emit(
                    gradient,
                    shot,
                    layer + (REACH if upper else 0),
                    spread_y,
                    omega_z[z : z + 1, :].astype(F32),
                    pool,
                    chunks,
                    total,
                    lines,
                )

    weights_x = omega_x[...].astype(F32)
    for shot in range(shots):
        sketch[shot : shot + 1, :] = before[shot : shot + 1, :] + jnp.sum(
            total[shot] * weights_x, axis=0, keepdims=True
        )


def gram_kernel(first, second, out):
    shots = out.shape[0]
    part = first.shape[0] // shots
    gram = jnp.zeros((2 * shots, 2 * shots), F32)
    for chunk in (first, second):

        def add(step, gram):
            rows = [
                chunk[pl.ds(2 * step + index, shots, stride=part), :] for index in range(2)
            ]
            high, low = two_parts(jnp.concatenate(rows, axis=1))
            both = jnp.concatenate([high, low], axis=0)
            return gram + dot_rows(both, both)

        gram = lax.fori_loop(0, part // 2, add, gram)
    folded = (gram[:shots, :shots] + gram[shots:, shots:]) + (
        gram[:shots, shots:] + gram[shots:, :shots]
    )
    out[...] = jnp.zeros_like(out)
    out[:, :shots] = folded


def spec(block=None, index=None):
    if block is None:
        return pl.BlockSpec(memory_space=pltpu.VMEM)
    return pl.BlockSpec(block, lambda step: index)


def run(kernel, out_shape, in_specs=None, out_specs=None, scratch=(), flops=0, moved=0, grid=None):
    options = {}
    if grid is not None:
        options["grid"] = grid
    return pl.pallas_call(
        kernel,
        out_shape=out_shape,
        in_specs=in_specs,
        out_specs=out_specs,
        scratch_shapes=scratch,
        compiler_params=pltpu.CompilerParams(vmem_limit_bytes=VMEM_BYTES),
        cost_estimate=pl.CostEstimate(flops=flops, bytes_accessed=moved, transcendentals=0),
        **options,
    )


def local(
    courant,
    adj_prev,
    adj_curr,
    forward_snaps,
    traces,
    receiver_z,
    receiver_x,
    receiver_y,
    pml_cells,
    omega_z,
    omega_x,
    omega_y,
):
    shots, cells_z, cells_x, cells_y = adj_curr.shape
    slabs = lax.axis_size("slab")
    groups = lax.axis_size("shot")
    total_z = cells_z * slabs
    last = cells_z - REACH
    inner = last - REACH
    rank = omega_z.shape[1]
    receivers = traces.shape[2]
    half_x = cells_x // 2
    part = inner * half_x // groups
    shape = jax.ShapeDtypeStruct
    plane = (cells_x, cells_y)
    high, low = band_parts(cells_y)
    band_y = jnp.asarray(np.concatenate([high, high, low], axis=0))
    high, low = band_parts(cells_x)
    band_x = jnp.asarray(np.concatenate([high, high, low], axis=1))
    pool = jnp.asarray(pool_matrix(cells_y))

    def from_below(layers):
        return lax.ppermute(layers, "slab", [(i, i + 1) for i in range(slabs - 1)])

    def from_above(layers):
        return lax.ppermute(layers, "slab", [(i + 1, i) for i in range(slabs - 1)])

    halo_low = from_below(adj_curr[:, last:])
    halo_high = from_above(adj_curr[:, :REACH])

    vmem = spec()
    field = shape((shots, cells_z) + plane, F32)
    gain = shape((cells_z,) + plane, F32)
    edge = shape((shots, REACH) + plane, F32)
    updated, rest, gain_self, gain_lap = run(
        functools.partial(begin_kernel, total_z),
        [field, field, gain, gain],
        in_specs=[pl.BlockSpec(memory_space=pltpu.SMEM)] + [vmem] * 9,
        out_specs=[vmem] * 4,
        scratch=[
            pltpu.VMEM((cells_z, cells_y), F32),
            pltpu.VMEM(plane, F32),
            pltpu.VMEM((shots, 2 * cells_y, 2 * receivers), BF16),
        ],
        flops=2 * 10**9,
        moved=11 * 2**20,
    )(
        pml_cells,
        courant,
        adj_prev,
        adj_curr,
        traces,
        receiver_z,
        receiver_x,
        receiver_y,
        band_y,
        band_x,
    )

    layers4 = (shots, REACH) + plane
    gains4 = (REACH,) + plane

    def complete(halo, upper):
        side = last // REACH if upper else 0
        return run(
            functools.partial(edge_kernel, upper),
            edge,
            in_specs=[
                spec(layers4, (0, side, 0, 0)),
                spec(layers4, (0, 0, 0, 0)),
                spec(gains4, (side, 0, 0)),
            ],
            out_specs=spec(layers4, (0, 0, 0, 0)),
            grid=(1,),
            flops=10**7,
            moved=2 * 2**20,
        )(updated, halo, gain_lap)

    edge_low = complete(halo_low, False)
    edge_high = complete(halo_high, True)
    next_high = from_above(edge_low)
    next_low = from_below(edge_high)

    chunk = shape((groups, shots, part, cells_y), F32)
    any_space = pl.BlockSpec(memory_space=pl.ANY)
    scratch_emit = [
        pltpu.VMEM((shots, cells_x, rank), F32),
        pltpu.VMEM((cells_y, rank), BF16),
        pltpu.VMEM(plane, F32),
    ]
    chunks_mid, part_low, part_high, sketch_mid = run(
        middle_kernel,
        [chunk, edge, edge, shape((shots, rank), F32)],
        in_specs=[any_space] * 3 + [vmem] * 10,
        out_specs=[vmem] * 4,
        scratch=[pltpu.VMEM((shots, cells_z) + plane, F32)]
        + scratch_emit
        + [pltpu.SemaphoreType.DMA((3,))],
        flops=2 * 10**9,
        moved=11 * 2**20,
    )(
        updated,
        edge_low,
        edge_high,
        rest,
        gain_self,
        gain_lap,
        forward_snaps,
        omega_z,
        omega_x,
        omega_y,
        band_y,
        band_x,
        pool,
    )
    got_mid = lax.all_to_all(chunks_mid, "shot", 0, 0, tiled=True)

    snap4 = (shots, 1, REACH) + plane
    top = last // REACH
    whole2 = lambda array: spec(array.shape, (0,) * array.ndim)
    chunks_edge, sketch_part = run(
        finish_kernel,
        [chunk, shape((shots, rank), F32)],
        in_specs=[spec(layers4, (0, 0, 0, 0))] * 4
        + [
            spec(gains4, (0, 0, 0)),
            spec(gains4, (top, 0, 0)),
            spec(snap4, (0, 1, 0, 0, 0)),
            spec(snap4, (0, 1, top, 0, 0)),
        ]
        + [whole2(omega_z), whole2(omega_x), whole2(omega_y), whole2(pool), whole2(sketch_mid)],
        out_specs=[spec(chunk.shape, (0, 0, 0, 0)), spec((shots, rank), (0, 0))],
        scratch=scratch_emit,
        grid=(1,),
        flops=5 * 10**8,
        moved=5 * 2**20,
    )(
        part_low,
        part_high,
        next_low,
        next_high,
        gain_lap,
        gain_lap,
        forward_snaps,
        forward_snaps,
        omega_z,
        omega_x,
        omega_y,
        pool,
        sketch_mid,
    )
    got_edge = lax.all_to_all(chunks_edge, "shot", 0, 0, tiled=True)

    def layers_of(chunks, count):
        folded = chunks.reshape(count, half_x // part, shots, part, cells_y)
        return folded.transpose(2, 0, 1, 3, 4).reshape(shots, count, half_x, cells_y)

    edges = layers_of(chunks_edge, 2 * REACH)
    coarse = jnp.concatenate(
        [edges[:, :REACH], layers_of(chunks_mid, inner), edges[:, REACH:]], axis=1
    ).reshape(shots, cells_z, half_x * cells_y)

    all_shots = groups * shots
    gram = run(
        gram_kernel,
        shape((all_shots, cells_y), F32),
        in_specs=[vmem, vmem],
        out_specs=vmem,
        flops=10**8,
        moved=2**20,
    )(
        got_mid.reshape(all_shots * part, cells_y),
        got_edge.reshape(all_shots * part, cells_y),
    )
    mine = lax.all_to_all(gram.reshape(groups, shots, cells_y), "shot", 0, 0, tiled=True).sum(0)
    terms = jnp.concatenate([sketch_part, mine], axis=0)
    sums = lax.all_to_all(
        jnp.broadcast_to(terms[None], (slabs,) + terms.shape), "slab", 0, 0, tiled=True
    ).sum(0)
    sketch = sums[:shots] * (1.0 / math.sqrt(total_z * cells_x * cells_y))
    group = lax.axis_index("shot")
    partner = jnp.remainder(group - 1 - jnp.arange(LAGS, dtype=jnp.int32), groups)
    wanted = (partner[:, None] * shots + jnp.arange(shots, dtype=jnp.int32)[None, :]).reshape(-1)
    picked = wanted[:, None] == jnp.arange(cells_y, dtype=jnp.int32)[None, :]
    band = jnp.sum(jnp.where(picked[None], sums[shots:, None, :], 0.0), axis=-1)
    gram_band = band.reshape(shots, LAGS, shots) * (
        1.0 / math.sqrt(total_z * cells_x * cells_y // 2)
    )
    return (sketch, coarse, gram_band)


def solution(mesh):
    return jax.shard_map(
        local,
        mesh=mesh,
        in_specs=(
            P("slab", None, None),
            P("shot", "slab", None, None),
            P("shot", "slab", None, None),
            P("shot", None, "slab", None, None),
            P("shot", None, None),
            P("shot", None),
            P("shot", None),
            P("shot", None),
            P(),
            P("slab", None),
            P(),
            P(),
        ),
        out_specs=(P("shot", None), P("shot", "slab", None), P("shot", None, None)),
        check_vma=False,
    )
```

time: 381 us -> 120 us (0.31)
  the two profiles are of different devices: /device:TPU:120 before, /device:TPU:1 now
where the time goes in v1:
time: 120 us; the launch traced here: 119 us
  starting transfers between devices  43.5 us (36%)
  waiting for transfers between devices  33.8 us (28%)
  Pallas kernels  21 us (18%)
  local copies, waits for them, and re-layouts  17.5 us (15%)
  other arithmetic  2.03 us (2%)
    unnamed x49, local copies, waits for them, and re-layouts  13.7 us
    all_to_all x1, waiting for transfers between devices, local(): got_edge = lax.all_to_all(chunks_edge, 'shot', 0, 0, tiled=True)  11.1 us
    all_to_all x1, starting transfers between devices, local(): lax.all_to_all(jnp.broadcast_to(terms[None], (slabs,) + terms.shape), 'sl...  10.8 us
    all_to_all x1, starting transfers between devices, local(): got_mid = lax.all_to_all(chunks_mid, 'shot', 0, 0, tiled=True)  8.71 us
    all_to_all x1, starting transfers between devices, local(): got_edge = lax.all_to_all(chunks_edge, 'shot', 0, 0, tiled=True)  7.51 us
    all_to_all x1, waiting for transfers between devices, local(): lax.all_to_all(gram.reshape(groups, shots, cells_y), 'shot', 0, 0, tiled=...  7.32 us
    ppermute x2, starting transfers between devices, from_above(): return lax.ppermute(layers, 'slab', [(i + 1, i) for i in range(slabs - 1)])  7.07 us
    pallas_call x1, Pallas kernels, local(): run(functools.partial(begin_kernel, total_z), [field, field, gain, gain],...  6.94 us
  transfers between devices with their start and end apart: 8, of which 5 were waited for; matrix products, arithmetic and copies ran while one was open for 3% of the time, Pallas kernels for 7%

profile of v1, /device:TPU:1, one launch (start us, length us, event | category | flops | bytes accessed | tf_op | source)
XLA Modules:
  0.0 118.8 jit_solution(17749987336662904281)
XLA Ops:
  0.7 1.4 %fusion.2 = (f32[2,4,128,128]{3,2,1,0:T(8,128)S(1)}, f32[2,4,128,128]{3,2,1,0:T(8,128)S(1)}) fusion(f32[2,16,128,128]{3,2,1,0:T(8,128)} %curr.1), kind=kLoop, calls=%fused_computation.12 | loop fusion | bytes 2097152 | tf_op jit(solution)/shard_map/slice | solution.py:399
  2.1 5.1 %collective-permute-start.1 = (f32[2,4,128,128]{3,2,1,0:T(8,128)S(1)}, f32[2,4,128,128]{3,2,1,0:T(8,128)S(1)}, u32[]{:S(2)}, u32[]{:S(2)}) collective-permute-start(f32[2,4,128,128]{3,2,1,0:T(8,128)S(1)} %get-tuple-element.35), channel_id=1, source_target_pairs={{1,0},{2,1},{3,2},{4,3},{5,4},{6,5},{7,6},{8,7},{9,8},{10,9},{11,1... | collective-permute-start | bytes 1572872 | tf_op jit(solution)/shard_map/ppermute | solution.py:396
  7.3 1.9 %collective-permute-start = (f32[2,4,128,128]{3,2,1,0:T(8,128)S(1)}, f32[2,4,128,128]{3,2,1,0:T(8,128)S(1)}, u32[]{:S(2)}, u32[]{:S(2)}) collective-permute-start(f32[2,4,128,128]{3,2,1,0:T(8,128)S(1)} %get-tuple-element.36), channel_id=1, source_target_pairs={{0,1},{1,2},{2,3},{3,4},{4,5},{5,6},{6,7},{7,8},{8,9},{9,10},{10,1... | collective-permute-start | bytes 1572872 | tf_op jit(solution)/shard_map/ppermute | solution.py:393
  9.2 0.9 copy-done.14
  10.1 0.9 copy-done.15
  11.0 1.6 %copy-done.17 = f32[2,16,128,128]{3,2,1,0:T(8,128)S(1)} copy-done((f32[2,16,128,128]{3,2,1,0:T(8,128)S(1)}, f32[2,16,128,128]{3,2,1,0:T(8,128)}, u32[]{:S(2)}) %copy-start.17) | copy-done | bytes 2097176
  12.6 1.2 %copy-done.18 = f32[16,128,128]{2,1,0:T(8,128)S(1)} copy-done((f32[16,128,128]{2,1,0:T(8,128)S(1)}, f32[16,128,128]{2,1,0:T(8,128)}, u32[]{:S(2)}) %copy-start.18) | copy-done | bytes 1048600
  14.5 0.7 copy-done.22
  15.2 6.9 %shard_map.166 = (f32[2,16,128,128]{3,2,1,0:T(8,128)S(1)}, f32[2,16,128,128]{3,2,1,0:T(8,128)S(1)}, f32[16,128,128]{2,1,0:T(8,128)S(1)}, f32[16,128,128]{2,1,0:T(8,128)S(1)}) custom-call(s32[3]{0:T(128)S(1)} %copy-done.23, f32[16,128,128]{2,1,0:T(8,128)S(1)} %copy-done.18, f32[2,16,128,128]{3,2,1,0:T(8,128)S(1)} %copy-done.17, ...), custom_call_target="tpu_custom_call" | custom-call | flops 2000000000 | bytes 11534336 | tf_op jit(solution)/shard_map/pallas_call | solution.py:405
  23.1 1.2 %copy-done = bf16[2,2,16,128,128]{4,3,2,1,0:T(8,128)(2,1)S(1)} copy-done((bf16[2,2,16,128,128]{4,3,2,1,0:T(8,128)(2,1)S(1)}, bf16[2,2,16,128,128]{4,3,2,1,0:T(8,128)(2,1)}, u32[]{:S(2)}) %copy-start) | copy-done | bytes 2097176
  24.3 6.2 %shard_map.169 = (f32[16,2,32,128]{3,2,1,0:T(8,128)S(1)}, f32[2,4,128,128]{3,2,1,0:T(8,128)S(1)}, f32[2,4,128,128]{3,2,1,0:T(8,128)S(1)}, f32[2,128]{1,0:T(2,128)S(1)}) custom-call(f32[2,16,128,128]{3,2,1,0:T(8,128)S(1)} %get-tuple-element.13.partial, f32[2,4,128,128]{3,2,1,0:T(8,128)S(1)} %shard_map.167.low, f32[2,4,128,128]{3,2,1,0:T(8,128)S(1)} %shard_map.168.high, ...), custom_call_target="tpu_custom_call" | custom-call | flops 2000000000 | bytes 11534336 | tf_op jit(solution)/shard_map/pallas_call | solution.py:461
  30.5 0.8 copy-done.1
  31.3 0.8 copy-done.7
  32.1 0.8 copy-done.9
  32.9 8.7 %all-to-all-start = ((f32[16,2,32,128]{3,2,1,0:T(8,128)}), f32[16,2,32,128]{3,2,1,0:T(8,128)}, u32[]{:S(2)}, u32[]{:S(2)}) async-start(f32[16,2,32,128]{3,2,1,0:T(8,128)} %copy-done.1), calls=%async_computation | async-start | bytes 1048576 | tf_op jit(solution)/shard_map/all_to_all | solution.py:486
  41.7 2.7 %collective-permute-start.2 = (f32[2,4,128,128]{3,2,1,0:T(8,128)}, f32[2,4,128,128]{3,2,1,0:T(8,128)S(1)}, u32[]{:S(2)}, u32[]{:S(2)}) collective-permute-start(f32[2,4,128,128]{3,2,1,0:T(8,128)} %copy-done.4), channel_id=1, source_target_pairs={{0,1},{1,2},{2,3},{3,4},{4,5},{5,6},{6,7},{7,8},{8,9},{9,10},{10,1... | collective-permute-start | bytes 1572872 | tf_op jit(solution)/shard_map/ppermute | solution.py:393
  44.3 1.9 %collective-permute-start.3 = (f32[2,4,128,128]{3,2,1,0:T(8,128)}, f32[2,4,128,128]{3,2,1,0:T(8,128)S(1)}, u32[]{:S(2)}, u32[]{:S(2)}) collective-permute-start(f32[2,4,128,128]{3,2,1,0:T(8,128)} %copy-done.5), channel_id=1, source_target_pairs={{1,0},{2,1},{3,2},{4,3},{5,4},{6,5},{7,6},{8,7},{9,8},{10,9},{11,1... | collective-permute-start | bytes 1572872 | tf_op jit(solution)/shard_map/ppermute | solution.py:396
  46.3 4.5 %collective-permute-done.2.halo_low = f32[2,4,128,128]{3,2,1,0:T(8,128)S(1)} collective-permute-done((f32[2,4,128,128]{3,2,1,0:T(8,128)}, f32[2,4,128,128]{3,2,1,0:T(8,128)S(1)}, u32[]{:S(2)}, u32[]{:S(2)}) %collective-permute-start.2) | collective-permute-done | bytes 524320 | tf_op jit(solution)/shard_map/ppermute | solution.py:393
  50.8 4.7 %collective-permute-done.3.halo_high = f32[2,4,128,128]{3,2,1,0:T(8,128)S(1)} collective-permute-done((f32[2,4,128,128]{3,2,1,0:T(8,128)}, f32[2,4,128,128]{3,2,1,0:T(8,128)S(1)}, u32[]{:S(2)}, u32[]{:S(2)}) %collective-permute-start.3) | collective-permute-done | bytes 524320 | tf_op jit(solution)/shard_map/ppermute | solution.py:396
  55.5 1.0 copy-done.8
  56.5 1.0 copy-done.10
  57.5 0.9 shard_map.170
  58.4 0.8 copy-done.2
  59.2 7.5 %all-to-all-start.1 = ((f32[16,2,32,128]{3,2,1,0:T(8,128)}), f32[16,2,32,128]{3,2,1,0:T(8,128)S(1)}, u32[]{:S(2)}, u32[]{:S(2)}) async-start(f32[16,2,32,128]{3,2,1,0:T(8,128)} %copy-done.2), calls=%async_computation.1 | async-start | bytes 1048576 | tf_op jit(solution)/shard_map/all_to_all | solution.py:522
  67.0 1.4 %copy.28 = f32[2,8,2,32,128]{4,1,3,2,0:T(8,128)S(1)} copy(f32[2,8,2,32,128]{4,3,0,2,1:T(8,128)} %bitcast.15) | data formatting | bytes 1048576 | tf_op jit(solution)/shard_map/transpose | solution.py:526
  68.4 11.1 %all-to-all-done.1 = f32[16,2,32,128]{3,2,1,0:T(8,128)S(1)} async-done(((f32[16,2,32,128]{3,2,1,0:T(8,128)}), f32[16,2,32,128]{3,2,1,0:T(8,128)S(1)}, u32[]{:S(2)}, u32[]{:S(2)}) %all-to-all-start.1) | async-done | bytes 524320 | tf_op jit(solution)/shard_map/all_to_all | solution.py:522
  79.5 6.7 %shard_map.171 = f32[32,128]{1,0:T(8,128)} custom-call(f32[1024,128]{1,0:T(8,128)} %bitcast.first, f32[1024,128]{1,0:T(8,128)S(1)} %bitcast.17), custom_call_target="tpu_custom_call" | custom-call | flops 100000000 | bytes 1048576 | tf_op jit(solution)/shard_map/pallas_call | solution.py:534
  86.2 4.9 %all-to-all-start.2 = ((f32[16,2,128]{2,1,0:T(2,128)}), f32[16,2,128]{2,1,0:T(2,128)S(1)}, u32[]{:S(2)}, u32[]{:S(2)}) async-start(f32[16,2,128]{2,1,0:T(2,128)} %bitcast.2), calls=%async_computation.2 | async-start | bytes 32768 | tf_op jit(solution)/shard_map/all_to_all | solution.py:545
  91.3 7.3 %all-to-all-done.2 = f32[16,2,128]{2,1,0:T(2,128)S(1)} async-done(((f32[16,2,128]{2,1,0:T(2,128)}), f32[16,2,128]{2,1,0:T(2,128)S(1)}, u32[]{:S(2)}, u32[]{:S(2)}) %all-to-all-start.2) | async-done | bytes 16416 | tf_op jit(solution)/shard_map/all_to_all | solution.py:545
  99.3 10.8 %all-to-all-start.3 = ((f32[16,4,128]{2,1,0:T(4,128)}), f32[16,4,128]{2,1,0:T(4,128)S(1)}, u32[]{:S(2)}, u32[]{:S(2)}) async-start(f32[16,4,128]{2,1,0:T(4,128)} %broadcast_in_dim.15), calls=%async_computation.3 | async-start | bytes 65536 | tf_op jit(solution)/shard_map/all_to_all | solution.py:547
  110.1 1.1 pad_maximum_fusion
  111.2 6.2 %all-to-all-done.3 = f32[16,4,128]{2,1,0:T(4,128)S(1)} async-done(((f32[16,4,128]{2,1,0:T(4,128)}), f32[16,4,128]{2,1,0:T(4,128)S(1)}, u32[]{:S(2)}, u32[]{:S(2)}) %all-to-all-start.3) | async-done | bytes 32800 | tf_op jit(solution)/shard_map/all_to_all | solution.py:547
  (58 shorter events, 4.3 us)
Async XLA Ops:
  0.6 8.6 %copy-start.6 = (f32[2,16,128,128]{3,2,1,0:T(8,128)S(1)}, f32[2,16,128,128]{3,2,1,0:T(8,128)}, u32[]{:S(2)}) copy-start(f32[2,16,128,128]{3,2,1,0:T(8,128)} %curr.1) | copy-start | bytes 6291460
  0.6 8.6 %copy-start.19 = (f32[2,2,128]{2,1,0:T(2,128)S(1)}, f32[2,2,128]{2,1,0:T(2,128)}, u32[]{:S(2)}) copy-start(f32[2,2,128]{2,1,0:T(2,128)} %traces.1) | copy-start | bytes 6148
  0.7 8.6 %copy-start.20 = (s32[2,128]{1,0:T(2,128)S(1)}, s32[2,128]{1,0:T(2,128)}, u32[]{:S(2)}) copy-start(s32[2,128]{1,0:T(2,128)} %place_z.1) | copy-start | bytes 3076
  0.7 8.6 %copy-start.23 = (s32[3]{0:T(128)S(1)}, s32[3]{0:T(128)}, u32[]{:S(2)}) copy-start(s32[3]{0:T(128)} %pml.1) | copy-start | bytes 40
  2.1 20.0 %collective-permute-start.1 = (f32[2,4,128,128]{3,2,1,0:T(8,128)S(1)}, f32[2,4,128,128]{3,2,1,0:T(8,128)S(1)}, u32[]{:S(2)}, u32[]{:S(2)}) collective-permute-start(f32[2,4,128,128]{3,2,1,0:T(8,128)S(1)} %get-tuple-element.35), channel_id=1, source_target_pairs={{1,0},{2,1},{3,2},{4,3},{5,4},{6,5},{7,6},{8,7},{9,8},{10,9},{11,1... | collective-permute-start | bytes 1572872 | tf_op jit(solution)/shard_map/ppermute | solution.py:396
  7.3 15.1 %collective-permute-start = (f32[2,4,128,128]{3,2,1,0:T(8,128)S(1)}, f32[2,4,128,128]{3,2,1,0:T(8,128)S(1)}, u32[]{:S(2)}, u32[]{:S(2)}) collective-permute-start(f32[2,4,128,128]{3,2,1,0:T(8,128)S(1)} %get-tuple-element.36), channel_id=1, source_target_pairs={{0,1},{1,2},{2,3},{3,4},{4,5},{5,6},{6,7},{7,8},{8,9},{9,10},{10,1... | collective-permute-start | bytes 1572872 | tf_op jit(solution)/shard_map/ppermute | solution.py:393
  9.2 0.9 copy-start.14
  10.1 0.9 copy-start.15
  11.0 1.6 %copy-start.17 = (f32[2,16,128,128]{3,2,1,0:T(8,128)S(1)}, f32[2,16,128,128]{3,2,1,0:T(8,128)}, u32[]{:S(2)}) copy-start(f32[2,16,128,128]{3,2,1,0:T(8,128)} %prev.1) | copy-start | bytes 6291460
  12.6 1.2 %copy-start.18 = (f32[16,128,128]{2,1,0:T(8,128)S(1)}, f32[16,128,128]{2,1,0:T(8,128)}, u32[]{:S(2)}) copy-start(f32[16,128,128]{2,1,0:T(8,128)} %courant.1) | copy-start | bytes 3145732
  13.8 0.7 copy-start.21
  14.5 0.7 copy-start.22
  22.3 0.8 copy-start.4
  22.3 2.0 %copy-start = (bf16[2,2,16,128,128]{4,3,2,1,0:T(8,128)(2,1)S(1)}, bf16[2,2,16,128,128]{4,3,2,1,0:T(8,128)(2,1)}, u32[]{:S(2)}) copy-start(bf16[2,2,16,128,128]{4,3,2,1,0:T(8,128)(2,1)} %snaps_high.1) | copy-start | bytes 6291460
  22.3 2.0 %copy-start.11 = (s32[128,128]{1,0:T(8,128)S(1)}, s32[128,128]{1,0:T(8,128)}, u32[]{:S(2)}) copy-start(s32[128,128]{1,0:T(8,128)} %omega_x.3) | copy-start | bytes 196612
  22.4 2.0 %copy-start.12 = (s32[128,128]{1,0:T(8,128)S(1)}, s32[128,128]{1,0:T(8,128)}, u32[]{:S(2)}) copy-start(s32[128,128]{1,0:T(8,128)} %omega_y.3) | copy-start | bytes 196612
  22.4 1.9 %copy-start.13 = (bf16[256,128]{1,0:T(8,128)(2,1)S(1)}, bf16[256,128]{1,0:T(8,128)(2,1)}, u32[]{:S(2)}) copy-start(bf16[256,128]{1,0:T(8,128)(2,1)} %constant.39.clone.pool) | copy-start | bytes 196612
  22.4 1.9 %copy-start.16 = (s32[16,128]{1,0:T(8,128)S(1)}, s32[16,128]{1,0:T(8,128)}, u32[]{:S(2)}) copy-start(s32[16,128]{1,0:T(8,128)} %omega_z.3) | copy-start | bytes 24580
  22.6 7.9 %copy-start.5 = (f32[2,4,128,128]{3,2,1,0:T(8,128)}, f32[2,4,128,128]{3,2,1,0:T(8,128)S(1)}, u32[]{:S(2)}) copy-start(f32[2,4,128,128]{3,2,1,0:T(8,128)S(1)} %shard_map.167.low) | copy-start | bytes 1572868
  30.5 0.8 copy-start.1
  31.3 0.8 copy-start.7
  32.1 0.8 copy-start.9
  32.9 26.3 %all-to-all-start = ((f32[16,2,32,128]{3,2,1,0:T(8,128)}), f32[16,2,32,128]{3,2,1,0:T(8,128)}, u32[]{:S(2)}, u32[]{:S(2)}) async-start(f32[16,2,32,128]{3,2,1,0:T(8,128)} %copy-done.1), calls=%async_computation | async-start | bytes 1048576 | tf_op jit(solution)/shard_map/all_to_all | solution.py:486
  41.7 9.1 %collective-permute-start.2 = (f32[2,4,128,128]{3,2,1,0:T(8,128)}, f32[2,4,128,128]{3,2,1,0:T(8,128)S(1)}, u32[]{:S(2)}, u32[]{:S(2)}) collective-permute-start(f32[2,4,128,128]{3,2,1,0:T(8,128)} %copy-done.4), channel_id=1, source_target_pairs={{0,1},{1,2},{2,3},{3,4},{4,5},{5,6},{6,7},{7,8},{8,9},{9,10},{10,1... | collective-permute-start | bytes 1572872 | tf_op jit(solution)/shard_map/ppermute | solution.py:393
  44.3 11.1 %collective-permute-start.3 = (f32[2,4,128,128]{3,2,1,0:T(8,128)}, f32[2,4,128,128]{3,2,1,0:T(8,128)S(1)}, u32[]{:S(2)}, u32[]{:S(2)}) collective-permute-start(f32[2,4,128,128]{3,2,1,0:T(8,128)} %copy-done.5), channel_id=1, source_target_pairs={{1,0},{2,1},{3,2},{4,3},{5,4},{6,5},{7,6},{8,7},{9,8},{10,9},{11,1... | collective-permute-start | bytes 1572872 | tf_op jit(solution)/shard_map/ppermute | solution.py:396
  55.5 1.0 copy-start.8
  56.5 1.0 copy-start.10
  58.4 0.8 copy-start.2
  59.2 9.1 %copy-start.3 = (f32[16,2,32,128]{3,2,1,0:T(8,128)S(1)}, f32[16,2,32,128]{3,2,1,0:T(8,128)}, u32[]{:S(2)}) copy-start(f32[16,2,32,128]{3,2,1,0:T(8,128)} %copy-done.2) | copy-start | bytes 1572868
  59.2 20.3 %all-to-all-start.1 = ((f32[16,2,32,128]{3,2,1,0:T(8,128)}), f32[16,2,32,128]{3,2,1,0:T(8,128)S(1)}, u32[]{:S(2)}, u32[]{:S(2)}) async-start(f32[16,2,32,128]{3,2,1,0:T(8,128)} %copy-done.2), calls=%async_computation.1 | async-start | bytes 1048576 | tf_op jit(solution)/shard_map/all_to_all | solution.py:522
  86.2 12.5 %all-to-all-start.2 = ((f32[16,2,128]{2,1,0:T(2,128)}), f32[16,2,128]{2,1,0:T(2,128)S(1)}, u32[]{:S(2)}, u32[]{:S(2)}) async-start(f32[16,2,128]{2,1,0:T(2,128)} %bitcast.2), calls=%async_computation.2 | async-start | bytes 32768 | tf_op jit(solution)/shard_map/all_to_all | solution.py:545
  99.3 18.1 %all-to-all-start.3 = ((f32[16,4,128]{2,1,0:T(4,128)}), f32[16,4,128]{2,1,0:T(4,128)S(1)}, u32[]{:S(2)}, u32[]{:S(2)}) async-start(f32[16,4,128]{2,1,0:T(4,128)} %broadcast_in_dim.15), calls=%async_computation.3 | async-start | bytes 65536 | tf_op jit(solution)/shard_map/all_to_all | solution.py:547

commit v2 on v1

v2 whole, which is shorter than its diff:
```python
import functools
import math

import jax
import jax.numpy as jnp
import ml_dtypes
import numpy as np
from jax import lax
from jax.experimental import pallas as pl
from jax.experimental.pallas import tpu as pltpu
from jax.sharding import PartitionSpec as P

LAGS = 4
REACH = 4
WHOLE_TAPS = (None, 8064.0, -1008.0, 128.0, -9.0)
DIVISOR = 5040.0
CENTRE = 3.0 * (-205.0 / 72.0)
DAMP_PEAK = 0.3
F32 = jnp.float32
BF16 = jnp.bfloat16
VMEM_BYTES = 24 * 1024 * 1024


def band_matrix(cells):
    index = np.arange(cells)
    apart = np.abs(index[:, None] - index[None, :])
    band = np.zeros((cells, cells), np.float32)
    for offset in range(1, REACH + 1):
        band[apart == offset] = WHOLE_TAPS[offset]
    return band.astype(ml_dtypes.bfloat16)


def pool_matrix(cells_y):
    half = cells_y // 2
    pool = np.zeros((2 * cells_y, 2 * half), np.float32)
    index = np.arange(cells_y)
    pool[index, index // 2] = 0.5
    pool[cells_y + index, half + index // 2] = 0.5
    return pool.astype(ml_dtypes.bfloat16)


def dot(left, right):
    return lax.dot_general(left, right, (((1,), (0,)), ((), ())), preferred_element_type=F32)


def dot_rows(left, right):
    return lax.dot_general(left, right, (((1,), (1,)), ((), ())), preferred_element_type=F32)


def two_parts(values):
    high = values.astype(BF16)
    low = (values - high.astype(F32)).astype(BF16)
    return high, low


def along_xy(planes, band_y, band_x):
    parts = [two_parts(plane) for plane in planes]
    rows = [jnp.concatenate(pair, axis=1) for pair in parts]
    columns = [jnp.concatenate(pair, axis=0) for pair in parts]
    over_y = dot(jnp.concatenate(rows, axis=0), band_y[...])
    over_x = dot(band_x[...], jnp.concatenate(columns, axis=1))
    cells_x, cells_y = planes[0].shape
    return [
        over_y[shot * cells_x : (shot + 1) * cells_x] + over_x[:, shot * cells_y : (shot + 1) * cells_y]
        for shot in range(len(planes))
    ]


def along_z(field, shot, z, cells_z):
    total = None
    for offset in range(1, REACH + 1):
        tap = WHOLE_TAPS[offset]
        below = jnp.where(z - offset >= 0, tap, 0.0)
        above = jnp.where(z + offset < cells_z, tap, 0.0)
        term = below * field[shot, jnp.maximum(z - offset, 0)]
        term += above * field[shot, jnp.minimum(z + offset, cells_z - 1)]
        total = term if total is None else total + term
    return total


def ramp_squared(index, length, thickness):
    distance = jnp.minimum(index, length - 1 - index).astype(F32)
    reach = jnp.full(index.shape, thickness, jnp.int32).astype(F32)
    ramp = jnp.maximum((reach - distance) / reach, 0.0)
    return ramp * ramp


def fetch(pairs, sems):
    copies = [
        pltpu.make_async_copy(source, target, sems.at[index])
        for index, (source, target) in enumerate(pairs)
    ]
    for copy in copies:
        copy.start()
    return copies


def begin_kernel(
    total_z,
    blocks,
    pml,
    curr,
    courant_hbm,
    prev_hbm,
    traces_hbm,
    place_z_hbm,
    place_x_hbm,
    place_y_hbm,
    band_y_hbm,
    band_x_hbm,
    updated,
    rest,
    gain_self,
    gain_lap,
    courant,
    prev,
    traces,
    place_z,
    place_x,
    place_y,
    band_y,
    band_x,
    ramp_z,
    ramp_xy,
    inject,
    sems,
):
    cells_z, cells_x, cells_y = courant.shape
    shots = curr.shape[0]
    step = cells_z // blocks
    pairs = [
        (traces_hbm, traces),
        (place_z_hbm, place_z),
        (place_x_hbm, place_x),
        (place_y_hbm, place_y),
        (band_y_hbm, band_y),
        (band_x_hbm, band_x),
    ]
    few = len(pairs)
    for block in range(blocks):
        span = pl.ds(block * step, step)
        pairs.append((courant_hbm.at[span], courant.at[span]))
        pairs.append((prev_hbm.at[:, span], prev.at[:, span]))
    copies = fetch(pairs, sems)
    first_z = lax.axis_index("slab") * cells_z
    plane = (cells_x, cells_y)
    row = lax.broadcasted_iota(jnp.int32, plane, 0)
    column = lax.broadcasted_iota(jnp.int32, plane, 1)
    ramp_z[...] = ramp_squared(
        lax.broadcasted_iota(jnp.int32, ramp_z.shape, 0) + first_z, total_z, pml[0]
    )
    ramp_xy[...] = ramp_squared(row, cells_x, pml[1]) + ramp_squared(column, cells_y, pml[2])
    for copy in copies[:few]:
        copy.wait()
    receivers = traces.shape[2]
    cell = lax.broadcasted_iota(jnp.int32, (cells_y, receivers), 0)
    for shot in range(shots):
        here = cell == place_y[shot : shot + 1, :]
        for instant in range(2):
            high, low = two_parts(jnp.where(here, traces[shot, instant : instant + 1, :], 0.0))
            span = slice(instant * cells_y, (instant + 1) * cells_y)
            inject[shot, span, :receivers] = high
            inject[shot, span, receivers:] = low
    line = lax.broadcasted_iota(jnp.int32, (cells_x, receivers), 0)

    def one_layer(z):
        damping = DAMP_PEAK * (ramp_z[pl.ds(z, 1), :] + ramp_xy[...])
        scale = 1.0 / (1.0 + damping)
        speed = courant[z]
        lap_gain = scale * (speed * speed)
        self_gain = 2.0 * scale + CENTRE * lap_gain
        lap_gain = lap_gain * (1.0 / DIVISOR)
        prev_gain = scale * (1.0 - damping)
        gain_self[z] = self_gain
        gain_lap[z] = lap_gain
        laps = along_xy([curr[shot, z] for shot in range(shots)], band_y, band_x)
        for shot in range(shots):
            now = curr[shot, z]
            lap = laps[shot] + along_z(curr, shot, z, cells_z)
            code = (place_z[shot : shot + 1, :] - first_z - z) * cells_x + place_x[shot : shot + 1, :]
            mark = jnp.where(line == code, 1.0, 0.0).astype(BF16)
            source = dot_rows(jnp.concatenate([mark, mark], axis=1), inject[shot])
            updated[shot, z] = (
                self_gain * now
                - prev_gain * prev[shot, z]
                + lap_gain * lap
                + scale * source[:, :cells_y]
            )
            rest[shot, z] = scale * source[:, cells_y:] - prev_gain * now

    for block in range(blocks):
        for copy in copies[few + 2 * block : few + 2 * block + 2]:
            copy.wait()
        pl.loop(block * step, (block + 1) * step)(one_layer)


def halo_terms(halo, shot, layer, upper):
    total = None
    for offset in range(1, REACH + 1):
        at = layer + offset - REACH if upper else layer - offset + REACH
        if 0 <= at < REACH:
            term = WHOLE_TAPS[offset] * halo[shot, at]
            total = term if total is None else total + term
    return total


def edge_kernel(upper, partial, halo, gain_lap, whole, out):
    @pl.loop(0, partial.shape[0])
    def _(shot):
        for layer in range(REACH):
            value = partial[shot, layer] + gain_lap[layer] * halo_terms(halo, shot, layer, upper)
            whole[shot, layer] = value
            out[shot, layer] = value


def emit(gradients, layer, spread_y, weight_z, pool, chunks, total, lines):
    shots = len(gradients)
    rounded = [gradient.astype(BF16) for gradient in gradients]
    cells_x = rounded[0].shape[0]
    spread = dot(jnp.concatenate(rounded, axis=0), spread_y[...])
    half = cells_x // 2
    pairs = []
    for shot in range(shots):
        total[shot] += spread[shot * cells_x : (shot + 1) * cells_x] * weight_z
        lines[shot] = rounded[shot].astype(F32)
        even = lines[shot, pl.ds(0, half, stride=2), :].astype(BF16)
        odd = lines[shot, pl.ds(1, half, stride=2), :].astype(BF16)
        pairs.append(jnp.concatenate([even, odd], axis=1))
    coarse = dot(jnp.concatenate(pairs, axis=0), pool[...])
    part = chunks.shape[2]
    pieces = half // part
    for shot in range(shots):
        for piece in range(pieces):
            start = shot * half + piece * part
            chunks[layer * pieces + piece, shot] = coarse[start : start + part]


def middle_kernel(
    blocks,
    wave,
    rest,
    gain_self,
    gain_lap,
    snaps_hbm,
    omega_z_hbm,
    omega_x_hbm,
    omega_y_hbm,
    band_y_hbm,
    band_x_hbm,
    pool_hbm,
    panels,
    edges,
    edge_gain,
    sketch,
    snaps,
    omega_z,
    omega_x,
    omega_y,
    band_y,
    band_x,
    pool,
    total,
    spread_y,
    lines,
    chunks,
    sems,
):
    shots, cells_z = wave.shape[:2]
    last = cells_z - REACH
    step = cells_z // blocks
    pairs = [
        (band_y_hbm, band_y),
        (band_x_hbm, band_x),
        (omega_y_hbm, omega_y),
        (omega_z_hbm, omega_z),
        (pool_hbm, pool),
        (omega_x_hbm, omega_x),
    ]
    few = len(pairs)
    order = list(range(1, blocks - 1)) + [0, blocks - 1]
    for block in order:
        span = pl.ds(block * step, step)
        pairs.append((snaps_hbm.at[:, :, span], snaps.at[:, :, span]))
    copies = fetch(pairs, sems)
    total[...] = jnp.zeros_like(total)
    for copy in copies[:few]:
        copy.wait()
    spread_y[...] = omega_y[...].astype(F32).astype(BF16)

    def gradients_at(z):
        laps = along_xy([wave[shot, z] for shot in range(shots)], band_y, band_x)
        gradients = []
        for shot in range(shots):
            lap = laps[shot] + along_z(wave, shot, z, cells_z)
            now = wave[shot, z]
            later = gain_self[z] * now + rest[shot, z] + gain_lap[z] * lap
            gradients.append(
                now * snaps[shot, 0, z].astype(F32) + later * snaps[shot, 1, z].astype(F32)
            )
        return gradients

    def middle_layer(z):
        weight_z = omega_z[pl.ds(z, 1), :].astype(F32)
        emit(gradients_at(z), z - REACH, spread_y, weight_z, pool, chunks, total, lines)

    def edge_layer(index):
        z = index + jnp.where(index >= REACH, last - REACH, 0)
        gradients = gradients_at(z)
        for shot in range(shots):
            edges[shot, index] = gradients[shot]
            edge_gain[shot, index] = gain_lap[z] * snaps[shot, 1, z].astype(F32)

    for place, block in enumerate(order[:-2]):
        copies[few + place].wait()
        pl.loop(block * step, (block + 1) * step)(middle_layer)
    send = pltpu.make_async_copy(
        chunks, panels.at[:, :, pl.ds(0, chunks.shape[2])], sems.at[len(pairs)]
    )
    send.start()
    for copy in copies[few + blocks - 2 :]:
        copy.wait()
    pl.loop(0, 2 * REACH)(edge_layer)
    weights_x = omega_x[...].astype(F32)
    for shot in range(shots):
        sketch[shot : shot + 1, :] = jnp.sum(total[shot] * weights_x, axis=0, keepdims=True)
    send.wait()


def finish_kernel(
    panels_before,
    edges,
    edge_gain,
    halo_low,
    halo_high,
    omega_z,
    omega_x,
    omega_y,
    pool,
    before,
    panels,
    sketch,
    total,
    spread_y,
    lines,
    chunks,
    sem,
):
    shots = edges.shape[0]
    cells_z = omega_z.shape[0]
    spread_y[...] = omega_y[...].astype(F32).astype(BF16)
    total[...] = jnp.zeros_like(total)
    for halo, upper in ((halo_low, False), (halo_high, True)):
        for layer in range(REACH):
            index = layer + (REACH if upper else 0)
            z = cells_z - REACH + layer if upper else layer
            gradients = [
                edges[shot, index]
                + edge_gain[shot, index] * halo_terms(halo, shot, layer, upper)
                for shot in range(shots)
            ]
            weight_z = omega_z[z : z + 1, :].astype(F32)
            emit(gradients, index, spread_y, weight_z, pool, chunks, total, lines)
    part = chunks.shape[2]
    send = pltpu.make_async_copy(chunks, panels.at[:, :, pl.ds(part, part)], sem.at[0])
    send.start()
    weights_x = omega_x[...].astype(F32)
    for shot in range(shots):
        sketch[shot : shot + 1, :] = before[shot : shot + 1, :] + jnp.sum(
            total[shot] * weights_x, axis=0, keepdims=True
        )
    send.wait()


def gram_kernel(panels, out):
    shots = out.shape[0]
    part = panels.shape[0] // shots
    width = 8
    gram = None
    for start in range(0, part, width):
        rows = [panels[pl.ds(start + index, shots, stride=part), :] for index in range(width)]
        high, low = two_parts(jnp.concatenate(rows, axis=1))
        both = jnp.concatenate([high, low], axis=0)
        term = dot_rows(both, both)
        gram = term if gram is None else gram + term
    folded = (gram[:shots, :shots] + gram[shots:, shots:]) + (
        gram[:shots, shots:] + gram[shots:, :shots]
    )
    out[...] = jnp.zeros_like(out)
    out[:, :shots] = folded


def spec(block=None, index=None):
    if block is None:
        return pl.BlockSpec(memory_space=pltpu.VMEM)
    return pl.BlockSpec(block, lambda step: index)


def run(kernel, out_shape, in_specs, out_specs, scratch=(), flops=0, moved=0, grid=None, **options):
    if grid is not None:
        options["grid"] = grid
    return pl.pallas_call(
        kernel,
        out_shape=out_shape,
        in_specs=in_specs,
        out_specs=out_specs,
        scratch_shapes=scratch,
        compiler_params=pltpu.CompilerParams(vmem_limit_bytes=VMEM_BYTES),
        cost_estimate=pl.CostEstimate(flops=flops, bytes_accessed=moved, transcendentals=0),
        **options,
    )


def local(
    courant,
    adj_prev,
    adj_curr,
    forward_snaps,
    traces,
    receiver_z,
    receiver_x,
    receiver_y,
    pml_cells,
    omega_z,
    omega_x,
    omega_y,
):
    shots, cells_z, cells_x, cells_y = adj_curr.shape
    slabs = lax.axis_size("slab")
    groups = lax.axis_size("shot")
    total_z = cells_z * slabs
    last = cells_z - REACH
    inner = last - REACH
    rank = omega_z.shape[1]
    receivers = traces.shape[2]
    half_x = cells_x // 2
    part = inner * half_x // groups
    blocks = cells_z // REACH
    shape = jax.ShapeDtypeStruct
    plane = (cells_x, cells_y)
    band = band_matrix(cells_y)
    band_y = jnp.asarray(np.concatenate([band, band], axis=0))
    band = band_matrix(cells_x)
    band_x = jnp.asarray(np.concatenate([band, band], axis=1))
    pool = jnp.asarray(pool_matrix(cells_y))

    def from_below(layers):
        return lax.ppermute(layers, "slab", [(i, i + 1) for i in range(slabs - 1)])

    def from_above(layers):
        return lax.ppermute(layers, "slab", [(i + 1, i) for i in range(slabs - 1)])

    halo_low = from_below(adj_curr[:, last:])
    halo_high = from_above(adj_curr[:, :REACH])

    vmem = spec()
    hbm = pl.BlockSpec(memory_space=pltpu.HBM)

    def pinned(*arrays):
        return [pltpu.with_memory_space_constraint(array, pltpu.HBM) for array in arrays]

    field = shape((shots, cells_z) + plane, F32)
    gain = shape((cells_z,) + plane, F32)
    edge = shape((shots, REACH) + plane, F32)
    like = lambda array: pltpu.VMEM(array.shape, array.dtype)
    updated, rest, gain_self, gain_lap = run(
        functools.partial(begin_kernel, total_z, blocks),
        [field, field, gain, gain],
        in_specs=[pl.BlockSpec(memory_space=pltpu.SMEM), vmem] + [hbm] * 8,
        out_specs=[vmem] * 4,
        scratch=[
            like(courant),
            like(adj_prev),
            like(traces),
            like(receiver_z),
            like(receiver_x),
            like(receiver_y),
            like(band_y),
            like(band_x),
            pltpu.VMEM((cells_z, cells_y), F32),
            pltpu.VMEM(plane, F32),
            pltpu.VMEM((shots, 2 * cells_y, 2 * receivers), BF16),
            pltpu.SemaphoreType.DMA((6 + 2 * blocks,)),
        ],
        flops=2 * 10**9,
        moved=11 * 2**20,
    )(
        pml_cells,
        adj_curr,
        *pinned(
            courant, adj_prev, traces, receiver_z, receiver_x, receiver_y, band_y, band_x
        ),
    )

    layers4 = (shots, REACH) + plane
    gains4 = (REACH,) + plane

    def complete(whole, halo, upper):
        side = blocks - 1 if upper else 0
        return run(
            functools.partial(edge_kernel, upper),
            [field, edge],
            in_specs=[
                spec(layers4, (0, side, 0, 0)),
                spec(layers4, (0, 0, 0, 0)),
                spec(gains4, (side, 0, 0)),
            ],
            out_specs=[spec(layers4, (0, side, 0, 0)), spec(layers4, (0, 0, 0, 0))],
            grid=(1,),
            flops=10**7,
            moved=2 * 2**20,
            input_output_aliases={0: 0},
        )(whole, halo, gain_lap)

    wave, edge_low = complete(updated, halo_low, False)
    wave, edge_high = complete(wave, halo_high, True)
    next_high = from_above(edge_low)
    next_low = from_below(edge_high)

    panel = shape((groups, shots, 2 * part, cells_y), F32)
    scratch_emit = [
        pltpu.VMEM((shots, cells_x, rank), F32),
        pltpu.VMEM((cells_y, rank), BF16),
        pltpu.VMEM((shots,) + plane, F32),
        pltpu.VMEM((groups, shots, part, cells_y), F32),
    ]
    both = shape((shots, 2 * REACH) + plane, F32)
    panels, edges, edge_gain, sketch_mid = run(
        functools.partial(middle_kernel, blocks),
        [panel, both, both, shape((shots, rank), F32)],
        in_specs=[vmem] * 4 + [hbm] * 7,
        out_specs=[hbm, vmem, vmem, vmem],
        scratch=[
            like(forward_snaps),
            like(omega_z),
            like(omega_x),
            like(omega_y),
            like(band_y),
            like(band_x),
            like(pool),
        ]
        + scratch_emit
        + [pltpu.SemaphoreType.DMA((7 + blocks,))],
        flops=2 * 10**9,
        moved=11 * 2**20,
    )(
        wave,
        rest,
        gain_self,
        gain_lap,
        *pinned(forward_snaps, omega_z, omega_x, omega_y, band_y, band_x, pool),
    )

    panels, sketch_part = run(
        finish_kernel,
        [panel, shape((shots, rank), F32)],
        in_specs=[hbm] + [vmem] * 9,
        out_specs=[hbm, vmem],
        scratch=scratch_emit + [pltpu.SemaphoreType.DMA((1,))],
        flops=5 * 10**8,
        moved=5 * 2**20,
        input_output_aliases={0: 0},
    )(
        panels,
        edges,
        edge_gain,
        next_low,
        next_high,
        omega_z,
        omega_x,
        omega_y,
        pool,
        sketch_mid,
    )
    got = lax.all_to_all(panels, "shot", 0, 0, tiled=True)

    folded = panels.reshape(inner, half_x // part, shots, 2, part, cells_y)
    folded = folded.transpose(3, 2, 0, 1, 4, 5).reshape(2, shots, inner, half_x, cells_y)
    coarse = jnp.concatenate(
        [folded[1, :, :REACH], folded[0], folded[1, :, REACH:]], axis=1
    ).reshape(shots, cells_z, half_x * cells_y)

    all_shots = groups * shots
    gram = run(
        gram_kernel,
        shape((all_shots, cells_y), F32),
        in_specs=[vmem],
        out_specs=vmem,
        flops=10**8,
        moved=2**20,
    )(got.reshape(all_shots * 2 * part, cells_y))
    mine = lax.all_to_all(gram.reshape(groups, shots, cells_y), "shot", 0, 0, tiled=True).sum(0)
    terms = jnp.concatenate([sketch_part, mine], axis=0)
    sums = lax.all_to_all(
        jnp.broadcast_to(terms[None], (slabs,) + terms.shape), "slab", 0, 0, tiled=True
    ).sum(0)
    sketch = sums[:shots] * (1.0 / math.sqrt(total_z * cells_x * cells_y))
    group = lax.axis_index("shot")
    partner = jnp.remainder(group - 1 - jnp.arange(LAGS, dtype=jnp.int32), groups)
    wanted = (partner[:, None] * shots + jnp.arange(shots, dtype=jnp.int32)[None, :]).reshape(-1)
    picked = wanted[:, None] == jnp.arange(cells_y, dtype=jnp.int32)[None, :]
    band = jnp.sum(jnp.where(picked[None], sums[shots:, None, :], 0.0), axis=-1)
    gram_band = band.reshape(shots, LAGS, shots) * (
        1.0 / math.sqrt(total_z * cells_x * cells_y // 2)
    )
    return (sketch, coarse, gram_band)


def solution(mesh):
    return jax.shard_map(
        local,
        mesh=mesh,
        in_specs=(
            P("slab", None, None),
            P("shot", "slab", None, None),
            P("shot", "slab", None, None),
            P("shot", None, "slab", None, None),
            P("shot", None, None),
            P("shot", None),
            P("shot", None),
            P("shot", None),
            P(),
            P("slab", None),
            P(),
            P(),
        ),
        out_specs=(P("shot", None), P("shot", "slab", None), P("shot", None, None)),
        check_vma=False,
    )
```

time: 120 us -> 99.5 us (0.83)
  local copies, waits for them, and re-layouts: 17.5 us -> 4.62 us
  starting transfers between devices: 43.5 us -> 34.5 us
  waiting for transfers between devices: 33.8 us -> 40.7 us
  Pallas kernels: 21 us -> 16.3 us
    all_to_all x2 -> x1, waiting for transfers between devices: 11.1 us -> 24.2 us  [local(): got = lax.all_to_all(panels, 'shot', 0, 0, tiled=True)]
    unnamed x49 -> x13, local copies, waits for them, and re-layouts: 13.7 us -> 0.71 us
    all_to_all x2 -> x1, starting transfers between devices: 16.2 us -> 9.31 us  [local(): got = lax.all_to_all(panels, 'shot', 0, 0, tiled=True)]
    pallas_call x6, Pallas kernels: 21 us -> 16.3 us  [the longest x1 6.51 us: local(): run(functools.partial(begin_kernel, total_z, blocks), [field, field, gain...]
    ppermute x2, waiting for transfers between devices: 4.49 us -> 0.01 us  [from_below(): return lax.ppermute(layers, 'slab', [(i, i + 1) for i in range(slabs - 1)])]
    ppermute x2, starting transfers between devices: 7.07 us -> 4.4 us  [from_above(): return lax.ppermute(layers, 'slab', [(i + 1, i) for i in range(slabs - 1)])]
    ppermute x2, starting transfers between devices: 4.6 us -> 6.43 us  [from_below(): return lax.ppermute(layers, 'slab', [(i, i + 1) for i in range(slabs - 1)])]
    transpose x1 -> x0, local copies, waits for them, and re-layouts: 1.35 us -> none  [layers_of(): folded.transpose(2, 0, 1, 3, 4).reshape(shots, count, half_x, cells_y)]
  transfers between devices with their start and end apart: 8 -> 7, of which waited for: 5 -> 5; matrix products, arithmetic and copies ran while one was open for 3% -> 3% of each run, Pallas kernels for 7% -> 13%
where the time goes in v2:
time: 99.5 us; the launch traced here: 99 us
  waiting for transfers between devices  40.7 us (41%)
  starting transfers between devices  34.5 us (35%)
  Pallas kernels  16.3 us (16%)
  local copies, waits for them, and re-layouts  4.62 us (5%)
  other arithmetic  2.03 us (2%)
    all_to_all x1, waiting for transfers between devices, local(): got = lax.all_to_all(panels, 'shot', 0, 0, tiled=True)  24.2 us
    all_to_all x1, starting transfers between devices, local(): lax.all_to_all(jnp.broadcast_to(terms[None], (slabs,) + terms.shape), 'sl...  9.94 us
    all_to_all x1, starting transfers between devices, local(): got = lax.all_to_all(panels, 'shot', 0, 0, tiled=True)  9.31 us
    all_to_all x1, waiting for transfers between devices, local(): lax.all_to_all(gram.reshape(groups, shots, cells_y), 'shot', 0, 0, tiled=...  6.91 us
    pallas_call x1, Pallas kernels, local(): run(functools.partial(begin_kernel, total_z, blocks), [field, field, gain...  6.51 us
    ppermute x2, starting transfers between devices, from_below(): return lax.ppermute(layers, 'slab', [(i, i + 1) for i in range(slabs - 1)])  6.43 us
    pallas_call x1, Pallas kernels, local(): run(functools.partial(middle_kernel, blocks), [panel, both, both, shape((...  6.33 us
    all_to_all x1, waiting for transfers between devices, local(): lax.all_to_all(jnp.broadcast_to(terms[None], (slabs,) + terms.shape), 'sl...  6.16 us
  transfers between devices with their start and end apart: 7, of which 5 were waited for; matrix products, arithmetic and copies ran while one was open for 3% of the time, Pallas kernels for 13%

profile of v2, /device:TPU:1, one launch (start us, length us, event | category | flops | bytes accessed | tf_op | source)
XLA Modules:
  0.0 99.0 jit_solution(8680785378364847565)
XLA Ops:
  0.7 1.4 %fusion.2 = (f32[2,4,128,128]{3,2,1,0:T(8,128)S(1)}, f32[2,4,128,128]{3,2,1,0:T(8,128)S(1)}) fusion(f32[2,16,128,128]{3,2,1,0:T(8,128)} %curr.1), kind=kLoop, calls=%fused_computation.13 | loop fusion | bytes 2097152 | tf_op jit(solution)/shard_map/slice | solution.py:453
  2.1 4.5 %collective-permute-start = (f32[2,4,128,128]{3,2,1,0:T(8,128)S(1)}, f32[2,4,128,128]{3,2,1,0:T(8,128)S(1)}, u32[]{:S(2)}, u32[]{:S(2)}) collective-permute-start(f32[2,4,128,128]{3,2,1,0:T(8,128)S(1)} %get-tuple-element.44), channel_id=1, source_target_pairs={{0,1},{1,2},{2,3},{3,4},{4,5},{5,6},{6,7},{7,8},{8,9},{9,10},{10,1... | collective-permute-start | bytes 1572872 | tf_op jit(solution)/shard_map/ppermute | solution.py:447
  6.6 2.0 %collective-permute-start.1 = (f32[2,4,128,128]{3,2,1,0:T(8,128)S(1)}, f32[2,4,128,128]{3,2,1,0:T(8,128)S(1)}, u32[]{:S(2)}, u32[]{:S(2)}) collective-permute-start(f32[2,4,128,128]{3,2,1,0:T(8,128)S(1)} %get-tuple-element.43), channel_id=1, source_target_pairs={{1,0},{2,1},{3,2},{4,3},{5,4},{6,5},{7,6},{8,7},{9,8},{10,9},{11,1... | collective-permute-start | bytes 1572872 | tf_op jit(solution)/shard_map/ppermute | solution.py:450
  8.6 6.5 %shard_map.166 = (f32[2,16,128,128]{3,2,1,0:T(8,128)S(1)}, f32[2,16,128,128]{3,2,1,0:T(8,128)S(1)}, f32[16,128,128]{2,1,0:T(8,128)S(1)}, f32[16,128,128]{2,1,0:T(8,128)S(1)}) custom-call(s32[3]{0:T(128)S(1)} %copy-done.5, f32[2,16,128,128]{3,2,1,0:T(8,128)S(1)} %copy-done, f32[16,128,128]{2,1,0:T(8,128)} %courant_hbm.1, f32[2,16,128,128]{3,2,1,0:T(8,128)} %prev_hbm.1, ...), custom_call_target="tpu_custom_call" | custom-call | flops 2000000000 | bytes 11534336 | tf_op jit(solution)/shard_map/pallas_call | solution.py:465
  15.1 0.2 shard_map.167
  15.3 1.8 %collective-permute-done.1.halo = f32[2,4,128,128]{3,2,1,0:T(8,128)S(1)} collective-permute-done((f32[2,4,128,128]{3,2,1,0:T(8,128)S(1)}, f32[2,4,128,128]{3,2,1,0:T(8,128)S(1)}, u32[]{:S(2)}, u32[]{:S(2)}) %collective-permute-start.1) | collective-permute-done | bytes 524320 | tf_op jit(solution)/shard_map/ppermute | solution.py:450
  17.1 0.2 shard_map.168
  17.3 1.9 %collective-permute-start.2 = (f32[2,4,128,128]{3,2,1,0:T(8,128)S(1)}, f32[2,4,128,128]{3,2,1,0:T(8,128)S(1)}, u32[]{:S(2)}, u32[]{:S(2)}) collective-permute-start(f32[2,4,128,128]{3,2,1,0:T(8,128)S(1)} %get-tuple-element.26), channel_id=1, source_target_pairs={{0,1},{1,2},{2,3},{3,4},{4,5},{5,6},{6,7},{7,8},{8,9},{9,10},{10,1... | collective-permute-start | bytes 1572872 | tf_op jit(solution)/shard_map/ppermute | solution.py:447
  19.2 2.4 %collective-permute-start.3 = (f32[2,4,128,128]{3,2,1,0:T(8,128)S(1)}, f32[2,4,128,128]{3,2,1,0:T(8,128)S(1)}, u32[]{:S(2)}, u32[]{:S(2)}) collective-permute-start(f32[2,4,128,128]{3,2,1,0:T(8,128)S(1)} %get-tuple-element.27), channel_id=1, source_target_pairs={{1,0},{2,1},{3,2},{4,3},{5,4},{6,5},{7,6},{8,7},{9,8},{10,9},{11,1... | collective-permute-start | bytes 1572872 | tf_op jit(solution)/shard_map/ppermute | solution.py:450
  21.7 6.3 %shard_map.169 = (f32[16,2,64,128]{3,2,1,0:T(8,128)}, f32[2,8,128,128]{3,2,1,0:T(8,128)S(1)}, f32[2,8,128,128]{3,2,1,0:T(8,128)S(1)}, f32[2,128]{1,0:T(2,128)S(1)}) custom-call(f32[2,16,128,128]{3,2,1,0:T(8,128)S(1)} %get-tuple-element.20.wave, f32[2,16,128,128]{3,2,1,0:T(8,128)S(1)} %get-tuple-element.21.rest, ...), custom_call_target="tpu_custom_call" | custom-call | flops 2000000000 | bytes 11534336 | tf_op jit(solution)/shard_map/pallas_call | solution.py:527
  28.1 1.7 %collective-permute-done.3.halo_high = f32[2,4,128,128]{3,2,1,0:T(8,128)S(1)} collective-permute-done((f32[2,4,128,128]{3,2,1,0:T(8,128)S(1)}, f32[2,4,128,128]{3,2,1,0:T(8,128)S(1)}, u32[]{:S(2)}, u32[]{:S(2)}) %collective-permute-start.3) | collective-permute-done | bytes 524320 | tf_op jit(solution)/shard_map/ppermute | solution.py:450
  29.8 1.5 %shard_map.170 = (f32[16,2,64,128]{3,2,1,0:T(8,128)}, f32[2,128]{1,0:T(2,128)S(1)}) custom-call(f32[16,2,64,128]{3,2,1,0:T(8,128)} %get-tuple-element.23.panels_before, f32[2,8,128,128]{3,2,1,0:T(8,128)S(1)} %get-tuple-element.24.edges, f32[2,8,128,128]{3,2,1,0:T(8,128)S(1)} %get-tuple-element.25.edge_gain, ...), custom_call_target="tpu_custom_call", output_to_operand_aliasing={{0}: (0, {})} | custom-call | flops 500000000 | bytes 5242880 | tf_op jit(solution)/shard_map/pallas_call | solution.py:553
  31.2 9.3 %all-to-all-start = ((f32[16,2,64,128]{3,2,1,0:T(8,128)}), f32[16,2,64,128]{3,2,1,0:T(8,128)S(1)}, u32[]{:S(2)}, u32[]{:S(2)}) async-start(f32[16,2,64,128]{3,2,1,0:T(8,128)} %get-tuple-element.30), calls=%async_computation | async-start | bytes 2097152 | tf_op jit(solution)/shard_map/all_to_all | solution.py:574
  40.6 0.1 iota_add_fusion
  40.7 0.1 add.35
  40.7 0.1 iota_compare_fusion
  40.8 1.3 %copy.35 = f32[8,2,2,2,32,128]{5,4,1,0,2,3:T(8,128)S(1)} copy(f32[8,2,2,2,32,128]{5,4,3,2,1,0:T(8,128)} %bitcast.2) | data formatting | bytes 2097152 | tf_op jit(solution)/shard_map/reshape | solution.py:576
  42.1 24.2 %all-to-all-done = f32[16,2,64,128]{3,2,1,0:T(8,128)S(1)} async-done(((f32[16,2,64,128]{3,2,1,0:T(8,128)}), f32[16,2,64,128]{3,2,1,0:T(8,128)S(1)}, u32[]{:S(2)}, u32[]{:S(2)}) %all-to-all-start) | async-done | bytes 1048608 | tf_op jit(solution)/shard_map/all_to_all | solution.py:574
  66.3 1.6 %shard_map.171 = f32[32,128]{1,0:T(8,128)} custom-call(f32[2048,128]{1,0:T(8,128)S(1)} %bitcast.14), custom_call_target="tpu_custom_call" | custom-call | flops 100000000 | bytes 1048576 | tf_op jit(solution)/shard_map/pallas_call | solution.py:583
  67.9 4.4 %all-to-all-start.1 = ((f32[16,2,128]{2,1,0:T(2,128)}), f32[16,2,128]{2,1,0:T(2,128)S(1)}, u32[]{:S(2)}, u32[]{:S(2)}) async-start(f32[16,2,128]{2,1,0:T(2,128)} %bitcast.1), calls=%async_computation.1 | async-start | bytes 32768 | tf_op jit(solution)/shard_map/all_to_all | solution.py:591
  72.4 0.1 concatenate.15
  72.5 0.1 concatenate.14
  72.6 0.1 concatenate.16
  72.7 6.9 %all-to-all-done.1 = f32[16,2,128]{2,1,0:T(2,128)S(1)} async-done(((f32[16,2,128]{2,1,0:T(2,128)}), f32[16,2,128]{2,1,0:T(2,128)S(1)}, u32[]{:S(2)}, u32[]{:S(2)}) %all-to-all-start.1) | async-done | bytes 16416 | tf_op jit(solution)/shard_map/all_to_all | solution.py:591
  79.7 0.6 broadcast_in_dim.15
  80.3 9.9 %all-to-all-start.2 = ((f32[16,4,128]{2,1,0:T(4,128)}), f32[16,4,128]{2,1,0:T(4,128)S(1)}, u32[]{:S(2)}, u32[]{:S(2)}) async-start(f32[16,4,128]{2,1,0:T(4,128)} %broadcast_in_dim.15), calls=%async_computation.2 | async-start | bytes 65536 | tf_op jit(solution)/shard_map/all_to_all | solution.py:593
  90.2 1.1 %pad_maximum_fusion = f32[2,16,8192]{2,1,0:T(8,128)} fusion(f32[2,4,8192]{2,1,0:T(4,128)S(1)} %concatenate.16, f32[2,8,8192]{2,1,0:T(8,128)S(1)} %concatenate.15, f32[2,4,8192]{2,1,0:T(4,128)S(1)} %concatenate.14), kind=kLoop, calls=%fused_computation | loop fusion | flops 524288 | bytes 2097152 | tf_op jit(solution)/shard_map/concatenate | solution.py:578
  91.4 6.2 %all-to-all-done.2 = f32[16,4,128]{2,1,0:T(4,128)S(1)} async-done(((f32[16,4,128]{2,1,0:T(4,128)}), f32[16,4,128]{2,1,0:T(4,128)S(1)}, u32[]{:S(2)}, u32[]{:S(2)}) %all-to-all-start.2) | async-done | bytes 32800 | tf_op jit(solution)/shard_map/all_to_all | solution.py:593
  97.6 0.6 fusion.4
  98.1 0.1 select_reduce_fusion
  98.2 0.1 mul.24
  98.3 0.7 copy.29
  (21 shorter events, 0.2 us)
Async XLA Ops:
  0.6 8.0 %copy-start = (f32[2,16,128,128]{3,2,1,0:T(8,128)S(1)}, f32[2,16,128,128]{3,2,1,0:T(8,128)}, u32[]{:S(2)}) copy-start(f32[2,16,128,128]{3,2,1,0:T(8,128)} %curr.1) | copy-start | bytes 6291460
  0.6 8.0 %copy-start.5 = (s32[3]{0:T(128)S(1)}, s32[3]{0:T(128)}, u32[]{:S(2)}) copy-start(s32[3]{0:T(128)} %pml.1) | copy-start | bytes 40
  2.1 13.0 %collective-permute-start = (f32[2,4,128,128]{3,2,1,0:T(8,128)S(1)}, f32[2,4,128,128]{3,2,1,0:T(8,128)S(1)}, u32[]{:S(2)}, u32[]{:S(2)}) collective-permute-start(f32[2,4,128,128]{3,2,1,0:T(8,128)S(1)} %get-tuple-element.44), channel_id=1, source_target_pairs={{0,1},{1,2},{2,3},{3,4},{4,5},{5,6},{6,7},{7,8},{8,9},{9,10},{10,1... | collective-permute-start | bytes 1572872 | tf_op jit(solution)/shard_map/ppermute | solution.py:447
  6.6 10.5 %collective-permute-start.1 = (f32[2,4,128,128]{3,2,1,0:T(8,128)S(1)}, f32[2,4,128,128]{3,2,1,0:T(8,128)S(1)}, u32[]{:S(2)}, u32[]{:S(2)}) collective-permute-start(f32[2,4,128,128]{3,2,1,0:T(8,128)S(1)} %get-tuple-element.43), channel_id=1, source_target_pairs={{1,0},{2,1},{3,2},{4,3},{5,4},{6,5},{7,6},{8,7},{9,8},{10,9},{11,1... | collective-permute-start | bytes 1572872 | tf_op jit(solution)/shard_map/ppermute | solution.py:450
  17.3 10.8 %collective-permute-start.2 = (f32[2,4,128,128]{3,2,1,0:T(8,128)S(1)}, f32[2,4,128,128]{3,2,1,0:T(8,128)S(1)}, u32[]{:S(2)}, u32[]{:S(2)}) collective-permute-start(f32[2,4,128,128]{3,2,1,0:T(8,128)S(1)} %get-tuple-element.26), channel_id=1, source_target_pairs={{0,1},{1,2},{2,3},{3,4},{4,5},{5,6},{6,7},{7,8},{8,9},{9,10},{10,1... | collective-permute-start | bytes 1572872 | tf_op jit(solution)/shard_map/ppermute | solution.py:447
  19.2 10.5 %collective-permute-start.3 = (f32[2,4,128,128]{3,2,1,0:T(8,128)S(1)}, f32[2,4,128,128]{3,2,1,0:T(8,128)S(1)}, u32[]{:S(2)}, u32[]{:S(2)}) collective-permute-start(f32[2,4,128,128]{3,2,1,0:T(8,128)S(1)} %get-tuple-element.27), channel_id=1, source_target_pairs={{1,0},{2,1},{3,2},{4,3},{5,4},{6,5},{7,6},{8,7},{9,8},{10,9},{11,1... | collective-permute-start | bytes 1572872 | tf_op jit(solution)/shard_map/ppermute | solution.py:450
  21.7 8.1 %copy-start.1 = (s32[128,128]{1,0:T(8,128)S(1)}, s32[128,128]{1,0:T(8,128)}, u32[]{:S(2)}) copy-start(s32[128,128]{1,0:T(8,128)} %omega_x.1) | copy-start | bytes 196612
  21.7 8.1 %copy-start.2 = (s32[128,128]{1,0:T(8,128)S(1)}, s32[128,128]{1,0:T(8,128)}, u32[]{:S(2)}) copy-start(s32[128,128]{1,0:T(8,128)} %omega_y.1) | copy-start | bytes 196612
  21.7 8.0 %copy-start.3 = (bf16[256,128]{1,0:T(8,128)(2,1)S(1)}, bf16[256,128]{1,0:T(8,128)(2,1)}, u32[]{:S(2)}) copy-start(bf16[256,128]{1,0:T(8,128)(2,1)} %constant.39.clone.pool_hbm.pool) | copy-start | bytes 196612
  21.7 8.0 %copy-start.4 = (s32[16,128]{1,0:T(8,128)S(1)}, s32[16,128]{1,0:T(8,128)}, u32[]{:S(2)}) copy-start(s32[16,128]{1,0:T(8,128)} %omega_z.1) | copy-start | bytes 24580
  31.2 35.1 %all-to-all-start = ((f32[16,2,64,128]{3,2,1,0:T(8,128)}), f32[16,2,64,128]{3,2,1,0:T(8,128)S(1)}, u32[]{:S(2)}, u32[]{:S(2)}) async-start(f32[16,2,64,128]{3,2,1,0:T(8,128)} %get-tuple-element.30), calls=%async_computation | async-start | bytes 2097152 | tf_op jit(solution)/shard_map/all_to_all | solution.py:574
  67.9 11.8 %all-to-all-start.1 = ((f32[16,2,128]{2,1,0:T(2,128)}), f32[16,2,128]{2,1,0:T(2,128)S(1)}, u32[]{:S(2)}, u32[]{:S(2)}) async-start(f32[16,2,128]{2,1,0:T(2,128)} %bitcast.1), calls=%async_computation.1 | async-start | bytes 32768 | tf_op jit(solution)/shard_map/all_to_all | solution.py:591
  80.3 17.2 %all-to-all-start.2 = ((f32[16,4,128]{2,1,0:T(4,128)}), f32[16,4,128]{2,1,0:T(4,128)S(1)}, u32[]{:S(2)}, u32[]{:S(2)}) async-start(f32[16,4,128]{2,1,0:T(4,128)} %broadcast_in_dim.15), calls=%async_computation.2 | async-start | bytes 65536 | tf_op jit(solution)/shard_map/all_to_all | solution.py:593

commit v3 on v2

--- a/solution.py
+++ b/solution.py
@@ -194,23 +194,53 @@
         pl.loop(block * step, (block + 1) * step)(one_layer)
 
 
-def halo_terms(halo, shot, layer, upper):
+def odd_slab():
+    return lax.rem(lax.axis_index("slab"), 2)
+
+
+def slice_kernel(curr, near, far, sems):
+    layers = near.shape[1]
+    last = curr.shape[1] - layers
+    odd = odd_slab()
+    copies = fetch(
+        [
+            (curr.at[:, pl.ds((1 - odd) * last, layers)], near),
+            (curr.at[:, pl.ds(odd * last, layers)], far),
+        ],
+        sems,
+    )
+    for copy in copies:
+        copy.wait()
+
+
+def halo_terms(halo, layer, upper):
     total = None
     for offset in range(1, REACH + 1):
         at = layer + offset - REACH if upper else layer - offset + REACH
         if 0 <= at < REACH:
-            term = WHOLE_TAPS[offset] * halo[shot, at]
+            term = WHOLE_TAPS[offset] * halo(at)
             total = term if total is None else total + term
     return total
 
 
-def edge_kernel(upper, partial, halo, gain_lap, whole, out):
-    @pl.loop(0, partial.shape[0])
-    def _(shot):
-        for layer in range(REACH):
-            value = partial[shot, layer] + gain_lap[layer] * halo_terms(halo, shot, layer, upper)
-            whole[shot, layer] = value
-            out[shot, layer] = value
+def edge_kernel(partial, near, far, gain_lap, whole, near_out, far_out):
+    odd = odd_slab()
+    step = pl.program_id(0)
+    for upper in (False, True):
+        for halo, out, parity in (
+            (near, near_out, 0 if upper else 1),
+            (far, far_out, 1 if upper else 0),
+        ):
+
+            @pl.when((step == int(upper)) & (odd == parity))
+            def _():
+                @pl.loop(0, partial.shape[0])
+                def _(shot):
+                    for layer in range(REACH):
+                        terms = halo_terms(lambda at: halo[shot, at], layer, upper)
+                        value = partial[shot, layer] + gain_lap[layer] * terms
+                        whole[shot, layer] = value
+                        out[shot, layer] = value
 
 
 def emit(gradients, layer, spread_y, weight_z, pool, chunks, total, lines):
@@ -330,8 +360,8 @@
     panels_before,
     edges,
     edge_gain,
-    halo_low,
-    halo_high,
+    near,
+    far,
     omega_z,
     omega_x,
     omega_y,
@@ -349,13 +379,19 @@
     cells_z = omega_z.shape[0]
     spread_y[...] = omega_y[...].astype(F32).astype(BF16)
     total[...] = jnp.zeros_like(total)
-    for halo, upper in ((halo_low, False), (halo_high, True)):
+    is_odd = odd_slab() == 1
+
+    def halo(shot, upper):
+        first, second = (far, near) if upper else (near, far)
+        return lambda at: jnp.where(is_odd, first[shot, at], second[shot, at])
+
+    for upper in (False, True):
         for layer in range(REACH):
             index = layer + (REACH if upper else 0)
             z = cells_z - REACH + layer if upper else layer
             gradients = [
                 edges[shot, index]
-                + edge_gain[shot, index] * halo_terms(halo, shot, layer, upper)
+                + edge_gain[shot, index] * halo_terms(halo(shot, upper), layer, upper)
                 for shot in range(shots)
             ]
             weight_z = omega_z[z : z + 1, :].astype(F32)
@@ -371,7 +407,8 @@
     send.wait()
 
 
-def gram_kernel(panels, out):
+def gram_kernel(panels, coarse, out):
+    del coarse
     shots = out.shape[0]
     part = panels.shape[0] // shots
     width = 8
@@ -387,6 +424,41 @@
     )
     out[...] = jnp.zeros_like(out)
     out[:, :shots] = folded
+
+
+def gather_kernel(mine, sketch, out):
+    shots = sketch.shape[0]
+    total = mine[0]
+    for source in range(1, mine.shape[0]):
+        total = total + mine[source]
+    for target in range(out.shape[0]):
+        out[target, :shots] = sketch[...]
+        out[target, shots:] = total
+
+
+def output_kernel(
+    groups, sketch_scale, gram_scale, terms, sketch_hbm, gram_hbm, sketch, gram_band, sems
+):
+    shots, _, lags = gram_band.shape
+    lanes = terms.shape[2]
+    total = terms[0]
+    for source in range(1, terms.shape[0]):
+        total = total + terms[source]
+    sketch[...] = total[:shots] * sketch_scale
+    group = lax.axis_index("shot")
+    lag = lax.broadcasted_iota(jnp.int32, (lags, lanes), 0)
+    lane = lax.broadcasted_iota(jnp.int32, (lags, lanes), 1)
+    partner = group - 1 - lag
+    partner = jnp.where(partner < 0, partner + groups, partner)
+    for shot in range(shots):
+        row = total[shots + shot : shots + shot + 1] * gram_scale
+        for other in range(shots):
+            wanted = lane == partner * shots + other
+            picked = jnp.sum(jnp.where(wanted, row, 0.0), axis=1, keepdims=True)
+            turned = jnp.sum(jnp.where(lane == lag, picked, 0.0), axis=0, keepdims=True)
+            gram_band[shot, other : other + 1, :] = turned[:, :lags]
+    for copy in fetch([(sketch, sketch_hbm), (gram_band, gram_hbm)], sems):
+        copy.wait()
 
 
 def spec(block=None, index=None):
@@ -443,14 +515,12 @@
     band_x = jnp.asarray(np.concatenate([band, band], axis=1))
     pool = jnp.asarray(pool_matrix(cells_y))
 
-    def from_below(layers):
-        return lax.ppermute(layers, "slab", [(i, i + 1) for i in range(slabs - 1)])
-
-    def from_above(layers):
-        return lax.ppermute(layers, "slab", [(i + 1, i) for i in range(slabs - 1)])
-
-    halo_low = from_below(adj_curr[:, last:])
-    halo_high = from_above(adj_curr[:, :REACH])
+    def with_near(layers):
+        return lax.ppermute(layers, "slab", [(i, i ^ 1) for i in range(slabs)])
+
+    def with_far(layers):
+        pairs = [(i, i + 1) for i in range(1, slabs - 1, 2)]
+        return lax.ppermute(layers, "slab", pairs + [(j, i) for i, j in pairs])
 
     vmem = spec()
     hbm = pl.BlockSpec(memory_space=pltpu.HBM)
@@ -462,6 +532,16 @@
     gain = shape((cells_z,) + plane, F32)
     edge = shape((shots, REACH) + plane, F32)
     like = lambda array: pltpu.VMEM(array.shape, array.dtype)
+    near, far = run(
+        slice_kernel,
+        [edge, edge],
+        in_specs=[hbm],
+        out_specs=[vmem, vmem],
+        scratch=[pltpu.SemaphoreType.DMA((2,))],
+        moved=2**21,
+    )(*pinned(adj_curr))
+    far = with_far(far)
+    near = with_near(near)
     updated, rest, gain_self, gain_lap = run(
         functools.partial(begin_kernel, total_z, blocks),
         [field, field, gain, gain],
@@ -494,27 +574,25 @@
     layers4 = (shots, REACH) + plane
     gains4 = (REACH,) + plane
 
-    def complete(whole, halo, upper):
-        side = blocks - 1 if upper else 0
-        return run(
-            functools.partial(edge_kernel, upper),
-            [field, edge],
-            in_specs=[
-                spec(layers4, (0, side, 0, 0)),
-                spec(layers4, (0, 0, 0, 0)),
-                spec(gains4, (side, 0, 0)),
-            ],
-            out_specs=[spec(layers4, (0, side, 0, 0)), spec(layers4, (0, 0, 0, 0))],
-            grid=(1,),
-            flops=10**7,
-            moved=2 * 2**20,
-            input_output_aliases={0: 0},
-        )(whole, halo, gain_lap)
-
-    wave, edge_low = complete(updated, halo_low, False)
-    wave, edge_high = complete(wave, halo_high, True)
-    next_high = from_above(edge_low)
-    next_low = from_below(edge_high)
+    whole4 = spec(layers4, (0, 0, 0, 0))
+    wave4 = pl.BlockSpec(layers4, lambda step: (0, step * (blocks - 1), 0, 0))
+    wave, near, far = run(
+        edge_kernel,
+        [field, edge, edge],
+        in_specs=[
+            wave4,
+            whole4,
+            whole4,
+            pl.BlockSpec(gains4, lambda step: (step * (blocks - 1), 0, 0)),
+        ],
+        out_specs=[wave4, whole4, whole4],
+        grid=(2,),
+        flops=10**7,
+        moved=2 * 2**20,
+        input_output_aliases={0: 0},
+    )(updated, near, far, gain_lap)
+    far = with_far(far)
+    near = with_near(near)
 
     panel = shape((groups, shots, 2 * part, cells_y), F32)
     scratch_emit = [
@@ -563,8 +641,8 @@
         panels,
         edges,
         edge_gain,
-        next_low,
-        next_high,
+        near,
+        far,
         omega_z,
         omega_x,
         omega_y,
@@ -583,26 +661,38 @@
     gram = run(
         gram_kernel,
         shape((all_shots, cells_y), F32),
-        in_specs=[vmem],
+        in_specs=[vmem, hbm],
         out_specs=vmem,
         flops=10**8,
         moved=2**20,
-    )(got.reshape(all_shots * 2 * part, cells_y))
-    mine = lax.all_to_all(gram.reshape(groups, shots, cells_y), "shot", 0, 0, tiled=True).sum(0)
-    terms = jnp.concatenate([sketch_part, mine], axis=0)
-    sums = lax.all_to_all(
-        jnp.broadcast_to(terms[None], (slabs,) + terms.shape), "slab", 0, 0, tiled=True
-    ).sum(0)
-    sketch = sums[:shots] * (1.0 / math.sqrt(total_z * cells_x * cells_y))
-    group = lax.axis_index("shot")
-    partner = jnp.remainder(group - 1 - jnp.arange(LAGS, dtype=jnp.int32), groups)
-    wanted = (partner[:, None] * shots + jnp.arange(shots, dtype=jnp.int32)[None, :]).reshape(-1)
-    picked = wanted[:, None] == jnp.arange(cells_y, dtype=jnp.int32)[None, :]
-    band = jnp.sum(jnp.where(picked[None], sums[shots:, None, :], 0.0), axis=-1)
-    gram_band = band.reshape(shots, LAGS, shots) * (
-        1.0 / math.sqrt(total_z * cells_x * cells_y // 2)
-    )
-    return (sketch, coarse, gram_band)
+    )(got.reshape(all_shots * 2 * part, cells_y), *pinned(coarse))
+    mine = lax.all_to_all(gram.reshape(groups, shots, cells_y), "shot", 0, 0, tiled=True)
+    terms = run(
+        gather_kernel,
+        shape((slabs, 2 * shots, rank), F32),
+        in_specs=[vmem, vmem],
+        out_specs=vmem,
+        moved=2**16,
+    )(mine, sketch_part)
+    terms = lax.all_to_all(terms, "slab", 0, 0, tiled=True)
+    sketch, gram_band = run(
+        functools.partial(
+            output_kernel,
+            groups,
+            1.0 / math.sqrt(total_z * cells_x * cells_y),
+            1.0 / math.sqrt(total_z * cells_x * cells_y // 2),
+        ),
+        [shape((shots, rank), F32), shape((shots, shots, LAGS), F32)],
+        in_specs=[vmem],
+        out_specs=[hbm, hbm],
+        scratch=[
+            pltpu.VMEM((shots, rank), F32),
+            pltpu.VMEM((shots, shots, LAGS), F32),
+            pltpu.SemaphoreType.DMA((2,)),
+        ],
+        moved=2**16,
+    )(terms)
+    return (sketch, coarse, gram_band.transpose(0, 2, 1))
 
 
 def solution(mesh):

time: 99.5 us -> 94.8 us (0.953)
  blocking collectives: 0 us -> 32.3 us
  starting transfers between devices: 34.5 us -> 14.9 us
  waiting for transfers between devices: 40.7 us -> 23.6 us
  Pallas kernels: 16.3 us -> 18.1 us
  local copies, waits for them, and re-layouts: 4.62 us -> 3.48 us
    all_to_all x0 -> x2, blocking collectives: none -> 32.3 us  [the longest x1 19.8 us: local(): terms = lax.all_to_all(terms, 'slab', 0, 0, tiled=True)]
    all_to_all x2 -> x0, starting transfers between devices: 14.4 us -> none  [the longest x1 9.94 us: local(): lax.all_to_all(jnp.broadcast_to(terms[None], (slabs,) + terms.shape), 'sl...]
    all_to_all x2 -> x0, waiting for transfers between devices: 13.1 us -> none  [the longest x1 6.91 us: local(): lax.all_to_all(gram.reshape(groups, shots, cells_y), 'shot', 0, 0, tiled=...]
    all_to_all x1, waiting for transfers between devices: 24.2 us -> 19.5 us  [local(): got = lax.all_to_all(panels, 'shot', 0, 0, tiled=True)]
    ppermute x4, starting transfers between devices: 10.8 us -> 7.34 us  [the longest x2 3.92 us: with_far(): return lax.ppermute(layers, 'slab', pairs + [(j, i) for i, j in pairs])]
    all_to_all x1, starting transfers between devices: 9.31 us -> 7.58 us  [local(): got = lax.all_to_all(panels, 'shot', 0, 0, tiled=True)]
    pallas_call x3 -> x5, Pallas kernels: 2.01 us -> 3.6 us  [the longest x1 1.37 us: local(): run(slice_kernel, [edge, edge], in_specs=[hbm], out_specs=[vmem, vmem], s...]
    slice x1 -> x0, local copies, waits for them, and re-layouts: 1.44 us -> none  [local(): halo_high = from_above(adj_curr[:, :REACH])]
  transfers between devices with their start and end apart: 7 -> 5, of which waited for: 5 -> 3; matrix products, arithmetic and copies ran while one was open for 3% -> 5% of each run, Pallas kernels for 13% -> 14%
where the time goes in v3:
time: 94.8 us; the launch traced here: 94.4 us
  blocking collectives  32.3 us (34%)
  waiting for transfers between devices  23.6 us (25%)
  Pallas kernels  18.1 us (19%)
  starting transfers between devices  14.9 us (16%)
  local copies, waits for them, and re-layouts  3.48 us (4%)
  other arithmetic  1.14 us (1%)
    all_to_all x1, blocking collectives, local(): terms = lax.all_to_all(terms, 'slab', 0, 0, tiled=True)  19.8 us
    all_to_all x1, waiting for transfers between devices, local(): got = lax.all_to_all(panels, 'shot', 0, 0, tiled=True)  19.5 us
    all_to_all x1, blocking collectives, local(): lax.all_to_all(gram.reshape(groups, shots, cells_y), 'shot', 0, 0, tiled=...  12.5 us
    all_to_all x1, starting transfers between devices, local(): got = lax.all_to_all(panels, 'shot', 0, 0, tiled=True)  7.58 us
    pallas_call x1, Pallas kernels, local(): run(functools.partial(begin_kernel, total_z, blocks), [field, field, gain...  6.51 us
    pallas_call x1, Pallas kernels, local(): run(functools.partial(middle_kernel, blocks), [panel, both, both, shape((...  6.33 us
    ppermute x2, waiting for transfers between devices, with_far(): return lax.ppermute(layers, 'slab', pairs + [(j, i) for i, j in pairs])  4.11 us
    ppermute x2, starting transfers between devices, with_far(): return lax.ppermute(layers, 'slab', pairs + [(j, i) for i, j in pairs])  3.92 us
  transfers between devices with their start and end apart: 5, of which 3 were waited for; matrix products, arithmetic and copies ran while one was open for 5% of the time, Pallas kernels for 14%

profile of v3, /device:TPU:1, one launch (start us, length us, event | category | flops | bytes accessed | tf_op | source)
XLA Modules:
  0.0 94.4 jit_solution(15072841581458915729)
XLA Ops:
  0.6 0.0 copy-start
  0.6 0.0 copy-start.5
  0.7 1.4 %shard_map.167 = (f32[2,4,128,128]{3,2,1,0:T(8,128)S(1)}, f32[2,4,128,128]{3,2,1,0:T(8,128)S(1)}) custom-call(f32[2,16,128,128]{3,2,1,0:T(8,128)} %curr.3), custom_call_target="tpu_custom_call" | custom-call | bytes 2097152 | tf_op jit(solution)/shard_map/pallas_call | solution.py:535
  2.0 3.3 %collective-permute-start = (f32[2,4,128,128]{3,2,1,0:T(8,128)S(1)}, f32[2,4,128,128]{3,2,1,0:T(8,128)S(1)}, u32[]{:S(2)}, u32[]{:S(2)}) collective-permute-start(f32[2,4,128,128]{3,2,1,0:T(8,128)S(1)} %get-tuple-element.21), channel_id=1, source_target_pairs={{0,1},{1,0},{2,3},{3,2},{4,5},{5,4},{6,7},{7,6},{8,9},{9,8},{10,11... | collective-permute-start | bytes 1572872 | tf_op jit(solution)/shard_map/ppermute | solution.py:519
  5.4 1.9 %collective-permute-start.1 = (f32[2,4,128,128]{3,2,1,0:T(8,128)S(1)}, f32[2,4,128,128]{3,2,1,0:T(8,128)S(1)}, u32[]{:S(2)}, u32[]{:S(2)}) collective-permute-start(f32[2,4,128,128]{3,2,1,0:T(8,128)S(1)} %get-tuple-element.22), channel_id=1, source_target_pairs={{1,2},{3,4},{5,6},{7,8},{9,10},{11,12},{13,14},{2,1},{4,3},{6,5},{... | collective-permute-start | bytes 1572872 | tf_op jit(solution)/shard_map/ppermute | solution.py:523
  7.3 0.0 copy-done
  7.3 0.0 copy-done.5
  7.3 6.5 %shard_map.166 = (f32[2,16,128,128]{3,2,1,0:T(8,128)S(1)}, f32[2,16,128,128]{3,2,1,0:T(8,128)S(1)}, f32[16,128,128]{2,1,0:T(8,128)S(1)}, f32[16,128,128]{2,1,0:T(8,128)S(1)}) custom-call(s32[3]{0:T(128)S(1)} %copy-done.5, f32[2,16,128,128]{3,2,1,0:T(8,128)S(1)} %copy-done, f32[16,128,128]{2,1,0:T(8,128)} %courant_hbm.1, f32[2,16,128,128]{3,2,1,0:T(8,128)} %prev_hbm.1, ...), custom_call_target="tpu_custom_call" | custom-call | flops 2000000000 | bytes 11534336 | tf_op jit(solution)/shard_map/pallas_call | solution.py:545
  13.8 0.0 collective-permute-done.near
  13.8 2.0 %collective-permute-done.1.far = f32[2,4,128,128]{3,2,1,0:T(8,128)S(1)} collective-permute-done((f32[2,4,128,128]{3,2,1,0:T(8,128)S(1)}, f32[2,4,128,128]{3,2,1,0:T(8,128)S(1)}, u32[]{:S(2)}, u32[]{:S(2)}) %collective-permute-start.1) | collective-permute-done | bytes 524320 | tf_op jit(solution)/shard_map/ppermute | solution.py:523
  15.8 0.5 shard_map.168
  16.4 0.1 collective-permute-start.2
  16.5 2.0 %collective-permute-start.3 = (f32[2,4,128,128]{3,2,1,0:T(8,128)S(1)}, f32[2,4,128,128]{3,2,1,0:T(8,128)S(1)}, u32[]{:S(2)}, u32[]{:S(2)}) collective-permute-start(f32[2,4,128,128]{3,2,1,0:T(8,128)S(1)} %get-tuple-element.31), channel_id=1, source_target_pairs={{1,2},{3,4},{5,6},{7,8},{9,10},{11,12},{13,14},{2,1},{4,3},{6,5},{... | collective-permute-start | bytes 1572872 | tf_op jit(solution)/shard_map/ppermute | solution.py:523
  18.5 0.0 copy-start.1
  18.5 0.0 copy-start.2
  18.5 0.0 copy-start.3
  18.5 0.0 copy-start.4
  18.5 6.3 %shard_map.169 = (f32[16,2,64,128]{3,2,1,0:T(8,128)}, f32[2,8,128,128]{3,2,1,0:T(8,128)S(1)}, f32[2,8,128,128]{3,2,1,0:T(8,128)S(1)}, f32[2,128]{1,0:T(2,128)S(1)}) custom-call(f32[2,16,128,128]{3,2,1,0:T(8,128)S(1)} %get-tuple-element.24.wave, f32[2,16,128,128]{3,2,1,0:T(8,128)S(1)} %get-tuple-element.25.rest, ...), custom_call_target="tpu_custom_call" | custom-call | flops 2000000000 | bytes 11534336 | tf_op jit(solution)/shard_map/pallas_call | solution.py:605
  24.9 0.0 collective-permute-done.2.near
  24.9 2.1 %collective-permute-done.3.far = f32[2,4,128,128]{3,2,1,0:T(8,128)S(1)} collective-permute-done((f32[2,4,128,128]{3,2,1,0:T(8,128)S(1)}, f32[2,4,128,128]{3,2,1,0:T(8,128)S(1)}, u32[]{:S(2)}, u32[]{:S(2)}) %collective-permute-start.3) | collective-permute-done | bytes 524320 | tf_op jit(solution)/shard_map/ppermute | solution.py:523
  27.0 1.7 %shard_map.170 = (f32[16,2,64,128]{3,2,1,0:T(8,128)}, f32[2,128]{1,0:T(2,128)S(1)}) custom-call(f32[16,2,64,128]{3,2,1,0:T(8,128)} %get-tuple-element.27.panels_before, f32[2,8,128,128]{3,2,1,0:T(8,128)S(1)} %get-tuple-element.28.edges, f32[2,8,128,128]{3,2,1,0:T(8,128)S(1)} %get-tuple-element.29.edge_gain, ...), custom_call_target="tpu_custom_call", output_to_operand_aliasing={{0}: (0, {})} | custom-call | flops 500000000 | bytes 5242880 | tf_op jit(solution)/shard_map/pallas_call | solution.py:631
  28.7 7.6 %all-to-all-start = ((f32[16,2,64,128]{3,2,1,0:T(8,128)}), f32[16,2,64,128]{3,2,1,0:T(8,128)S(1)}, u32[]{:S(2)}, u32[]{:S(2)}) async-start(f32[16,2,64,128]{3,2,1,0:T(8,128)} %get-tuple-element.33), calls=%async_computation | async-start | bytes 2097152 | tf_op jit(solution)/shard_map/all_to_all | solution.py:652
  36.3 1.9 %copy.24 = f32[8,2,2,2,32,128]{5,0,4,1,2,3:T(8,128)S(1)} copy(f32[8,2,2,2,32,128]{5,4,3,2,1,0:T(8,128)} %bitcast.1) | data formatting | bytes 2097152 | tf_op jit(solution)/shard_map/reshape | solution.py:654
  38.2 1.3 %copy.21 = f32[2,2,8,2,32,128]{5,4,3,2,1,0:T(8,128)S(1)} copy(f32[2,2,8,2,32,128]{5,4,0,1,3,2:T(8,128)} %bitcast.3) | data formatting | bytes 2097152 | tf_op jit(solution)/shard_map/transpose | solution.py:655
  39.5 0.1 concatenate.10
  39.6 0.1 concatenate.12
  39.8 1.1 %pad_maximum_fusion.coarse = f32[2,16,8192]{2,1,0:T(8,128)} fusion(f32[2,4,8192]{2,1,0:T(4,128)S(1)} %concatenate.12, f32[2,8,8192]{2,1,0:T(8,128)S(1)} %bitcast.19, f32[2,4,8192]{2,1,0:T(4,128)S(1)} %concatenate.10), kind=kLoop, calls=%fused_computation | loop fusion | flops 524288 | bytes 2097152 | tf_op jit(solution)/shard_map/concatenate | solution.py:656
  40.9 19.5 %all-to-all-done = f32[16,2,64,128]{3,2,1,0:T(8,128)S(1)} async-done(((f32[16,2,64,128]{3,2,1,0:T(8,128)}), f32[16,2,64,128]{3,2,1,0:T(8,128)S(1)}, u32[]{:S(2)}, u32[]{:S(2)}) %all-to-all-start) | async-done | bytes 1048608 | tf_op jit(solution)/shard_map/all_to_all | solution.py:652
  60.4 1.0 %shard_map.171 = f32[32,128]{1,0:T(8,128)S(1)} custom-call(f32[2048,128]{1,0:T(8,128)S(1)} %bitcast.15, f32[2,16,8192]{2,1,0:T(8,128)} %pad_maximum_fusion.coarse), custom_call_target="tpu_custom_call" | custom-call | flops 100000000 | bytes 1048576 | tf_op jit(solution)/shard_map/pallas_call | solution.py:661
  61.4 12.5 %all_to_all.15.mine = f32[16,2,128]{2,1,0:T(2,128)S(1)} all-to-all(f32[16,2,128]{2,1,0:T(2,128)S(1)} %bitcast.16), channel_id=1, replica_groups=mesh['shot'=16,'slab'=16] {'shot'}, dimensions={0} | all-to-all | bytes 32768 | tf_op jit(solution)/shard_map/all_to_all | solution.py:669
  73.9 19.8 %all_to_all.16.terms = f32[16,4,128]{2,1,0:T(4,128)S(1)} all-to-all(f32[16,4,128]{2,1,0:T(4,128)S(1)} %shard_map.172), channel_id=1, replica_groups=mesh['shot'=16,'slab'=16] {'slab'}, dimensions={0} | all-to-all | bytes 65536 | tf_op jit(solution)/shard_map/all_to_all | solution.py:677
  93.7 0.7 shard_map.173
  (7 shorter events, 0.1 us)
Async XLA Ops:
  0.6 6.6 %copy-start = (f32[2,16,128,128]{3,2,1,0:T(8,128)S(1)}, f32[2,16,128,128]{3,2,1,0:T(8,128)}, u32[]{:S(2)}) copy-start(f32[2,16,128,128]{3,2,1,0:T(8,128)} %curr.3) | copy-start | bytes 6291460
  0.6 6.6 %copy-start.5 = (s32[3]{0:T(128)S(1)}, s32[3]{0:T(128)}, u32[]{:S(2)}) copy-start(s32[3]{0:T(128)} %pml.1) | copy-start | bytes 40
  2.0 11.8 %collective-permute-start = (f32[2,4,128,128]{3,2,1,0:T(8,128)S(1)}, f32[2,4,128,128]{3,2,1,0:T(8,128)S(1)}, u32[]{:S(2)}, u32[]{:S(2)}) collective-permute-start(f32[2,4,128,128]{3,2,1,0:T(8,128)S(1)} %get-tuple-element.21), channel_id=1, source_target_pairs={{0,1},{1,0},{2,3},{3,2},{4,5},{5,4},{6,7},{7,6},{8,9},{9,8},{10,11... | collective-permute-start | bytes 1572872 | tf_op jit(solution)/shard_map/ppermute | solution.py:519
  5.4 10.5 %collective-permute-start.1 = (f32[2,4,128,128]{3,2,1,0:T(8,128)S(1)}, f32[2,4,128,128]{3,2,1,0:T(8,128)S(1)}, u32[]{:S(2)}, u32[]{:S(2)}) collective-permute-start(f32[2,4,128,128]{3,2,1,0:T(8,128)S(1)} %get-tuple-element.22), channel_id=1, source_target_pairs={{1,2},{3,4},{5,6},{7,8},{9,10},{11,12},{13,14},{2,1},{4,3},{6,5},{... | collective-permute-start | bytes 1572872 | tf_op jit(solution)/shard_map/ppermute | solution.py:523
  16.4 8.5 %collective-permute-start.2 = (f32[2,4,128,128]{3,2,1,0:T(8,128)S(1)}, f32[2,4,128,128]{3,2,1,0:T(8,128)S(1)}, u32[]{:S(2)}, u32[]{:S(2)}) collective-permute-start(f32[2,4,128,128]{3,2,1,0:T(8,128)S(1)} %get-tuple-element.30), channel_id=1, source_target_pairs={{0,1},{1,0},{2,3},{3,2},{4,5},{5,4},{6,7},{7,6},{8,9},{9,8},{10,11... | collective-permute-start | bytes 1572872 | tf_op jit(solution)/shard_map/ppermute | solution.py:519
  16.5 10.5 %collective-permute-start.3 = (f32[2,4,128,128]{3,2,1,0:T(8,128)S(1)}, f32[2,4,128,128]{3,2,1,0:T(8,128)S(1)}, u32[]{:S(2)}, u32[]{:S(2)}) collective-permute-start(f32[2,4,128,128]{3,2,1,0:T(8,128)S(1)} %get-tuple-element.31), channel_id=1, source_target_pairs={{1,2},{3,4},{5,6},{7,8},{9,10},{11,12},{13,14},{2,1},{4,3},{6,5},{... | collective-permute-start | bytes 1572872 | tf_op jit(solution)/shard_map/ppermute | solution.py:523
  18.5 8.5 %copy-start.1 = (s32[128,128]{1,0:T(8,128)S(1)}, s32[128,128]{1,0:T(8,128)}, u32[]{:S(2)}) copy-start(s32[128,128]{1,0:T(8,128)} %omega_x.1) | copy-start | bytes 196612
  18.5 8.5 %copy-start.2 = (s32[128,128]{1,0:T(8,128)S(1)}, s32[128,128]{1,0:T(8,128)}, u32[]{:S(2)}) copy-start(s32[128,128]{1,0:T(8,128)} %omega_y.1) | copy-start | bytes 196612
  18.5 8.5 %copy-start.3 = (bf16[256,128]{1,0:T(8,128)(2,1)S(1)}, bf16[256,128]{1,0:T(8,128)(2,1)}, u32[]{:S(2)}) copy-start(bf16[256,128]{1,0:T(8,128)(2,1)} %constant.8.clone.pool_hbm.pool) | copy-start | bytes 196612
  18.5 8.5 %copy-start.4 = (s32[16,128]{1,0:T(8,128)S(1)}, s32[16,128]{1,0:T(8,128)}, u32[]{:S(2)}) copy-start(s32[16,128]{1,0:T(8,128)} %omega_z.1) | copy-start | bytes 24580
  28.7 31.7 %all-to-all-start = ((f32[16,2,64,128]{3,2,1,0:T(8,128)}), f32[16,2,64,128]{3,2,1,0:T(8,128)S(1)}, u32[]{:S(2)}, u32[]{:S(2)}) async-start(f32[16,2,64,128]{3,2,1,0:T(8,128)} %get-tuple-element.33), calls=%async_computation | async-start | bytes 2097152 | tf_op jit(solution)/shard_map/all_to_all | solution.py:652

commit v4 on v3

--- a/solution.py
+++ b/solution.py
@@ -99,7 +99,7 @@
     total_z,
     blocks,
     pml,
-    curr,
+    curr_hbm,
     courant_hbm,
     prev_hbm,
     traces_hbm,
@@ -112,6 +112,7 @@
     rest,
     gain_self,
     gain_lap,
+    curr,
     courant,
     prev,
     traces,
@@ -139,6 +140,7 @@
     few = len(pairs)
     for block in range(blocks):
         span = pl.ds(block * step, step)
+        pairs.append((curr_hbm.at[:, span], curr.at[:, span]))
         pairs.append((courant_hbm.at[span], courant.at[span]))
         pairs.append((prev_hbm.at[:, span], prev.at[:, span]))
     copies = fetch(pairs, sems)
@@ -188,8 +190,11 @@
             )
             rest[shot, z] = scale * source[:, cells_y:] - prev_gain * now
 
+    copies[few].wait()
     for block in range(blocks):
-        for copy in copies[few + 2 * block : few + 2 * block + 2]:
+        if block + 1 < blocks:
+            copies[few + 3 * block + 3].wait()
+        for copy in copies[few + 3 * block + 1 : few + 3 * block + 3]:
             copy.wait()
         pl.loop(block * step, (block + 1) * step)(one_layer)
 
@@ -273,7 +278,6 @@
     gain_lap,
     snaps_hbm,
     omega_z_hbm,
-    omega_x_hbm,
     omega_y_hbm,
     band_y_hbm,
     band_x_hbm,
@@ -281,15 +285,13 @@
     panels,
     edges,
     edge_gain,
-    sketch,
+    total,
     snaps,
     omega_z,
-    omega_x,
     omega_y,
     band_y,
     band_x,
     pool,
-    total,
     spread_y,
     lines,
     chunks,
@@ -304,7 +306,6 @@
         (omega_y_hbm, omega_y),
         (omega_z_hbm, omega_z),
         (pool_hbm, pool),
-        (omega_x_hbm, omega_x),
     ]
     few = len(pairs)
     order = list(range(1, blocks - 1)) + [0, blocks - 1]
@@ -350,9 +351,6 @@
     for copy in copies[few + blocks - 2 :]:
         copy.wait()
     pl.loop(0, 2 * REACH)(edge_layer)
-    weights_x = omega_x[...].astype(F32)
-    for shot in range(shots):
-        sketch[shot : shot + 1, :] = jnp.sum(total[shot] * weights_x, axis=0, keepdims=True)
     send.wait()
 
 
@@ -363,12 +361,10 @@
     near,
     far,
     omega_z,
-    omega_x,
     omega_y,
     pool,
     before,
     panels,
-    sketch,
     total,
     spread_y,
     lines,
@@ -378,8 +374,11 @@
     shots = edges.shape[0]
     cells_z = omega_z.shape[0]
     spread_y[...] = omega_y[...].astype(F32).astype(BF16)
-    total[...] = jnp.zeros_like(total)
+    total[...] = before[...]
     is_odd = odd_slab() == 1
+    part = chunks.shape[2]
+    pieces = chunks.shape[0] // (2 * REACH)
+    sends = []
 
     def halo(shot, upper):
         first, second = (far, near) if upper else (near, far)
@@ -396,19 +395,24 @@
             ]
             weight_z = omega_z[z : z + 1, :].astype(F32)
             emit(gradients, index, spread_y, weight_z, pool, chunks, total, lines)
-    part = chunks.shape[2]
-    send = pltpu.make_async_copy(chunks, panels.at[:, :, pl.ds(part, part)], sem.at[0])
-    send.start()
+            span = pl.ds(index * pieces, pieces)
+            send = pltpu.make_async_copy(
+                chunks.at[span], panels.at[span, :, pl.ds(part, part)], sem.at[index]
+            )
+            send.start()
+            sends.append(send)
+    for send in sends:
+        send.wait()
+
+
+def sketch_kernel(total, omega_x, sketch):
     weights_x = omega_x[...].astype(F32)
-    for shot in range(shots):
-        sketch[shot : shot + 1, :] = before[shot : shot + 1, :] + jnp.sum(
-            total[shot] * weights_x, axis=0, keepdims=True
-        )
-    send.wait()
-
-
-def gram_kernel(panels, coarse, out):
-    del coarse
+    for shot in range(sketch.shape[0]):
+        sketch[shot : shot + 1, :] = jnp.sum(total[shot] * weights_x, axis=0, keepdims=True)
+
+
+def gram_kernel(panels, coarse, sketch, out):
+    del coarse, sketch
     shots = out.shape[0]
     part = panels.shape[0] // shots
     width = 8
@@ -545,9 +549,10 @@
     updated, rest, gain_self, gain_lap = run(
         functools.partial(begin_kernel, total_z, blocks),
         [field, field, gain, gain],
-        in_specs=[pl.BlockSpec(memory_space=pltpu.SMEM), vmem] + [hbm] * 8,
+        in_specs=[pl.BlockSpec(memory_space=pltpu.SMEM)] + [hbm] * 9,
         out_specs=[vmem] * 4,
         scratch=[
+            like(adj_curr),
             like(courant),
             like(adj_prev),
             like(traces),
@@ -559,15 +564,22 @@
             pltpu.VMEM((cells_z, cells_y), F32),
             pltpu.VMEM(plane, F32),
             pltpu.VMEM((shots, 2 * cells_y, 2 * receivers), BF16),
-            pltpu.SemaphoreType.DMA((6 + 2 * blocks,)),
+            pltpu.SemaphoreType.DMA((6 + 3 * blocks,)),
         ],
         flops=2 * 10**9,
         moved=11 * 2**20,
     )(
         pml_cells,
-        adj_curr,
         *pinned(
-            courant, adj_prev, traces, receiver_z, receiver_x, receiver_y, band_y, band_x
+            adj_curr,
+            courant,
+            adj_prev,
+            traces,
+            receiver_z,
+            receiver_x,
+            receiver_y,
+            band_y,
+            band_x,
         ),
     )
 
@@ -595,29 +607,28 @@
     near = with_near(near)
 
     panel = shape((groups, shots, 2 * part, cells_y), F32)
+    spread = shape((shots, cells_x, rank), F32)
     scratch_emit = [
-        pltpu.VMEM((shots, cells_x, rank), F32),
         pltpu.VMEM((cells_y, rank), BF16),
         pltpu.VMEM((shots,) + plane, F32),
         pltpu.VMEM((groups, shots, part, cells_y), F32),
     ]
     both = shape((shots, 2 * REACH) + plane, F32)
-    panels, edges, edge_gain, sketch_mid = run(
+    panels, edges, edge_gain, total_mid = run(
         functools.partial(middle_kernel, blocks),
-        [panel, both, both, shape((shots, rank), F32)],
-        in_specs=[vmem] * 4 + [hbm] * 7,
+        [panel, both, both, spread],
+        in_specs=[vmem] * 4 + [hbm] * 6,
         out_specs=[hbm, vmem, vmem, vmem],
         scratch=[
             like(forward_snaps),
             like(omega_z),
-            like(omega_x),
             like(omega_y),
             like(band_y),
             like(band_x),
             like(pool),
         ]
         + scratch_emit
-        + [pltpu.SemaphoreType.DMA((7 + blocks,))],
+        + [pltpu.SemaphoreType.DMA((6 + blocks,))],
         flops=2 * 10**9,
         moved=11 * 2**20,
     )(
@@ -625,15 +636,15 @@
         rest,
         gain_self,
         gain_lap,
-        *pinned(forward_snaps, omega_z, omega_x, omega_y, band_y, band_x, pool),
-    )
-
-    panels, sketch_part = run(
+        *pinned(forward_snaps, omega_z, omega_y, band_y, band_x, pool),
+    )
+
+    panels, total = run(
         finish_kernel,
-        [panel, shape((shots, rank), F32)],
-        in_specs=[hbm] + [vmem] * 9,
+        [panel, spread],
+        in_specs=[hbm] + [vmem] * 8,
         out_specs=[hbm, vmem],
-        scratch=scratch_emit + [pltpu.SemaphoreType.DMA((1,))],
+        scratch=scratch_emit + [pltpu.SemaphoreType.DMA((2 * REACH,))],
         flops=5 * 10**8,
         moved=5 * 2**20,
         input_output_aliases={0: 0},
@@ -644,11 +655,18 @@
         near,
         far,
         omega_z,
-        omega_x,
         omega_y,
         pool,
-        sketch_mid,
-    )
+        total_mid,
+    )
+    sketch_part = run(
+        sketch_kernel,
+        shape((shots, rank), F32),
+        in_specs=[vmem, vmem],
+        out_specs=vmem,
+        flops=2 * 10**5,
+        moved=2**18,
+    )(total, omega_x)
     got = lax.all_to_all(panels, "shot", 0, 0, tiled=True)
 
     folded = panels.reshape(inner, half_x // part, shots, 2, part, cells_y)
@@ -661,11 +679,11 @@
     gram = run(
         gram_kernel,
         shape((all_shots, cells_y), F32),
-        in_specs=[vmem, hbm],
+        in_specs=[vmem, hbm, hbm],
         out_specs=vmem,
         flops=10**8,
         moved=2**20,
-    )(got.reshape(all_shots * 2 * part, cells_y), *pinned(coarse))
+    )(got.reshape(all_shots * 2 * part, cells_y), *pinned(coarse, sketch_part))
     mine = lax.all_to_all(gram.reshape(groups, shots, cells_y), "shot", 0, 0, tiled=True)
     terms = run(
         gather_kernel,

time: 94.8 us -> 94.7 us (level)
    pallas_call x3 -> x4, Pallas kernels: 8.99 us -> 8.56 us  [the longest x1 6 us: local(): run(functools.partial(middle_kernel, blocks), [panel, both, both, spread]...]
  transfers between devices with their start and end apart: 5 -> 5, of which waited for: 3 -> 3; matrix products, arithmetic and copies ran while one was open for 5% -> 5% of each run, Pallas kernels for 14% -> 13%
where the time goes in v4:
time: 94.7 us; the launch traced here: 94.3 us
  blocking collectives  32.5 us (34%)
  waiting for transfers between devices  23.7 us (25%)
  Pallas kernels  17.6 us (19%)
  starting transfers between devices  15.1 us (16%)
  local copies, waits for them, and re-layouts  3.46 us (4%)
  other arithmetic  1.14 us (1%)
    all_to_all x1, blocking collectives, local(): terms = lax.all_to_all(terms, 'slab', 0, 0, tiled=True)  20.3 us
    all_to_all x1, waiting for transfers between devices, local(): got = lax.all_to_all(panels, 'shot', 0, 0, tiled=True)  19.3 us
    all_to_all x1, blocking collectives, local(): lax.all_to_all(gram.reshape(groups, shots, cells_y), 'shot', 0, 0, tiled=...  12.2 us
    all_to_all x1, starting transfers between devices, local(): got = lax.all_to_all(panels, 'shot', 0, 0, tiled=True)  7.71 us
    pallas_call x1, Pallas kernels, local(): run(functools.partial(begin_kernel, total_z, blocks), [field, field, gain...  6.58 us
    pallas_call x1, Pallas kernels, local(): run(functools.partial(middle_kernel, blocks), [panel, both, both, spread]...  6 us
    ppermute x2, waiting for transfers between devices, with_far(): return lax.ppermute(layers, 'slab', pairs + [(j, i) for i, j in pairs])  4.39 us
    ppermute x2, starting transfers between devices, with_far(): return lax.ppermute(layers, 'slab', pairs + [(j, i) for i, j in pairs])  3.92 us
  transfers between devices with their start and end apart: 5, of which 3 were waited for; matrix products, arithmetic and copies ran while one was open for 5% of the time, Pallas kernels for 13%

profile of v4, /device:TPU:1, one launch (start us, length us, event | category | flops | bytes accessed | tf_op | source)
XLA Modules:
  0.0 94.3 jit_solution(9921593655350784114)
XLA Ops:
  0.6 1.2 %shard_map.167 = (f32[2,4,128,128]{3,2,1,0:T(8,128)S(1)}, f32[2,4,128,128]{3,2,1,0:T(8,128)S(1)}) custom-call(f32[2,16,128,128]{3,2,1,0:T(8,128)} %curr.1), custom_call_target="tpu_custom_call" | custom-call | bytes 2097152 | tf_op jit(solution)/shard_map/pallas_call | solution.py:539
  1.9 3.3 %collective-permute-start = (f32[2,4,128,128]{3,2,1,0:T(8,128)S(1)}, f32[2,4,128,128]{3,2,1,0:T(8,128)S(1)}, u32[]{:S(2)}, u32[]{:S(2)}) collective-permute-start(f32[2,4,128,128]{3,2,1,0:T(8,128)S(1)} %get-tuple-element.21), channel_id=1, source_target_pairs={{0,1},{1,0},{2,3},{3,2},{4,5},{5,4},{6,7},{7,6},{8,9},{9,8},{10,11... | collective-permute-start | bytes 1572872 | tf_op jit(solution)/shard_map/ppermute | solution.py:523
  5.2 1.9 %collective-permute-start.1 = (f32[2,4,128,128]{3,2,1,0:T(8,128)S(1)}, f32[2,4,128,128]{3,2,1,0:T(8,128)S(1)}, u32[]{:S(2)}, u32[]{:S(2)}) collective-permute-start(f32[2,4,128,128]{3,2,1,0:T(8,128)S(1)} %get-tuple-element.22), channel_id=1, source_target_pairs={{1,2},{3,4},{5,6},{7,8},{9,10},{11,12},{13,14},{2,1},{4,3},{6,5},{... | collective-permute-start | bytes 1572872 | tf_op jit(solution)/shard_map/ppermute | solution.py:527
  7.1 6.6 %shard_map.166 = (f32[2,16,128,128]{3,2,1,0:T(8,128)S(1)}, f32[2,16,128,128]{3,2,1,0:T(8,128)S(1)}, f32[16,128,128]{2,1,0:T(8,128)S(1)}, f32[16,128,128]{2,1,0:T(8,128)S(1)}) custom-call(s32[3]{0:T(128)S(1)} %copy-done.6, f32[2,16,128,128]{3,2,1,0:T(8,128)} %curr.1, f32[16,128,128]{2,1,0:T(8,128)} %courant_hbm.1, f32[2,16,128,128]{3,2,1,0:T(8,128)} %prev_hbm.1, ...), custom_call_target="tpu_custom_call" | custom-call | flops 2000000000 | bytes 11534336 | tf_op jit(solution)/shard_map/pallas_call | solution.py:549
  13.7 0.0 collective-permute-done.near
  13.7 2.0 %collective-permute-done.1.far = f32[2,4,128,128]{3,2,1,0:T(8,128)S(1)} collective-permute-done((f32[2,4,128,128]{3,2,1,0:T(8,128)S(1)}, f32[2,4,128,128]{3,2,1,0:T(8,128)S(1)}, u32[]{:S(2)}, u32[]{:S(2)}) %collective-permute-start.1) | collective-permute-done | bytes 524320 | tf_op jit(solution)/shard_map/ppermute | solution.py:527
  15.7 0.5 shard_map.168
  16.2 0.1 collective-permute-start.2
  16.3 2.0 %collective-permute-start.3 = (f32[2,4,128,128]{3,2,1,0:T(8,128)S(1)}, f32[2,4,128,128]{3,2,1,0:T(8,128)S(1)}, u32[]{:S(2)}, u32[]{:S(2)}) collective-permute-start(f32[2,4,128,128]{3,2,1,0:T(8,128)S(1)} %get-tuple-element.31), channel_id=1, source_target_pairs={{1,2},{3,4},{5,6},{7,8},{9,10},{11,12},{13,14},{2,1},{4,3},{6,5},{... | collective-permute-start | bytes 1572872 | tf_op jit(solution)/shard_map/ppermute | solution.py:527
  18.3 0.0 copy-start
  18.4 0.0 copy-start.1
  18.4 0.0 copy-start.3
  18.4 6.0 %shard_map.169 = (f32[16,2,64,128]{3,2,1,0:T(8,128)}, f32[2,8,128,128]{3,2,1,0:T(8,128)S(1)}, f32[2,8,128,128]{3,2,1,0:T(8,128)S(1)}, f32[2,128,128]{2,1,0:T(8,128)S(1)}) custom-call(f32[2,16,128,128]{3,2,1,0:T(8,128)S(1)} %get-tuple-element.24.wave, f32[2,16,128,128]{3,2,1,0:T(8,128)S(1)} %get-tuple-element.25.rest, ...), custom_call_target="tpu_custom_call" | custom-call | flops 2000000000 | bytes 11534336 | tf_op jit(solution)/shard_map/pallas_call | solution.py:617
  24.4 0.0 collective-permute-done.2.near
  24.4 2.4 %collective-permute-done.3.far = f32[2,4,128,128]{3,2,1,0:T(8,128)S(1)} collective-permute-done((f32[2,4,128,128]{3,2,1,0:T(8,128)S(1)}, f32[2,4,128,128]{3,2,1,0:T(8,128)S(1)}, u32[]{:S(2)}, u32[]{:S(2)}) %collective-permute-start.3) | collective-permute-done | bytes 524320 | tf_op jit(solution)/shard_map/ppermute | solution.py:527
  26.8 0.0 copy-done.1
  26.8 1.5 %shard_map.170 = (f32[16,2,64,128]{3,2,1,0:T(8,128)}, f32[2,128,128]{2,1,0:T(8,128)S(1)}) custom-call(f32[16,2,64,128]{3,2,1,0:T(8,128)} %get-tuple-element.27.panels_before, f32[2,8,128,128]{3,2,1,0:T(8,128)S(1)} %get-tuple-element.28.edges, f32[2,8,128,128]{3,2,1,0:T(8,128)S(1)} %get-tuple-element.29.edge_gain, ...), custom_call_target="tpu_custom_call", output_to_operand_aliasing={{0}: (0, {})} | custom-call | flops 500000000 | bytes 5242880 | tf_op jit(solution)/shard_map/pallas_call | solution.py:642
  28.4 0.0 copy-start.2
  28.4 7.7 %all-to-all-start = ((f32[16,2,64,128]{3,2,1,0:T(8,128)}), f32[16,2,64,128]{3,2,1,0:T(8,128)S(1)}, u32[]{:S(2)}, u32[]{:S(2)}) async-start(f32[16,2,64,128]{3,2,1,0:T(8,128)} %get-tuple-element.33), calls=%async_computation | async-start | bytes 2097152 | tf_op jit(solution)/shard_map/all_to_all | solution.py:670
  36.2 0.0 copy-start.4
  36.2 1.8 %copy.24 = f32[8,2,2,2,32,128]{5,0,4,1,2,3:T(8,128)S(1)} copy(f32[8,2,2,2,32,128]{5,4,3,2,1,0:T(8,128)} %bitcast.1) | data formatting | bytes 2097152 | tf_op jit(solution)/shard_map/reshape | solution.py:672
  38.1 1.3 %copy.21 = f32[2,2,8,2,32,128]{5,4,3,2,1,0:T(8,128)S(1)} copy(f32[2,2,8,2,32,128]{5,4,0,1,3,2:T(8,128)} %bitcast.3) | data formatting | bytes 2097152 | tf_op jit(solution)/shard_map/transpose | solution.py:673
  39.4 0.0 copy-done.4
  39.4 0.1 concatenate.10
  39.5 0.1 concatenate.12
  39.6 0.0 copy-start.5
  39.7 1.1 %pad_maximum_fusion.coarse = f32[2,16,8192]{2,1,0:T(8,128)} fusion(f32[2,4,8192]{2,1,0:T(4,128)S(1)} %concatenate.12, f32[2,8,8192]{2,1,0:T(8,128)S(1)} %bitcast.19, f32[2,4,8192]{2,1,0:T(4,128)S(1)} %concatenate.10), kind=kLoop, calls=%fused_computation | loop fusion | flops 524288 | bytes 2097152 | tf_op jit(solution)/shard_map/concatenate | solution.py:674
  40.8 19.3 %all-to-all-done = f32[16,2,64,128]{3,2,1,0:T(8,128)S(1)} async-done(((f32[16,2,64,128]{3,2,1,0:T(8,128)}), f32[16,2,64,128]{3,2,1,0:T(8,128)S(1)}, u32[]{:S(2)}, u32[]{:S(2)}) %all-to-all-start) | async-done | bytes 1048608 | tf_op jit(solution)/shard_map/all_to_all | solution.py:670
  60.1 1.0 %shard_map.172 = f32[32,128]{1,0:T(8,128)S(1)} custom-call(f32[2048,128]{1,0:T(8,128)S(1)} %bitcast.15, f32[2,16,8192]{2,1,0:T(8,128)} %pad_maximum_fusion.coarse, f32[2,128]{1,0:T(2,128)} %copy-done.4), custom_call_target="tpu_custom_call" | custom-call | flops 100000000 | bytes 1048576 | tf_op jit(solution)/shard_map/pallas_call | solution.py:679
  61.0 12.2 %all_to_all.15.mine = f32[16,2,128]{2,1,0:T(2,128)S(1)} all-to-all(f32[16,2,128]{2,1,0:T(2,128)S(1)} %bitcast.16), channel_id=1, replica_groups=mesh['shot'=16,'slab'=16] {'shot'}, dimensions={0} | all-to-all | bytes 32768 | tf_op jit(solution)/shard_map/all_to_all | solution.py:687
  73.2 20.3 %all_to_all.16.terms = f32[16,4,128]{2,1,0:T(4,128)S(1)} all-to-all(f32[16,4,128]{2,1,0:T(4,128)S(1)} %shard_map.173), channel_id=1, replica_groups=mesh['shot'=16,'slab'=16] {'slab'}, dimensions={0} | all-to-all | bytes 65536 | tf_op jit(solution)/shard_map/all_to_all | solution.py:695
  93.6 0.7 shard_map.174
  (10 shorter events, 0.1 us)
Async XLA Ops:
  0.6 6.5 %copy-start.6 = (s32[3]{0:T(128)S(1)}, s32[3]{0:T(128)}, u32[]{:S(2)}) copy-start(s32[3]{0:T(128)} %pml.1) | copy-start | bytes 40
  1.9 11.8 %collective-permute-start = (f32[2,4,128,128]{3,2,1,0:T(8,128)S(1)}, f32[2,4,128,128]{3,2,1,0:T(8,128)S(1)}, u32[]{:S(2)}, u32[]{:S(2)}) collective-permute-start(f32[2,4,128,128]{3,2,1,0:T(8,128)S(1)} %get-tuple-element.21), channel_id=1, source_target_pairs={{0,1},{1,0},{2,3},{3,2},{4,5},{5,4},{6,7},{7,6},{8,9},{9,8},{10,11... | collective-permute-start | bytes 1572872 | tf_op jit(solution)/shard_map/ppermute | solution.py:523
  5.2 10.5 %collective-permute-start.1 = (f32[2,4,128,128]{3,2,1,0:T(8,128)S(1)}, f32[2,4,128,128]{3,2,1,0:T(8,128)S(1)}, u32[]{:S(2)}, u32[]{:S(2)}) collective-permute-start(f32[2,4,128,128]{3,2,1,0:T(8,128)S(1)} %get-tuple-element.22), channel_id=1, source_target_pairs={{1,2},{3,4},{5,6},{7,8},{9,10},{11,12},{13,14},{2,1},{4,3},{6,5},{... | collective-permute-start | bytes 1572872 | tf_op jit(solution)/shard_map/ppermute | solution.py:527
  16.2 8.2 %collective-permute-start.2 = (f32[2,4,128,128]{3,2,1,0:T(8,128)S(1)}, f32[2,4,128,128]{3,2,1,0:T(8,128)S(1)}, u32[]{:S(2)}, u32[]{:S(2)}) collective-permute-start(f32[2,4,128,128]{3,2,1,0:T(8,128)S(1)} %get-tuple-element.30), channel_id=1, source_target_pairs={{0,1},{1,0},{2,3},{3,2},{4,5},{5,4},{6,7},{7,6},{8,9},{9,8},{10,11... | collective-permute-start | bytes 1572872 | tf_op jit(solution)/shard_map/ppermute | solution.py:523
  16.3 10.5 %collective-permute-start.3 = (f32[2,4,128,128]{3,2,1,0:T(8,128)S(1)}, f32[2,4,128,128]{3,2,1,0:T(8,128)S(1)}, u32[]{:S(2)}, u32[]{:S(2)}) collective-permute-start(f32[2,4,128,128]{3,2,1,0:T(8,128)S(1)} %get-tuple-element.31), channel_id=1, source_target_pairs={{1,2},{3,4},{5,6},{7,8},{9,10},{11,12},{13,14},{2,1},{4,3},{6,5},{... | collective-permute-start | bytes 1572872 | tf_op jit(solution)/shard_map/ppermute | solution.py:527
  18.3 8.5 %copy-start = (s32[128,128]{1,0:T(8,128)S(1)}, s32[128,128]{1,0:T(8,128)}, u32[]{:S(2)}) copy-start(s32[128,128]{1,0:T(8,128)} %omega_y.1) | copy-start | bytes 196612
  18.4 8.5 %copy-start.1 = (bf16[256,128]{1,0:T(8,128)(2,1)S(1)}, bf16[256,128]{1,0:T(8,128)(2,1)}, u32[]{:S(2)}) copy-start(bf16[256,128]{1,0:T(8,128)(2,1)} %constant.8.clone.pool_hbm.pool) | copy-start | bytes 196612
  18.4 8.5 %copy-start.3 = (s32[16,128]{1,0:T(8,128)S(1)}, s32[16,128]{1,0:T(8,128)}, u32[]{:S(2)}) copy-start(s32[16,128]{1,0:T(8,128)} %omega_z.1) | copy-start | bytes 24580
  28.4 7.7 %copy-start.2 = (s32[128,128]{1,0:T(8,128)S(1)}, s32[128,128]{1,0:T(8,128)}, u32[]{:S(2)}) copy-start(s32[128,128]{1,0:T(8,128)} %omega_x.1) | copy-start | bytes 196612
  28.4 31.7 %all-to-all-start = ((f32[16,2,64,128]{3,2,1,0:T(8,128)}), f32[16,2,64,128]{3,2,1,0:T(8,128)S(1)}, u32[]{:S(2)}, u32[]{:S(2)}) async-start(f32[16,2,64,128]{3,2,1,0:T(8,128)} %get-tuple-element.33), calls=%async_computation | async-start | bytes 2097152 | tf_op jit(solution)/shard_map/all_to_all | solution.py:670
  36.2 3.2 %copy-start.4 = (f32[2,128]{1,0:T(2,128)}, f32[2,128]{1,0:T(2,128)S(1)}, u32[]{:S(2)}) copy-start(f32[2,128]{1,0:T(2,128)S(1)} %shard_map.171.sketch) | copy-start | bytes 3076
  39.6 33.6 %copy-start.5 = (f32[2,128]{1,0:T(2,128)S(1)}, f32[2,128]{1,0:T(2,128)}, u32[]{:S(2)}) copy-start(f32[2,128]{1,0:T(2,128)} %copy-done.4) | copy-start | bytes 3076

commit v5 on v4

--- a/solution.py
+++ b/solution.py
@@ -355,11 +355,11 @@
 
 
 def finish_kernel(
+    is_far,
     panels_before,
     edges,
     edge_gain,
-    near,
-    far,
+    halo,
     omega_z,
     omega_y,
     pool,
@@ -375,34 +375,32 @@
     cells_z = omega_z.shape[0]
     spread_y[...] = omega_y[...].astype(F32).astype(BF16)
     total[...] = before[...]
-    is_odd = odd_slab() == 1
     part = chunks.shape[2]
     pieces = chunks.shape[0] // (2 * REACH)
-    sends = []
-
-    def halo(shot, upper):
-        first, second = (far, near) if upper else (near, far)
-        return lambda at: jnp.where(is_odd, first[shot, at], second[shot, at])
-
     for upper in (False, True):
-        for layer in range(REACH):
-            index = layer + (REACH if upper else 0)
-            z = cells_z - REACH + layer if upper else layer
-            gradients = [
-                edges[shot, index]
-                + edge_gain[shot, index] * halo_terms(halo(shot, upper), layer, upper)
-                for shot in range(shots)
-            ]
-            weight_z = omega_z[z : z + 1, :].astype(F32)
-            emit(gradients, index, spread_y, weight_z, pool, chunks, total, lines)
-            span = pl.ds(index * pieces, pieces)
-            send = pltpu.make_async_copy(
-                chunks.at[span], panels.at[span, :, pl.ds(part, part)], sem.at[index]
-            )
-            send.start()
-            sends.append(send)
-    for send in sends:
-        send.wait()
+
+        @pl.when(odd_slab() == int(upper == is_far))
+        def _():
+            sends = []
+            for layer in range(REACH):
+                index = layer + (REACH if upper else 0)
+                z = cells_z - REACH + layer if upper else layer
+                gradients = [
+                    edges[shot, index]
+                    + edge_gain[shot, index]
+                    * halo_terms(lambda at: halo[shot, at], layer, upper)
+                    for shot in range(shots)
+                ]
+                weight_z = omega_z[z : z + 1, :].astype(F32)
+                emit(gradients, index, spread_y, weight_z, pool, chunks, total, lines)
+                span = pl.ds(index * pieces, pieces)
+                send = pltpu.make_async_copy(
+                    chunks.at[span], panels.at[span, :, pl.ds(part, part)], sem.at[layer]
+                )
+                send.start()
+                sends.append(send)
+            for send in sends:
+                send.wait()
 
 
 def sketch_kernel(total, omega_x, sketch):
@@ -639,26 +637,20 @@
         *pinned(forward_snaps, omega_z, omega_y, band_y, band_x, pool),
     )
 
-    panels, total = run(
-        finish_kernel,
-        [panel, spread],
-        in_specs=[hbm] + [vmem] * 8,
-        out_specs=[hbm, vmem],
-        scratch=scratch_emit + [pltpu.SemaphoreType.DMA((2 * REACH,))],
-        flops=5 * 10**8,
-        moved=5 * 2**20,
-        input_output_aliases={0: 0},
-    )(
-        panels,
-        edges,
-        edge_gain,
-        near,
-        far,
-        omega_z,
-        omega_y,
-        pool,
-        total_mid,
-    )
+    def finish(is_far, panels, halo, total):
+        return run(
+            functools.partial(finish_kernel, is_far),
+            [panel, spread],
+            in_specs=[hbm] + [vmem] * 7,
+            out_specs=[hbm, vmem],
+            scratch=scratch_emit + [pltpu.SemaphoreType.DMA((REACH,))],
+            flops=3 * 10**8,
+            moved=3 * 2**20,
+            input_output_aliases={0: 0},
+        )(panels, edges, edge_gain, halo, omega_z, omega_y, pool, total)
+
+    panels, total = finish(False, panels, near, total_mid)
+    panels, total = finish(True, panels, far, total)
     sketch_part = run(
         sketch_kernel,
         shape((shots, rank), F32),

time: 94.7 us -> 94 us (level)
  blocking collectives: 32.5 us -> 30.7 us
    all_to_all x1, waiting for transfers between devices: 19.3 us -> 20.8 us  [local(): got = lax.all_to_all(panels, 'shot', 0, 0, tiled=True)]
    all_to_all x1, blocking collectives: 20.3 us -> 19 us  [local(): terms = lax.all_to_all(terms, 'slab', 0, 0, tiled=True)]
    ppermute x2, waiting for transfers between devices: 4.39 us -> 3.3 us  [with_far(): return lax.ppermute(layers, 'slab', pairs + [(j, i) for i, j in pairs])]
    pallas_call x1 -> x2, Pallas kernels: 1.55 us -> 2.12 us  [finish(): run(functools.partial(finish_kernel, is_far), [panel, spread], in_specs=[...]
  transfers between devices with their start and end apart: 5 -> 5, of which waited for: 3 -> 3; matrix products, arithmetic and copies ran while one was open for 5% -> 5% of each run, Pallas kernels for 13% -> 15%
where the time goes in v5:
time: 94 us; the launch traced here: 93.6 us
  blocking collectives  30.7 us (33%)
  waiting for transfers between devices  24.1 us (26%)
  Pallas kernels  18.2 us (19%)
  starting transfers between devices  15.1 us (16%)
  local copies, waits for them, and re-layouts  3.46 us (4%)
  other arithmetic  1.14 us (1%)
    all_to_all x1, waiting for transfers between devices, local(): got = lax.all_to_all(panels, 'shot', 0, 0, tiled=True)  20.8 us
    all_to_all x1, blocking collectives, local(): terms = lax.all_to_all(terms, 'slab', 0, 0, tiled=True)  19 us
    all_to_all x1, blocking collectives, local(): lax.all_to_all(gram.reshape(groups, shots, cells_y), 'shot', 0, 0, tiled=...  11.7 us
    all_to_all x1, starting transfers between devices, local(): got = lax.all_to_all(panels, 'shot', 0, 0, tiled=True)  7.75 us
    pallas_call x1, Pallas kernels, local(): run(functools.partial(begin_kernel, total_z, blocks), [field, field, gain...  6.58 us
    pallas_call x1, Pallas kernels, local(): run(functools.partial(middle_kernel, blocks), [panel, both, both, spread]...  6 us
    ppermute x2, starting transfers between devices, with_far(): return lax.ppermute(layers, 'slab', pairs + [(j, i) for i, j in pairs])  3.92 us
    ppermute x2, starting transfers between devices, with_near(): return lax.ppermute(layers, 'slab', [(i, i ^ 1) for i in range(slabs)])  3.42 us
  transfers between devices with their start and end apart: 5, of which 3 were waited for; matrix products, arithmetic and copies ran while one was open for 5% of the time, Pallas kernels for 15%

profile of v5, /device:TPU:1, one launch (start us, length us, event | category | flops | bytes accessed | tf_op | source)
XLA Modules:
  0.0 93.6 jit_solution(2979336280317932905)
XLA Ops:
  0.6 1.2 %shard_map.167 = (f32[2,4,128,128]{3,2,1,0:T(8,128)S(1)}, f32[2,4,128,128]{3,2,1,0:T(8,128)S(1)}) custom-call(f32[2,16,128,128]{3,2,1,0:T(8,128)} %curr.1), custom_call_target="tpu_custom_call" | custom-call | bytes 2097152 | tf_op jit(solution)/shard_map/pallas_call | solution.py:537
  1.9 3.3 %collective-permute-start = (f32[2,4,128,128]{3,2,1,0:T(8,128)S(1)}, f32[2,4,128,128]{3,2,1,0:T(8,128)S(1)}, u32[]{:S(2)}, u32[]{:S(2)}) collective-permute-start(f32[2,4,128,128]{3,2,1,0:T(8,128)S(1)} %get-tuple-element.23), channel_id=1, source_target_pairs={{0,1},{1,0},{2,3},{3,2},{4,5},{5,4},{6,7},{7,6},{8,9},{9,8},{10,11... | collective-permute-start | bytes 1572872 | tf_op jit(solution)/shard_map/ppermute | solution.py:521
  5.2 1.9 %collective-permute-start.1 = (f32[2,4,128,128]{3,2,1,0:T(8,128)S(1)}, f32[2,4,128,128]{3,2,1,0:T(8,128)S(1)}, u32[]{:S(2)}, u32[]{:S(2)}) collective-permute-start(f32[2,4,128,128]{3,2,1,0:T(8,128)S(1)} %get-tuple-element.24), channel_id=1, source_target_pairs={{1,2},{3,4},{5,6},{7,8},{9,10},{11,12},{13,14},{2,1},{4,3},{6,5},{... | collective-permute-start | bytes 1572872 | tf_op jit(solution)/shard_map/ppermute | solution.py:525
  7.1 6.6 %shard_map.166 = (f32[2,16,128,128]{3,2,1,0:T(8,128)S(1)}, f32[2,16,128,128]{3,2,1,0:T(8,128)S(1)}, f32[16,128,128]{2,1,0:T(8,128)S(1)}, f32[16,128,128]{2,1,0:T(8,128)S(1)}) custom-call(s32[3]{0:T(128)S(1)} %copy-done.6, f32[2,16,128,128]{3,2,1,0:T(8,128)} %curr.1, f32[16,128,128]{2,1,0:T(8,128)} %courant_hbm.1, f32[2,16,128,128]{3,2,1,0:T(8,128)} %prev_hbm.1, ...), custom_call_target="tpu_custom_call" | custom-call | flops 2000000000 | bytes 11534336 | tf_op jit(solution)/shard_map/pallas_call | solution.py:547
  13.7 0.0 collective-permute-done.near
  13.7 2.0 %collective-permute-done.1.far = f32[2,4,128,128]{3,2,1,0:T(8,128)S(1)} collective-permute-done((f32[2,4,128,128]{3,2,1,0:T(8,128)S(1)}, f32[2,4,128,128]{3,2,1,0:T(8,128)S(1)}, u32[]{:S(2)}, u32[]{:S(2)}) %collective-permute-start.1) | collective-permute-done | bytes 524320 | tf_op jit(solution)/shard_map/ppermute | solution.py:525
  15.7 0.5 shard_map.168
  16.2 0.1 collective-permute-start.2
  16.3 2.0 %collective-permute-start.3 = (f32[2,4,128,128]{3,2,1,0:T(8,128)S(1)}, f32[2,4,128,128]{3,2,1,0:T(8,128)S(1)}, u32[]{:S(2)}, u32[]{:S(2)}) collective-permute-start(f32[2,4,128,128]{3,2,1,0:T(8,128)S(1)} %get-tuple-element.35), channel_id=1, source_target_pairs={{1,2},{3,4},{5,6},{7,8},{9,10},{11,12},{13,14},{2,1},{4,3},{6,5},{... | collective-permute-start | bytes 1572872 | tf_op jit(solution)/shard_map/ppermute | solution.py:525
  18.3 0.0 copy-start
  18.4 0.0 copy-start.1
  18.4 0.0 copy-start.2
  18.4 6.0 %shard_map.169 = (f32[16,2,64,128]{3,2,1,0:T(8,128)}, f32[2,8,128,128]{3,2,1,0:T(8,128)S(1)}, f32[2,8,128,128]{3,2,1,0:T(8,128)S(1)}, f32[2,128,128]{2,1,0:T(8,128)S(1)}) custom-call(f32[2,16,128,128]{3,2,1,0:T(8,128)S(1)} %get-tuple-element.26.wave, f32[2,16,128,128]{3,2,1,0:T(8,128)S(1)} %get-tuple-element.27.rest, ...), custom_call_target="tpu_custom_call" | custom-call | flops 2000000000 | bytes 11534336 | tf_op jit(solution)/shard_map/pallas_call | solution.py:615
  24.4 0.0 collective-permute-done.2.halo
  24.4 0.0 copy-done
  24.4 0.0 copy-done.1
  24.4 1.1 %shard_map.170 = (f32[16,2,64,128]{3,2,1,0:T(8,128)}, f32[2,128,128]{2,1,0:T(8,128)S(1)}) custom-call(f32[16,2,64,128]{3,2,1,0:T(8,128)} %get-tuple-element.29.panels_before, f32[2,8,128,128]{3,2,1,0:T(8,128)S(1)} %get-tuple-element.30.edges, f32[2,8,128,128]{3,2,1,0:T(8,128)S(1)} %get-tuple-element.31.edge_gain, ...), custom_call_target="tpu_custom_call", output_to_operand_aliasing={{0}: (0, {})} | custom-call | flops 300000000 | bytes 3145728 | tf_op jit(solution)/shard_map/pallas_call | solution.py:641
  25.5 1.3 %collective-permute-done.3.halo = f32[2,4,128,128]{3,2,1,0:T(8,128)S(1)} collective-permute-done((f32[2,4,128,128]{3,2,1,0:T(8,128)S(1)}, f32[2,4,128,128]{3,2,1,0:T(8,128)S(1)}, u32[]{:S(2)}, u32[]{:S(2)}) %collective-permute-start.3) | collective-permute-done | bytes 524320 | tf_op jit(solution)/shard_map/ppermute | solution.py:525
  26.8 1.1 %shard_map.171 = (f32[16,2,64,128]{3,2,1,0:T(8,128)}, f32[2,128,128]{2,1,0:T(8,128)S(1)}) custom-call(f32[16,2,64,128]{3,2,1,0:T(8,128)} %get-tuple-element.34.panels_before, f32[2,8,128,128]{3,2,1,0:T(8,128)S(1)} %get-tuple-element.30.edges, f32[2,8,128,128]{3,2,1,0:T(8,128)S(1)} %get-tuple-element.31.edge_gain, ...), custom_call_target="tpu_custom_call", output_to_operand_aliasing={{0}: (0, {})} | custom-call | flops 300000000 | bytes 3145728 | tf_op jit(solution)/shard_map/pallas_call | solution.py:641
  27.9 7.7 %all-to-all-start = ((f32[16,2,64,128]{3,2,1,0:T(8,128)}), f32[16,2,64,128]{3,2,1,0:T(8,128)S(1)}, u32[]{:S(2)}, u32[]{:S(2)}) async-start(f32[16,2,64,128]{3,2,1,0:T(8,128)} %get-tuple-element.37), calls=%async_computation | async-start | bytes 2097152 | tf_op jit(solution)/shard_map/all_to_all | solution.py:662
  35.7 0.0 copy-start.4
  35.7 1.8 %copy.25 = f32[8,2,2,2,32,128]{5,0,4,1,2,3:T(8,128)S(1)} copy(f32[8,2,2,2,32,128]{5,4,3,2,1,0:T(8,128)} %bitcast.1) | data formatting | bytes 2097152 | tf_op jit(solution)/shard_map/reshape | solution.py:664
  37.6 1.3 %copy.22 = f32[2,2,8,2,32,128]{5,4,3,2,1,0:T(8,128)S(1)} copy(f32[2,2,8,2,32,128]{5,4,0,1,3,2:T(8,128)} %bitcast.3) | data formatting | bytes 2097152 | tf_op jit(solution)/shard_map/transpose | solution.py:665
  39.0 0.1 concatenate.10
  39.1 0.1 concatenate.12
  39.2 0.0 copy-start.5
  39.2 1.1 %pad_maximum_fusion.coarse = f32[2,16,8192]{2,1,0:T(8,128)} fusion(f32[2,4,8192]{2,1,0:T(4,128)S(1)} %concatenate.12, f32[2,8,8192]{2,1,0:T(8,128)S(1)} %bitcast.19, f32[2,4,8192]{2,1,0:T(4,128)S(1)} %concatenate.10), kind=kLoop, calls=%fused_computation | loop fusion | flops 524288 | bytes 2097152 | tf_op jit(solution)/shard_map/concatenate | solution.py:666
  40.3 20.8 %all-to-all-done = f32[16,2,64,128]{3,2,1,0:T(8,128)S(1)} async-done(((f32[16,2,64,128]{3,2,1,0:T(8,128)}), f32[16,2,64,128]{3,2,1,0:T(8,128)S(1)}, u32[]{:S(2)}, u32[]{:S(2)}) %all-to-all-start) | async-done | bytes 1048608 | tf_op jit(solution)/shard_map/all_to_all | solution.py:662
  61.2 1.0 %shard_map.173 = f32[32,128]{1,0:T(8,128)S(1)} custom-call(f32[2048,128]{1,0:T(8,128)S(1)} %bitcast.15, f32[2,16,8192]{2,1,0:T(8,128)} %pad_maximum_fusion.coarse, f32[2,128]{1,0:T(2,128)} %copy-done.4), custom_call_target="tpu_custom_call" | custom-call | flops 100000000 | bytes 1048576 | tf_op jit(solution)/shard_map/pallas_call | solution.py:671
  62.2 11.7 %all_to_all.15.mine = f32[16,2,128]{2,1,0:T(2,128)S(1)} all-to-all(f32[16,2,128]{2,1,0:T(2,128)S(1)} %bitcast.16), channel_id=1, replica_groups=mesh['shot'=16,'slab'=16] {'shot'}, dimensions={0} | all-to-all | bytes 32768 | tf_op jit(solution)/shard_map/all_to_all | solution.py:679
  73.9 19.0 %all_to_all.16.terms = f32[16,4,128]{2,1,0:T(4,128)S(1)} all-to-all(f32[16,4,128]{2,1,0:T(4,128)S(1)} %shard_map.174), channel_id=1, replica_groups=mesh['shot'=16,'slab'=16] {'slab'}, dimensions={0} | all-to-all | bytes 65536 | tf_op jit(solution)/shard_map/all_to_all | solution.py:687
  92.9 0.7 shard_map.175
  (11 shorter events, 0.1 us)
Async XLA Ops:
  0.6 6.5 %copy-start.6 = (s32[3]{0:T(128)S(1)}, s32[3]{0:T(128)}, u32[]{:S(2)}) copy-start(s32[3]{0:T(128)} %pml.1) | copy-start | bytes 40
  1.9 11.8 %collective-permute-start = (f32[2,4,128,128]{3,2,1,0:T(8,128)S(1)}, f32[2,4,128,128]{3,2,1,0:T(8,128)S(1)}, u32[]{:S(2)}, u32[]{:S(2)}) collective-permute-start(f32[2,4,128,128]{3,2,1,0:T(8,128)S(1)} %get-tuple-element.23), channel_id=1, source_target_pairs={{0,1},{1,0},{2,3},{3,2},{4,5},{5,4},{6,7},{7,6},{8,9},{9,8},{10,11... | collective-permute-start | bytes 1572872 | tf_op jit(solution)/shard_map/ppermute | solution.py:521
  5.2 10.5 %collective-permute-start.1 = (f32[2,4,128,128]{3,2,1,0:T(8,128)S(1)}, f32[2,4,128,128]{3,2,1,0:T(8,128)S(1)}, u32[]{:S(2)}, u32[]{:S(2)}) collective-permute-start(f32[2,4,128,128]{3,2,1,0:T(8,128)S(1)} %get-tuple-element.24), channel_id=1, source_target_pairs={{1,2},{3,4},{5,6},{7,8},{9,10},{11,12},{13,14},{2,1},{4,3},{6,5},{... | collective-permute-start | bytes 1572872 | tf_op jit(solution)/shard_map/ppermute | solution.py:525
  16.2 8.2 %collective-permute-start.2 = (f32[2,4,128,128]{3,2,1,0:T(8,128)S(1)}, f32[2,4,128,128]{3,2,1,0:T(8,128)S(1)}, u32[]{:S(2)}, u32[]{:S(2)}) collective-permute-start(f32[2,4,128,128]{3,2,1,0:T(8,128)S(1)} %get-tuple-element.32), channel_id=1, source_target_pairs={{0,1},{1,0},{2,3},{3,2},{4,5},{5,4},{6,7},{7,6},{8,9},{9,8},{10,11... | collective-permute-start | bytes 1572872 | tf_op jit(solution)/shard_map/ppermute | solution.py:521
  16.3 10.5 %collective-permute-start.3 = (f32[2,4,128,128]{3,2,1,0:T(8,128)S(1)}, f32[2,4,128,128]{3,2,1,0:T(8,128)S(1)}, u32[]{:S(2)}, u32[]{:S(2)}) collective-permute-start(f32[2,4,128,128]{3,2,1,0:T(8,128)S(1)} %get-tuple-element.35), channel_id=1, source_target_pairs={{1,2},{3,4},{5,6},{7,8},{9,10},{11,12},{13,14},{2,1},{4,3},{6,5},{... | collective-permute-start | bytes 1572872 | tf_op jit(solution)/shard_map/ppermute | solution.py:525
  18.3 6.1 %copy-start = (s32[128,128]{1,0:T(8,128)S(1)}, s32[128,128]{1,0:T(8,128)}, u32[]{:S(2)}) copy-start(s32[128,128]{1,0:T(8,128)} %omega_y.3) | copy-start | bytes 196612
  18.4 6.1 %copy-start.1 = (bf16[256,128]{1,0:T(8,128)(2,1)S(1)}, bf16[256,128]{1,0:T(8,128)(2,1)}, u32[]{:S(2)}) copy-start(bf16[256,128]{1,0:T(8,128)(2,1)} %constant.8.clone.pool_hbm.pool) | copy-start | bytes 196612
  18.4 6.0 %copy-start.2 = (s32[16,128]{1,0:T(8,128)S(1)}, s32[16,128]{1,0:T(8,128)}, u32[]{:S(2)}) copy-start(s32[16,128]{1,0:T(8,128)} %omega_z.3) | copy-start | bytes 24580
  26.8 8.8 %copy-start.3 = (s32[128,128]{1,0:T(8,128)S(1)}, s32[128,128]{1,0:T(8,128)}, u32[]{:S(2)}) copy-start(s32[128,128]{1,0:T(8,128)} %omega_x.1) | copy-start | bytes 196612
  27.9 33.3 %all-to-all-start = ((f32[16,2,64,128]{3,2,1,0:T(8,128)}), f32[16,2,64,128]{3,2,1,0:T(8,128)S(1)}, u32[]{:S(2)}, u32[]{:S(2)}) async-start(f32[16,2,64,128]{3,2,1,0:T(8,128)} %get-tuple-element.37), calls=%async_computation | async-start | bytes 2097152 | tf_op jit(solution)/shard_map/all_to_all | solution.py:662
  35.7 3.2 %copy-start.4 = (f32[2,128]{1,0:T(2,128)}, f32[2,128]{1,0:T(2,128)S(1)}, u32[]{:S(2)}) copy-start(f32[2,128]{1,0:T(2,128)S(1)} %shard_map.172.sketch) | copy-start | bytes 3076
  39.2 34.7 %copy-start.5 = (f32[2,128]{1,0:T(2,128)S(1)}, f32[2,128]{1,0:T(2,128)}, u32[]{:S(2)}) copy-start(f32[2,128]{1,0:T(2,128)} %copy-done.4) | copy-start | bytes 3076

commit v6 on v5

--- a/solution.py
+++ b/solution.py
@@ -228,24 +228,18 @@
     return total
 
 
-def edge_kernel(partial, near, far, gain_lap, whole, near_out, far_out):
-    odd = odd_slab()
-    step = pl.program_id(0)
+def edge_kernel(side, partial, halo, gain_lap, whole, out):
     for upper in (False, True):
-        for halo, out, parity in (
-            (near, near_out, 0 if upper else 1),
-            (far, far_out, 1 if upper else 0),
-        ):
-
-            @pl.when((step == int(upper)) & (odd == parity))
-            def _():
-                @pl.loop(0, partial.shape[0])
-                def _(shot):
-                    for layer in range(REACH):
-                        terms = halo_terms(lambda at: halo[shot, at], layer, upper)
-                        value = partial[shot, layer] + gain_lap[layer] * terms
-                        whole[shot, layer] = value
-                        out[shot, layer] = value
+
+        @pl.when(side[0] == int(upper))
+        def _():
+            @pl.loop(0, partial.shape[0])
+            def _(shot):
+                for layer in range(REACH):
+                    terms = halo_terms(lambda at: halo[shot, at], layer, upper)
+                    value = partial[shot, layer] + gain_lap[layer] * terms
+                    whole[shot, layer] = value
+                    out[shot, layer] = value
 
 
 def emit(gradients, layer, spread_y, weight_z, pool, chunks, total, lines):
@@ -584,23 +578,33 @@
     layers4 = (shots, REACH) + plane
     gains4 = (REACH,) + plane
 
-    whole4 = spec(layers4, (0, 0, 0, 0))
-    wave4 = pl.BlockSpec(layers4, lambda step: (0, step * (blocks - 1), 0, 0))
-    wave, near, far = run(
-        edge_kernel,
-        [field, edge, edge],
-        in_specs=[
-            wave4,
-            whole4,
-            whole4,
-            pl.BlockSpec(gains4, lambda step: (step * (blocks - 1), 0, 0)),
-        ],
-        out_specs=[wave4, whole4, whole4],
-        grid=(2,),
-        flops=10**7,
-        moved=2 * 2**20,
-        input_output_aliases={0: 0},
-    )(updated, near, far, gain_lap)
+    whole4 = pl.BlockSpec(layers4, lambda step, side: (0, 0, 0, 0))
+    wave4 = pl.BlockSpec(layers4, lambda step, side: (0, side[0] * (blocks - 1), 0, 0))
+
+    def complete(side, wave, halo):
+        return pl.pallas_call(
+            edge_kernel,
+            out_shape=[field, edge],
+            grid_spec=pltpu.PrefetchScalarGridSpec(
+                num_scalar_prefetch=1,
+                grid=(1,),
+                in_specs=[
+                    wave4,
+                    whole4,
+                    pl.BlockSpec(gains4, lambda step, side: (side[0] * (blocks - 1), 0, 0)),
+                ],
+                out_specs=[wave4, whole4],
+            ),
+            compiler_params=pltpu.CompilerParams(vmem_limit_bytes=VMEM_BYTES),
+            cost_estimate=pl.CostEstimate(
+                flops=10**7, bytes_accessed=2 * 2**20, transcendentals=0
+            ),
+            input_output_aliases={1: 0},
+        )(side, wave, halo, gain_lap)
+
+    side = jnp.remainder(lax.axis_index("slab"), 2).astype(jnp.int32).reshape(1)
+    wave, near = complete(1 - side, updated, near)
+    wave, far = complete(side, wave, far)
     far = with_far(far)
     near = with_near(near)
 

time: 94 us -> 91.7 us (0.976)
  waiting for transfers between devices: 24.1 us -> 22.9 us
    all_to_all x1, blocking collectives: 19 us -> 17.6 us  [local(): terms = lax.all_to_all(terms, 'slab', 0, 0, tiled=True)]
where the time goes in v6:
time: 91.7 us; the launch traced here: 91.3 us
  blocking collectives  29.8 us (32%)
  waiting for transfers between devices  22.9 us (25%)
  Pallas kernels  18.1 us (20%)
  starting transfers between devices  15 us (16%)
  local copies, waits for them, and re-layouts  3.46 us (4%)
  other arithmetic  1.14 us (1%)
    all_to_all x1, waiting for transfers between devices, local(): got = lax.all_to_all(panels, 'shot', 0, 0, tiled=True)  20 us
    all_to_all x1, blocking collectives, local(): terms = lax.all_to_all(terms, 'slab', 0, 0, tiled=True)  17.6 us
    all_to_all x1, blocking collectives, local(): lax.all_to_all(gram.reshape(groups, shots, cells_y), 'shot', 0, 0, tiled=...  12.2 us
    all_to_all x1, starting transfers between devices, local(): got = lax.all_to_all(panels, 'shot', 0, 0, tiled=True)  7.58 us
    pallas_call x1, Pallas kernels, local(): run(functools.partial(begin_kernel, total_z, blocks), [field, field, gain...  6.59 us
    pallas_call x1, Pallas kernels, local(): run(functools.partial(middle_kernel, blocks), [panel, both, both, spread]...  6 us
    ppermute x2, starting transfers between devices, with_far(): return lax.ppermute(layers, 'slab', pairs + [(j, i) for i, j in pairs])  3.96 us
    ppermute x2, starting transfers between devices, with_near(): return lax.ppermute(layers, 'slab', [(i, i ^ 1) for i in range(slabs)])  3.42 us
  transfers between devices with their start and end apart: 5, of which 3 were waited for; matrix products, arithmetic and copies ran while one was open for 5% of the time, Pallas kernels for 15%

profile of v6, /device:TPU:1, one launch (start us, length us, event | category | flops | bytes accessed | tf_op | source)
XLA Modules:
  0.0 91.3 jit_solution(9253925221531532387)
XLA Ops:
  0.6 1.2 %shard_map.167 = (f32[2,4,128,128]{3,2,1,0:T(8,128)S(1)}, f32[2,4,128,128]{3,2,1,0:T(8,128)S(1)}) custom-call(f32[2,16,128,128]{3,2,1,0:T(8,128)} %curr.1), custom_call_target="tpu_custom_call" | custom-call | bytes 2097152 | tf_op jit(solution)/shard_map/pallas_call | solution.py:531
  1.9 3.3 %collective-permute-start = (f32[2,4,128,128]{3,2,1,0:T(8,128)S(1)}, f32[2,4,128,128]{3,2,1,0:T(8,128)S(1)}, u32[]{:S(2)}, u32[]{:S(2)}) collective-permute-start(f32[2,4,128,128]{3,2,1,0:T(8,128)S(1)} %get-tuple-element.24), channel_id=1, source_target_pairs={{0,1},{1,0},{2,3},{3,2},{4,5},{5,4},{6,7},{7,6},{8,9},{9,8},{10,11... | collective-permute-start | bytes 1572872 | tf_op jit(solution)/shard_map/ppermute | solution.py:515
  5.2 1.9 %collective-permute-start.1 = (f32[2,4,128,128]{3,2,1,0:T(8,128)S(1)}, f32[2,4,128,128]{3,2,1,0:T(8,128)S(1)}, u32[]{:S(2)}, u32[]{:S(2)}) collective-permute-start(f32[2,4,128,128]{3,2,1,0:T(8,128)S(1)} %get-tuple-element.27), channel_id=1, source_target_pairs={{1,2},{3,4},{5,6},{7,8},{9,10},{11,12},{13,14},{2,1},{4,3},{6,5},{... | collective-permute-start | bytes 1572872 | tf_op jit(solution)/shard_map/ppermute | solution.py:519
  7.1 0.0 copy-done.6
  7.1 6.6 %shard_map.166 = (f32[2,16,128,128]{3,2,1,0:T(8,128)S(1)}, f32[2,16,128,128]{3,2,1,0:T(8,128)S(1)}, f32[16,128,128]{2,1,0:T(8,128)S(1)}, f32[16,128,128]{2,1,0:T(8,128)S(1)}) custom-call(s32[3]{0:T(128)S(1)} %copy-done.6, f32[2,16,128,128]{3,2,1,0:T(8,128)} %curr.1, f32[16,128,128]{2,1,0:T(8,128)} %courant_hbm.1, f32[2,16,128,128]{3,2,1,0:T(8,128)} %prev_hbm.1, ...), custom_call_target="tpu_custom_call" | custom-call | flops 2000000000 | bytes 11534336 | tf_op jit(solution)/shard_map/pallas_call | solution.py:541
  13.7 0.0 collective-permute-done.halo
  13.7 0.2 shard_map.168
  14.0 0.1 collective-permute-start.2
  14.1 1.6 %collective-permute-done.1.halo = f32[2,4,128,128]{3,2,1,0:T(8,128)S(1)} collective-permute-done((f32[2,4,128,128]{3,2,1,0:T(8,128)S(1)}, f32[2,4,128,128]{3,2,1,0:T(8,128)S(1)}, u32[]{:S(2)}, u32[]{:S(2)}) %collective-permute-start.1) | collective-permute-done | bytes 524320 | tf_op jit(solution)/shard_map/ppermute | solution.py:519
  15.7 0.2 shard_map.169
  15.9 2.1 %collective-permute-start.3 = (f32[2,4,128,128]{3,2,1,0:T(8,128)S(1)}, f32[2,4,128,128]{3,2,1,0:T(8,128)S(1)}, u32[]{:S(2)}, u32[]{:S(2)}) collective-permute-start(f32[2,4,128,128]{3,2,1,0:T(8,128)S(1)} %get-tuple-element.37), channel_id=1, source_target_pairs={{1,2},{3,4},{5,6},{7,8},{9,10},{11,12},{13,14},{2,1},{4,3},{6,5},{... | collective-permute-start | bytes 1572872 | tf_op jit(solution)/shard_map/ppermute | solution.py:519
  18.0 0.0 copy-start
  18.0 0.0 copy-start.1
  18.0 0.0 copy-start.2
  18.0 6.0 %shard_map.170 = (f32[16,2,64,128]{3,2,1,0:T(8,128)}, f32[2,8,128,128]{3,2,1,0:T(8,128)S(1)}, f32[2,8,128,128]{3,2,1,0:T(8,128)S(1)}, f32[2,128,128]{2,1,0:T(8,128)S(1)}) custom-call(f32[2,16,128,128]{3,2,1,0:T(8,128)S(1)} %get-tuple-element.28.wave, f32[2,16,128,128]{3,2,1,0:T(8,128)S(1)} %get-tuple-element.29.rest, ...), custom_call_target="tpu_custom_call" | custom-call | flops 2000000000 | bytes 11534336 | tf_op jit(solution)/shard_map/pallas_call | solution.py:619
  24.0 0.0 collective-permute-done.2.halo
  24.1 1.1 %shard_map.171 = (f32[16,2,64,128]{3,2,1,0:T(8,128)}, f32[2,128,128]{2,1,0:T(8,128)S(1)}) custom-call(f32[16,2,64,128]{3,2,1,0:T(8,128)} %get-tuple-element.31.panels_before, f32[2,8,128,128]{3,2,1,0:T(8,128)S(1)} %get-tuple-element.32.edges, f32[2,8,128,128]{3,2,1,0:T(8,128)S(1)} %get-tuple-element.33.edge_gain, ...), custom_call_target="tpu_custom_call", output_to_operand_aliasing={{0}: (0, {})} | custom-call | flops 300000000 | bytes 3145728 | tf_op jit(solution)/shard_map/pallas_call | solution.py:645
  25.1 1.3 %collective-permute-done.3.halo = f32[2,4,128,128]{3,2,1,0:T(8,128)S(1)} collective-permute-done((f32[2,4,128,128]{3,2,1,0:T(8,128)S(1)}, f32[2,4,128,128]{3,2,1,0:T(8,128)S(1)}, u32[]{:S(2)}, u32[]{:S(2)}) %collective-permute-start.3) | collective-permute-done | bytes 524320 | tf_op jit(solution)/shard_map/ppermute | solution.py:519
  26.4 1.1 %shard_map.172 = (f32[16,2,64,128]{3,2,1,0:T(8,128)}, f32[2,128,128]{2,1,0:T(8,128)S(1)}) custom-call(f32[16,2,64,128]{3,2,1,0:T(8,128)} %get-tuple-element.36.panels_before, f32[2,8,128,128]{3,2,1,0:T(8,128)S(1)} %get-tuple-element.32.edges, f32[2,8,128,128]{3,2,1,0:T(8,128)S(1)} %get-tuple-element.33.edge_gain, ...), custom_call_target="tpu_custom_call", output_to_operand_aliasing={{0}: (0, {})} | custom-call | flops 300000000 | bytes 3145728 | tf_op jit(solution)/shard_map/pallas_call | solution.py:645
  27.5 7.6 %all-to-all-start = ((f32[16,2,64,128]{3,2,1,0:T(8,128)}), f32[16,2,64,128]{3,2,1,0:T(8,128)S(1)}, u32[]{:S(2)}, u32[]{:S(2)}) async-start(f32[16,2,64,128]{3,2,1,0:T(8,128)} %get-tuple-element.39), calls=%async_computation | async-start | bytes 2097152 | tf_op jit(solution)/shard_map/all_to_all | solution.py:666
  35.1 0.0 copy-start.4
  35.1 1.8 %copy.26 = f32[8,2,2,2,32,128]{5,0,4,1,2,3:T(8,128)S(1)} copy(f32[8,2,2,2,32,128]{5,4,3,2,1,0:T(8,128)} %bitcast.2) | data formatting | bytes 2097152 | tf_op jit(solution)/shard_map/reshape | solution.py:668
  37.0 1.3 %copy.23 = f32[2,2,8,2,32,128]{5,4,3,2,1,0:T(8,128)S(1)} copy(f32[2,2,8,2,32,128]{5,4,0,1,3,2:T(8,128)} %bitcast.4) | data formatting | bytes 2097152 | tf_op jit(solution)/shard_map/transpose | solution.py:669
  38.4 0.1 concatenate.10
  38.5 0.1 concatenate.12
  38.6 0.0 copy-start.5
  38.6 1.1 %pad_maximum_fusion.coarse = f32[2,16,8192]{2,1,0:T(8,128)} fusion(f32[2,4,8192]{2,1,0:T(4,128)S(1)} %concatenate.12, f32[2,8,8192]{2,1,0:T(8,128)S(1)} %bitcast.20, f32[2,4,8192]{2,1,0:T(4,128)S(1)} %concatenate.10), kind=kLoop, calls=%fused_computation | loop fusion | flops 524288 | bytes 2097152 | tf_op jit(solution)/shard_map/concatenate | solution.py:670
  39.8 20.0 %all-to-all-done = f32[16,2,64,128]{3,2,1,0:T(8,128)S(1)} async-done(((f32[16,2,64,128]{3,2,1,0:T(8,128)}), f32[16,2,64,128]{3,2,1,0:T(8,128)S(1)}, u32[]{:S(2)}, u32[]{:S(2)}) %all-to-all-start) | async-done | bytes 1048608 | tf_op jit(solution)/shard_map/all_to_all | solution.py:666
  59.8 1.0 %shard_map.174 = f32[32,128]{1,0:T(8,128)S(1)} custom-call(f32[2048,128]{1,0:T(8,128)S(1)} %bitcast.16, f32[2,16,8192]{2,1,0:T(8,128)} %pad_maximum_fusion.coarse, f32[2,128]{1,0:T(2,128)} %copy-done.4), custom_call_target="tpu_custom_call" | custom-call | flops 100000000 | bytes 1048576 | tf_op jit(solution)/shard_map/pallas_call | solution.py:675
  60.8 12.2 %all_to_all.15.mine = f32[16,2,128]{2,1,0:T(2,128)S(1)} all-to-all(f32[16,2,128]{2,1,0:T(2,128)S(1)} %bitcast.17), channel_id=1, replica_groups=mesh['shot'=16,'slab'=16] {'shot'}, dimensions={0} | all-to-all | bytes 32768 | tf_op jit(solution)/shard_map/all_to_all | solution.py:683
  73.0 17.6 %all_to_all.16.terms = f32[16,4,128]{2,1,0:T(4,128)S(1)} all-to-all(f32[16,4,128]{2,1,0:T(4,128)S(1)} %shard_map.175), channel_id=1, replica_groups=mesh['shot'=16,'slab'=16] {'slab'}, dimensions={0} | all-to-all | bytes 65536 | tf_op jit(solution)/shard_map/all_to_all | solution.py:691
  90.6 0.7 shard_map.176
  (12 shorter events, 0.1 us)
Async XLA Ops:
  0.6 6.5 %copy-start.6 = (s32[3]{0:T(128)S(1)}, s32[3]{0:T(128)}, u32[]{:S(2)}) copy-start(s32[3]{0:T(128)} %pml.1) | copy-start | bytes 40
  1.9 11.9 %collective-permute-start = (f32[2,4,128,128]{3,2,1,0:T(8,128)S(1)}, f32[2,4,128,128]{3,2,1,0:T(8,128)S(1)}, u32[]{:S(2)}, u32[]{:S(2)}) collective-permute-start(f32[2,4,128,128]{3,2,1,0:T(8,128)S(1)} %get-tuple-element.24), channel_id=1, source_target_pairs={{0,1},{1,0},{2,3},{3,2},{4,5},{5,4},{6,7},{7,6},{8,9},{9,8},{10,11... | collective-permute-start | bytes 1572872 | tf_op jit(solution)/shard_map/ppermute | solution.py:515
  5.2 10.5 %collective-permute-start.1 = (f32[2,4,128,128]{3,2,1,0:T(8,128)S(1)}, f32[2,4,128,128]{3,2,1,0:T(8,128)S(1)}, u32[]{:S(2)}, u32[]{:S(2)}) collective-permute-start(f32[2,4,128,128]{3,2,1,0:T(8,128)S(1)} %get-tuple-element.27), channel_id=1, source_target_pairs={{1,2},{3,4},{5,6},{7,8},{9,10},{11,12},{13,14},{2,1},{4,3},{6,5},{... | collective-permute-start | bytes 1572872 | tf_op jit(solution)/shard_map/ppermute | solution.py:519
  14.0 10.0 %collective-permute-start.2 = (f32[2,4,128,128]{3,2,1,0:T(8,128)S(1)}, f32[2,4,128,128]{3,2,1,0:T(8,128)S(1)}, u32[]{:S(2)}, u32[]{:S(2)}) collective-permute-start(f32[2,4,128,128]{3,2,1,0:T(8,128)S(1)} %get-tuple-element.34), channel_id=1, source_target_pairs={{0,1},{1,0},{2,3},{3,2},{4,5},{5,4},{6,7},{7,6},{8,9},{9,8},{10,11... | collective-permute-start | bytes 1572872 | tf_op jit(solution)/shard_map/ppermute | solution.py:515
  15.9 10.5 %collective-permute-start.3 = (f32[2,4,128,128]{3,2,1,0:T(8,128)S(1)}, f32[2,4,128,128]{3,2,1,0:T(8,128)S(1)}, u32[]{:S(2)}, u32[]{:S(2)}) collective-permute-start(f32[2,4,128,128]{3,2,1,0:T(8,128)S(1)} %get-tuple-element.37), channel_id=1, source_target_pairs={{1,2},{3,4},{5,6},{7,8},{9,10},{11,12},{13,14},{2,1},{4,3},{6,5},{... | collective-permute-start | bytes 1572872 | tf_op jit(solution)/shard_map/ppermute | solution.py:519
  18.0 6.1 %copy-start = (s32[128,128]{1,0:T(8,128)S(1)}, s32[128,128]{1,0:T(8,128)}, u32[]{:S(2)}) copy-start(s32[128,128]{1,0:T(8,128)} %omega_y.3) | copy-start | bytes 196612
  18.0 6.1 %copy-start.1 = (bf16[256,128]{1,0:T(8,128)(2,1)S(1)}, bf16[256,128]{1,0:T(8,128)(2,1)}, u32[]{:S(2)}) copy-start(bf16[256,128]{1,0:T(8,128)(2,1)} %constant.27.clone.pool_hbm.pool) | copy-start | bytes 196612
  18.0 6.0 %copy-start.2 = (s32[16,128]{1,0:T(8,128)S(1)}, s32[16,128]{1,0:T(8,128)}, u32[]{:S(2)}) copy-start(s32[16,128]{1,0:T(8,128)} %omega_z.3) | copy-start | bytes 24580
  26.4 8.7 %copy-start.3 = (s32[128,128]{1,0:T(8,128)S(1)}, s32[128,128]{1,0:T(8,128)}, u32[]{:S(2)}) copy-start(s32[128,128]{1,0:T(8,128)} %omega_x.1) | copy-start | bytes 196612
  27.5 32.3 %all-to-all-start = ((f32[16,2,64,128]{3,2,1,0:T(8,128)}), f32[16,2,64,128]{3,2,1,0:T(8,128)S(1)}, u32[]{:S(2)}, u32[]{:S(2)}) async-start(f32[16,2,64,128]{3,2,1,0:T(8,128)} %get-tuple-element.39), calls=%async_computation | async-start | bytes 2097152 | tf_op jit(solution)/shard_map/all_to_all | solution.py:666
  35.1 3.2 %copy-start.4 = (f32[2,128]{1,0:T(2,128)}, f32[2,128]{1,0:T(2,128)S(1)}, u32[]{:S(2)}) copy-start(f32[2,128]{1,0:T(2,128)S(1)} %shard_map.173.sketch) | copy-start | bytes 3076
  38.6 34.4 %copy-start.5 = (f32[2,128]{1,0:T(2,128)S(1)}, f32[2,128]{1,0:T(2,128)}, u32[]{:S(2)}) copy-start(f32[2,128]{1,0:T(2,128)} %copy-done.4) | copy-start | bytes 3076

commit v7 on v6

--- a/solution.py
+++ b/solution.py
@@ -112,6 +112,7 @@
     rest,
     gain_self,
     gain_lap,
+    near,
     curr,
     courant,
     prev,
@@ -190,6 +191,12 @@
             )
             rest[shot, z] = scale * source[:, cells_y:] - prev_gain * now
 
+    layers = near.shape[1]
+    near_span = pl.ds((1 - odd_slab()) * (cells_z - layers), layers)
+    near_copy = pltpu.make_async_copy(
+        curr_hbm.at[:, near_span], near, sems.at[few + 3 * blocks]
+    )
+    near_copy.start()
     copies[few].wait()
     for block in range(blocks):
         if block + 1 < blocks:
@@ -197,24 +204,17 @@
         for copy in copies[few + 3 * block + 1 : few + 3 * block + 3]:
             copy.wait()
         pl.loop(block * step, (block + 1) * step)(one_layer)
+    near_copy.wait()
 
 
 def odd_slab():
     return lax.rem(lax.axis_index("slab"), 2)
 
 
-def slice_kernel(curr, near, far, sems):
-    layers = near.shape[1]
+def slice_kernel(curr, far, sems):
+    layers = far.shape[1]
     last = curr.shape[1] - layers
-    odd = odd_slab()
-    copies = fetch(
-        [
-            (curr.at[:, pl.ds((1 - odd) * last, layers)], near),
-            (curr.at[:, pl.ds(odd * last, layers)], far),
-        ],
-        sems,
-    )
-    for copy in copies:
+    for copy in fetch([(curr.at[:, pl.ds(odd_slab() * last, layers)], far)], sems):
         copy.wait()
 
 
@@ -528,21 +528,20 @@
     gain = shape((cells_z,) + plane, F32)
     edge = shape((shots, REACH) + plane, F32)
     like = lambda array: pltpu.VMEM(array.shape, array.dtype)
-    near, far = run(
+    far = run(
         slice_kernel,
-        [edge, edge],
+        edge,
         in_specs=[hbm],
-        out_specs=[vmem, vmem],
-        scratch=[pltpu.SemaphoreType.DMA((2,))],
-        moved=2**21,
+        out_specs=vmem,
+        scratch=[pltpu.SemaphoreType.DMA((1,))],
+        moved=2**20,
     )(*pinned(adj_curr))
     far = with_far(far)
-    near = with_near(near)
-    updated, rest, gain_self, gain_lap = run(
+    updated, rest, gain_self, gain_lap, near = run(
         functools.partial(begin_kernel, total_z, blocks),
-        [field, field, gain, gain],
+        [field, field, gain, gain, edge],
         in_specs=[pl.BlockSpec(memory_space=pltpu.SMEM)] + [hbm] * 9,
-        out_specs=[vmem] * 4,
+        out_specs=[vmem] * 5,
         scratch=[
             like(adj_curr),
             like(courant),
@@ -556,7 +555,7 @@
             pltpu.VMEM((cells_z, cells_y), F32),
             pltpu.VMEM(plane, F32),
             pltpu.VMEM((shots, 2 * cells_y, 2 * receivers), BF16),
-            pltpu.SemaphoreType.DMA((6 + 3 * blocks,)),
+            pltpu.SemaphoreType.DMA((7 + 3 * blocks,)),
         ],
         flops=2 * 10**9,
         moved=11 * 2**20,
@@ -603,6 +602,7 @@
         )(side, wave, halo, gain_lap)
 
     side = jnp.remainder(lax.axis_index("slab"), 2).astype(jnp.int32).reshape(1)
+    near = with_near(near)
     wave, near = complete(1 - side, updated, near)
     wave, far = complete(side, wave, far)
     far = with_far(far)

time: 91.7 us -> 104 us (1.13)
  blocking collectives: 29.8 us -> 35.4 us
  Pallas kernels: 18.1 us -> 21.4 us
  local copies, waits for them, and re-layouts: 3.46 us -> 6.41 us
    all_to_all x1, blocking collectives: 17.6 us -> 23.8 us  [local(): terms = lax.all_to_all(terms, 'slab', 0, 0, tiled=True)]
    ppermute x2, waiting for transfers between devices: 2.91 us -> 8.97 us  [with_far(): return lax.ppermute(layers, 'slab', pairs + [(j, i) for i, j in pairs])]
    all_to_all x1, waiting for transfers between devices: 20 us -> 14.5 us  [local(): got = lax.all_to_all(panels, 'shot', 0, 0, tiled=True)]
    unnamed x14 -> x22, local copies, waits for them, and re-layouts: 0.04 us -> 3 us
    pallas_call x2, Pallas kernels: 0.43 us -> 2.4 us  [complete(): pl.pallas_call(edge_kernel, out_shape=[field, edge], grid_spec=pltpu.Pref...]
  transfers between devices with their start and end apart: 5 -> 5, of which waited for: 3 -> 3; matrix products, arithmetic and copies ran while one was open for 5% -> 4% of each run, Pallas kernels for 15% -> 11%
where the time goes in v7:
time: 104 us; the launch traced here: 103 us
  blocking collectives  35.4 us (34%)
  waiting for transfers between devices  23.5 us (23%)
  Pallas kernels  21.4 us (21%)
  starting transfers between devices  14.8 us (14%)
  local copies, waits for them, and re-layouts  6.41 us (6%)
  other arithmetic  1.14 us (1%)
    all_to_all x1, blocking collectives, local(): terms = lax.all_to_all(terms, 'slab', 0, 0, tiled=True)  23.8 us
    all_to_all x1, waiting for transfers between devices, local(): got = lax.all_to_all(panels, 'shot', 0, 0, tiled=True)  14.5 us
    all_to_all x1, blocking collectives, local(): lax.all_to_all(gram.reshape(groups, shots, cells_y), 'shot', 0, 0, tiled=...  11.6 us
    ppermute x2, waiting for transfers between devices, with_far(): return lax.ppermute(layers, 'slab', pairs + [(j, i) for i, j in pairs])  8.97 us
    all_to_all x1, starting transfers between devices, local(): got = lax.all_to_all(panels, 'shot', 0, 0, tiled=True)  7.58 us
    pallas_call x1, Pallas kernels, local(): run(functools.partial(begin_kernel, total_z, blocks), [field, field, gain...  7.36 us
    pallas_call x1, Pallas kernels, local(): run(functools.partial(middle_kernel, blocks), [panel, both, both, spread]...  5.95 us
    ppermute x2, starting transfers between devices, with_far(): return lax.ppermute(layers, 'slab', pairs + [(j, i) for i, j in pairs])  3.85 us
  transfers between devices with their start and end apart: 5, of which 3 were waited for; matrix products, arithmetic and copies ran while one was open for 4% of the time, Pallas kernels for 11%

profile of v7, /device:TPU:1, one launch (start us, length us, event | category | flops | bytes accessed | tf_op | source)
XLA Modules:
  0.0 103.5 jit_solution(3935909735738986873)
XLA Ops:
  0.6 0.6 copy-done.10
  1.3 7.4 %shard_map.166 = (f32[2,16,128,128]{3,2,1,0:T(8,128)S(1)}, f32[2,16,128,128]{3,2,1,0:T(8,128)S(1)}, f32[16,128,128]{2,1,0:T(8,128)S(1)}, f32[16,128,128]{2,1,0:T(8,128)S(1)}, f32[2,4,128,128]{3,2,1,0:T(8,128)}) custom-call(s32[3]{0:T(128)S(1)} %copy-done.10, f32[2,16,128,128]{3,2,1,0:T(8,128)} %curr.1, f32[16,128,128]{2,1,0:T(8,128)} %courant_hbm.1, ...), custom_call_target="tpu_custom_call" | custom-call | flops 2000000000 | bytes 11534336 | tf_op jit(solution)/shard_map/pallas_call | solution.py:540
  8.7 1.3 %copy-done = f32[2,16,128,128]{3,2,1,0:T(8,128)} copy-done((f32[2,16,128,128]{3,2,1,0:T(8,128)}, f32[2,16,128,128]{3,2,1,0:T(8,128)S(1)}, u32[]{:S(2)}) %copy-start) | copy-done | bytes 2097176
  10.0 1.0 copy-done.2
  11.0 3.2 %collective-permute-start = (f32[2,4,128,128]{3,2,1,0:T(8,128)}, f32[2,4,128,128]{3,2,1,0:T(8,128)}, u32[]{:S(2)}, u32[]{:S(2)}) collective-permute-start(f32[2,4,128,128]{3,2,1,0:T(8,128)} %get-tuple-element.23), channel_id=1, source_target_pairs={{0,1},{1,0},{2,3},{3,2},{4,5},{5,4},{6,7},{7,6},{8,9},{9,8},{10,11... | collective-permute-start | bytes 1572872 | tf_op jit(solution)/shard_map/ppermute | solution.py:515
  14.2 1.8 %shard_map.168 = f32[2,4,128,128]{3,2,1,0:T(8,128)} custom-call(f32[2,16,128,128]{3,2,1,0:T(8,128)} %curr.1), custom_call_target="tpu_custom_call" | custom-call | bytes 1048576 | tf_op jit(solution)/shard_map/pallas_call | solution.py:531
  16.1 1.9 %collective-permute-start.1 = (f32[2,4,128,128]{3,2,1,0:T(8,128)}, f32[2,4,128,128]{3,2,1,0:T(8,128)}, u32[]{:S(2)}, u32[]{:S(2)}) collective-permute-start(f32[2,4,128,128]{3,2,1,0:T(8,128)} %shard_map.168), channel_id=1, source_target_pairs={{1,2},{3,4},{5,6},{7,8},{9,10},{11,12},{13,14},{2,1},{4,3},{6,5},{... | collective-permute-start | bytes 1572872 | tf_op jit(solution)/shard_map/ppermute | solution.py:519
  18.0 1.2 %shard_map.167 = (f32[2,16,128,128]{3,2,1,0:T(8,128)S(1)}, f32[2,4,128,128]{3,2,1,0:T(8,128)S(1)}) custom-call(s32[1]{0:T(128)S(6)} %sub.3.side, f32[2,16,128,128]{3,2,1,0:T(8,128)S(1)} %get-tuple-element.22.partial, f32[2,4,128,128]{3,2,1,0:T(8,128)} %collective-permute-done.halo, ...), custom_call_target="tpu_custom_call", output_to_operand_aliasing={{0}: (1, {})} | custom-call | flops 10000000 | bytes 2097152 | tf_op jit(solution)/shard_map/pallas_call | solution.py:584
  19.2 0.0 copy-start.3
  19.3 0.1 collective-permute-start.2
  19.4 7.5 %collective-permute-done.1.halo = f32[2,4,128,128]{3,2,1,0:T(8,128)} collective-permute-done((f32[2,4,128,128]{3,2,1,0:T(8,128)}, f32[2,4,128,128]{3,2,1,0:T(8,128)}, u32[]{:S(2)}, u32[]{:S(2)}) %collective-permute-start.1) | collective-permute-done | bytes 524320 | tf_op jit(solution)/shard_map/ppermute | solution.py:519
  26.9 1.2 %shard_map.169 = (f32[2,16,128,128]{3,2,1,0:T(8,128)S(1)}, f32[2,4,128,128]{3,2,1,0:T(8,128)S(1)}) custom-call(s32[1]{0:T(128)} %bitcast.side, f32[2,16,128,128]{3,2,1,0:T(8,128)S(1)} %get-tuple-element.25.partial, f32[2,4,128,128]{3,2,1,0:T(8,128)} %collective-permute-done.1.halo, ...), custom_call_target="tpu_custom_call", output_to_operand_aliasing={{0}: (1, {})} | custom-call | flops 10000000 | bytes 2097152 | tf_op jit(solution)/shard_map/pallas_call | solution.py:584
  28.1 1.9 %collective-permute-start.3 = (f32[2,4,128,128]{3,2,1,0:T(8,128)S(1)}, f32[2,4,128,128]{3,2,1,0:T(8,128)S(1)}, u32[]{:S(2)}, u32[]{:S(2)}) collective-permute-start(f32[2,4,128,128]{3,2,1,0:T(8,128)S(1)} %get-tuple-element.35), channel_id=1, source_target_pairs={{1,2},{3,4},{5,6},{7,8},{9,10},{11,12},{13,14},{2,1},{4,3},{6,5},{... | collective-permute-start | bytes 1572872 | tf_op jit(solution)/shard_map/ppermute | solution.py:519
  30.0 0.0 copy-start.4
  30.1 0.0 copy-start.5
  30.1 0.0 copy-start.6
  30.1 6.0 %shard_map.170 = (f32[16,2,64,128]{3,2,1,0:T(8,128)}, f32[2,8,128,128]{3,2,1,0:T(8,128)S(1)}, f32[2,8,128,128]{3,2,1,0:T(8,128)S(1)}, f32[2,128,128]{2,1,0:T(8,128)S(1)}) custom-call(f32[2,16,128,128]{3,2,1,0:T(8,128)S(1)} %get-tuple-element.26.wave, f32[2,16,128,128]{3,2,1,0:T(8,128)S(1)} %copy-done.1, f32[16,128,128]{2,1,0:T(8,128)S(1)} %copy-done.3, ...), custom_call_target="tpu_custom_call" | custom-call | flops 2000000000 | bytes 11534336 | tf_op jit(solution)/shard_map/pallas_call | solution.py:619
  36.1 1.1 %shard_map.171 = (f32[16,2,64,128]{3,2,1,0:T(8,128)}, f32[2,128,128]{2,1,0:T(8,128)S(1)}) custom-call(f32[16,2,64,128]{3,2,1,0:T(8,128)} %get-tuple-element.29.panels_before, f32[2,8,128,128]{3,2,1,0:T(8,128)S(1)} %get-tuple-element.30.edges, f32[2,8,128,128]{3,2,1,0:T(8,128)S(1)} %get-tuple-element.31.edge_gain, ...), custom_call_target="tpu_custom_call", output_to_operand_aliasing={{0}: (0, {})} | custom-call | flops 300000000 | bytes 3145728 | tf_op jit(solution)/shard_map/pallas_call | solution.py:645
  37.1 1.4 %collective-permute-done.3.halo = f32[2,4,128,128]{3,2,1,0:T(8,128)S(1)} collective-permute-done((f32[2,4,128,128]{3,2,1,0:T(8,128)S(1)}, f32[2,4,128,128]{3,2,1,0:T(8,128)S(1)}, u32[]{:S(2)}, u32[]{:S(2)}) %collective-permute-start.3) | collective-permute-done | bytes 524320 | tf_op jit(solution)/shard_map/ppermute | solution.py:519
  38.6 1.0 %shard_map.172 = (f32[16,2,64,128]{3,2,1,0:T(8,128)}, f32[2,128,128]{2,1,0:T(8,128)S(1)}) custom-call(f32[16,2,64,128]{3,2,1,0:T(8,128)} %get-tuple-element.34.panels_before, f32[2,8,128,128]{3,2,1,0:T(8,128)S(1)} %get-tuple-element.30.edges, f32[2,8,128,128]{3,2,1,0:T(8,128)S(1)} %get-tuple-element.31.edge_gain, ...), custom_call_target="tpu_custom_call", output_to_operand_aliasing={{0}: (0, {})} | custom-call | flops 300000000 | bytes 3145728 | tf_op jit(solution)/shard_map/pallas_call | solution.py:645
  39.6 7.6 %all-to-all-start = ((f32[16,2,64,128]{3,2,1,0:T(8,128)}), f32[16,2,64,128]{3,2,1,0:T(8,128)S(1)}, u32[]{:S(2)}, u32[]{:S(2)}) async-start(f32[16,2,64,128]{3,2,1,0:T(8,128)} %get-tuple-element.37), calls=%async_computation | async-start | bytes 2097152 | tf_op jit(solution)/shard_map/all_to_all | solution.py:666
  47.3 0.0 copy-start.8
  47.3 1.8 %copy.26 = f32[8,2,2,2,32,128]{5,0,4,1,2,3:T(8,128)S(1)} copy(f32[8,2,2,2,32,128]{5,4,3,2,1,0:T(8,128)} %bitcast.2) | data formatting | bytes 2097152 | tf_op jit(solution)/shard_map/reshape | solution.py:668
  49.2 1.3 %copy.23 = f32[2,2,8,2,32,128]{5,4,3,2,1,0:T(8,128)S(1)} copy(f32[2,2,8,2,32,128]{5,4,0,1,3,2:T(8,128)} %bitcast.4) | data formatting | bytes 2097152 | tf_op jit(solution)/shard_map/transpose | solution.py:669
  50.5 0.1 concatenate.10
  50.6 0.1 concatenate.12
  50.8 1.1 %pad_maximum_fusion.coarse = f32[2,16,8192]{2,1,0:T(8,128)} fusion(f32[2,4,8192]{2,1,0:T(4,128)S(1)} %concatenate.12, f32[2,8,8192]{2,1,0:T(8,128)S(1)} %bitcast.20, f32[2,4,8192]{2,1,0:T(4,128)S(1)} %concatenate.10), kind=kLoop, calls=%fused_computation | loop fusion | flops 524288 | bytes 2097152 | tf_op jit(solution)/shard_map/concatenate | solution.py:670
  51.9 14.5 %all-to-all-done = f32[16,2,64,128]{3,2,1,0:T(8,128)S(1)} async-done(((f32[16,2,64,128]{3,2,1,0:T(8,128)}), f32[16,2,64,128]{3,2,1,0:T(8,128)S(1)}, u32[]{:S(2)}, u32[]{:S(2)}) %all-to-all-start) | async-done | bytes 1048608 | tf_op jit(solution)/shard_map/all_to_all | solution.py:666
  66.4 1.0 shard_map.174
  67.4 11.6 %all_to_all.15.mine = f32[16,2,128]{2,1,0:T(2,128)S(1)} all-to-all(f32[16,2,128]{2,1,0:T(2,128)S(1)} %bitcast.17), channel_id=1, replica_groups=mesh['shot'=16,'slab'=16] {'shot'}, dimensions={0} | all-to-all | bytes 32768 | tf_op jit(solution)/shard_map/all_to_all | solution.py:683
  79.0 23.8 %all_to_all.16.terms = f32[16,4,128]{2,1,0:T(4,128)S(1)} all-to-all(f32[16,4,128]{2,1,0:T(4,128)S(1)} %shard_map.175), channel_id=1, replica_groups=mesh['shot'=16,'slab'=16] {'slab'}, dimensions={0} | all-to-all | bytes 65536 | tf_op jit(solution)/shard_map/all_to_all | solution.py:691
  102.8 0.7 shard_map.176
  (20 shorter events, 0.2 us)
Async XLA Ops:
  0.6 0.7 copy-start.10
  8.7 1.3 %copy-start = (f32[2,16,128,128]{3,2,1,0:T(8,128)}, f32[2,16,128,128]{3,2,1,0:T(8,128)S(1)}, u32[]{:S(2)}) copy-start(f32[2,16,128,128]{3,2,1,0:T(8,128)S(1)} %get-tuple-element.27.rest) | copy-start | bytes 6291460
  10.0 1.0 copy-start.2
  11.0 7.0 %collective-permute-start = (f32[2,4,128,128]{3,2,1,0:T(8,128)}, f32[2,4,128,128]{3,2,1,0:T(8,128)}, u32[]{:S(2)}, u32[]{:S(2)}) collective-permute-start(f32[2,4,128,128]{3,2,1,0:T(8,128)} %get-tuple-element.23), channel_id=1, source_target_pairs={{0,1},{1,0},{2,3},{3,2},{4,5},{5,4},{6,7},{7,6},{8,9},{9,8},{10,11... | collective-permute-start | bytes 1572872 | tf_op jit(solution)/shard_map/ppermute | solution.py:515
  16.1 10.8 %collective-permute-start.1 = (f32[2,4,128,128]{3,2,1,0:T(8,128)}, f32[2,4,128,128]{3,2,1,0:T(8,128)}, u32[]{:S(2)}, u32[]{:S(2)}) collective-permute-start(f32[2,4,128,128]{3,2,1,0:T(8,128)} %shard_map.168), channel_id=1, source_target_pairs={{1,2},{3,4},{5,6},{7,8},{9,10},{11,12},{13,14},{2,1},{4,3},{6,5},{... | collective-permute-start | bytes 1572872 | tf_op jit(solution)/shard_map/ppermute | solution.py:519
  19.2 10.8 %copy-start.1 = (f32[2,16,128,128]{3,2,1,0:T(8,128)S(1)}, f32[2,16,128,128]{3,2,1,0:T(8,128)}, u32[]{:S(2)}) copy-start(f32[2,16,128,128]{3,2,1,0:T(8,128)} %copy-done) | copy-start | bytes 6291460
  19.2 10.8 %copy-start.3 = (f32[16,128,128]{2,1,0:T(8,128)S(1)}, f32[16,128,128]{2,1,0:T(8,128)}, u32[]{:S(2)}) copy-start(f32[16,128,128]{2,1,0:T(8,128)} %copy-done.2) | copy-start | bytes 3145732
  19.3 16.8 %collective-permute-start.2 = (f32[2,4,128,128]{3,2,1,0:T(8,128)S(1)}, f32[2,4,128,128]{3,2,1,0:T(8,128)S(1)}, u32[]{:S(2)}, u32[]{:S(2)}) collective-permute-start(f32[2,4,128,128]{3,2,1,0:T(8,128)S(1)} %get-tuple-element.32), channel_id=1, source_target_pairs={{0,1},{1,0},{2,3},{3,2},{4,5},{5,4},{6,7},{7,6},{8,9},{9,8},{10,11... | collective-permute-start | bytes 1572872 | tf_op jit(solution)/shard_map/ppermute | solution.py:515
  28.1 10.5 %collective-permute-start.3 = (f32[2,4,128,128]{3,2,1,0:T(8,128)S(1)}, f32[2,4,128,128]{3,2,1,0:T(8,128)S(1)}, u32[]{:S(2)}, u32[]{:S(2)}) collective-permute-start(f32[2,4,128,128]{3,2,1,0:T(8,128)S(1)} %get-tuple-element.35), channel_id=1, source_target_pairs={{1,2},{3,4},{5,6},{7,8},{9,10},{11,12},{13,14},{2,1},{4,3},{6,5},{... | collective-permute-start | bytes 1572872 | tf_op jit(solution)/shard_map/ppermute | solution.py:519
  30.0 6.0 %copy-start.4 = (s32[128,128]{1,0:T(8,128)S(1)}, s32[128,128]{1,0:T(8,128)}, u32[]{:S(2)}) copy-start(s32[128,128]{1,0:T(8,128)} %omega_y.3) | copy-start | bytes 196612
  30.1 6.0 %copy-start.5 = (bf16[256,128]{1,0:T(8,128)(2,1)S(1)}, bf16[256,128]{1,0:T(8,128)(2,1)}, u32[]{:S(2)}) copy-start(bf16[256,128]{1,0:T(8,128)(2,1)} %constant.27.clone.pool_hbm.pool) | copy-start | bytes 196612
  30.1 6.0 %copy-start.6 = (s32[16,128]{1,0:T(8,128)S(1)}, s32[16,128]{1,0:T(8,128)}, u32[]{:S(2)}) copy-start(s32[16,128]{1,0:T(8,128)} %omega_z.3) | copy-start | bytes 24580
  38.6 8.6 %copy-start.7 = (s32[128,128]{1,0:T(8,128)S(1)}, s32[128,128]{1,0:T(8,128)}, u32[]{:S(2)}) copy-start(s32[128,128]{1,0:T(8,128)} %omega_x.1) | copy-start | bytes 196612
  39.6 26.8 %all-to-all-start = ((f32[16,2,64,128]{3,2,1,0:T(8,128)}), f32[16,2,64,128]{3,2,1,0:T(8,128)S(1)}, u32[]{:S(2)}, u32[]{:S(2)}) async-start(f32[16,2,64,128]{3,2,1,0:T(8,128)} %get-tuple-element.37), calls=%async_computation | async-start | bytes 2097152 | tf_op jit(solution)/shard_map/all_to_all | solution.py:666
  47.3 3.2 %copy-start.8 = (f32[2,128]{1,0:T(2,128)}, f32[2,128]{1,0:T(2,128)S(1)}, u32[]{:S(2)}) copy-start(f32[2,128]{1,0:T(2,128)S(1)} %shard_map.173.sketch) | copy-start | bytes 3076
  50.8 28.2 %copy-start.9 = (f32[2,128]{1,0:T(2,128)S(1)}, f32[2,128]{1,0:T(2,128)}, u32[]{:S(2)}) copy-start(f32[2,128]{1,0:T(2,128)} %copy-done.8) | copy-start | bytes 3076
